TPU v7x, 512 devices: a whole 4x8x8 slice. The times are simulated.
512 devices in a mesh: dp: 32 (over z, y_hi, core), group: 16 (over x, y_lo).
Axes of the slice: x: 4, y: 8 (y_hi: 2, y_lo: 4; y = y_hi * 4 + y_lo), z: 8, core: 2. Of those that a mesh axis runs over, the one named last changes fastest.
Arguments:
- features: bfloat16 [32768, 5, 2048], P(('dp', 'group')), may hold values from -24 to 24
- labels: int32 [32768], P(('dp', 'group')), may hold values from 0 to 2
- weight: float32 [2048, 384], P('group'), may hold values from -0.125 to 0.125
- head: float32 [384, 3], replicated, may hold values from -24 to 24
- moment_one: float32 [2048, 384], P('group'), may hold values from -3 to 3
- moment_two: float32 [2048, 384], P('group'), may hold values from 0.1 to 2
Outputs:
- input_grad: bfloat16 [32768, 5, 2048], P(('dp', 'group'))
- new_weight: float32 [2048, 384], P('group')
- new_first: float32 [2048, 384], P('group')
- new_second: float32 [2048, 384], P('group')
All inputs are finite; a program needn't handle non-finite values.
Results may differ from a plain program's by a relative error of at most 0.012.
Values may be sent and summed in bfloat16 or wider, within the bound.
No kernel may reach another device: no remote copies, remote signals or barrier semaphores. Data moves between devices by JAX's collectives and lax.ppermute only.
A program may use at most 128 MiB of HBM per device.

v0:
```python
import jax
import jax.numpy as jnp
from jax import lax
from jax.sharding import PartitionSpec as P

beta_one = 0.9
beta_two = 0.999
learn_rate = 0.01
epsilon = 1e-08
bias_steps = 10.0


def gelu_tanh(value):
    return jax.nn.gelu(value, approximate=True)


def adam_update(weight, grad, first, second):
    new_first = beta_one * first + (1.0 - beta_one) * grad
    new_second = beta_two * second + (1.0 - beta_two) * grad * grad
    first_hat = new_first / (1.0 - beta_one**bias_steps)
    second_hat = new_second / (1.0 - beta_two**bias_steps)
    new_weight = weight - learn_rate * first_hat / (jnp.sqrt(second_hat) + epsilon)
    return (new_weight, new_first, new_second)


def per_device(features, labels, weight, head, moment_one, moment_two):
    pile_count = features.shape[0]
    positions = features.shape[1]
    channels = features.shape[2]
    outputs = weight.shape[1]
    rows = features.reshape(pile_count * positions, channels)
    low_weight = weight.astype(jnp.bfloat16)
    columns = rows
    pre = jnp.dot(
        columns,
        lax.all_gather(low_weight, "group", axis=0, tiled=True),
        preferred_element_type=jnp.float32,
    )
    act, back = jax.vjp(gelu_tanh, pre)
    pooled = jnp.sum(act.reshape(pile_count, positions, outputs), axis=1) / positions
    logits = jnp.dot(pooled, head, precision=lax.Precision.HIGHEST)
    prob = jax.nn.softmax(logits, axis=-1)
    dlogits = prob - jax.nn.one_hot(labels, head.shape[1], dtype=jnp.float32)
    dpooled = jnp.dot(dlogits, head.T, precision=lax.Precision.HIGHEST)
    dact = jnp.broadcast_to(dpooled[:, None, :] / positions, (pile_count, positions, outputs))
    dpre = back(dact.reshape(pile_count * positions, outputs))[0].astype(jnp.bfloat16)
    back_rows = lax.dot_general(
        dpre,
        lax.all_gather(low_weight, "group", axis=0, tiled=True),
        (((1,), (1,)), ((), ())),
        preferred_element_type=jnp.float32,
    )
    input_grad = back_rows.astype(jnp.bfloat16).reshape(pile_count, positions, channels)
    columns = rows
    grad_shard = lax.psum_scatter(
        lax.dot_general(
            columns, dpre, (((0,), (0,)), ((), ())), preferred_element_type=jnp.float32
        ),
        "group",
        scatter_dimension=0,
        tiled=True,
    )
    grad_total = lax.psum(grad_shard, "dp")
    new_weight, new_first, new_second = adam_update(weight, grad_total, moment_one, moment_two)
    return (input_grad, new_weight, new_first, new_second)


def solution(mesh):
    return jax.shard_map(
        per_device,
        mesh=mesh,
        in_specs=(
            P(("dp", "group"), None, None),
            P(("dp", "group")),
            P("group", None),
            P(),
            P("group", None),
            P("group", None),
        ),
        out_specs=(
            P(("dp", "group"), None, None),
            P("group", None),
            P("group", None),
            P("group", None),
        ),
        check_vma=False,
    )
```

profile of v0, /device:TPU:1, one launch (start us, length us, event | category | flops | bytes accessed | tf_op | source)
XLA Modules:
  0.0 548.1 jit_solution(2324300472714627321)
XLA Ops:
  7.2 0.0 copy-start
  7.2 0.0 all-gather.2.cloned.1.call-start
  7.2 1.6 convert_element_type.13
  8.8 0.0 all-gather.2.cloned.1.call-update
  8.8 0.0 reduce-scatter.2.cloned.1.call-start
  8.9 2.1 copy.17
  10.9 0.6 reshape.25
  11.5 83.0 %all-gather.2.cloned.1.call-done = bf16[2048,384]{1,0:T(8,128)(2,1)} async-done(((bf16[128,384]{1,0:T(8,128)(2,1)}), bf16[2048,384]{1,0:T(8,128)(2,1)}) %all-gather.2.cloned.1.call-update) | async-done | bytes 1572880 | tf_op jit(solution)/shard_map/all_gather | solution.py:36
  94.5 2.3 multiply_multiply_fusion.2
  96.9 0.0 copy-start.8
  96.9 0.1 reshape.26
  97.0 0.2 reduce_sum.18
  97.2 0.0 copy-done
  97.2 0.2 fusion.18
  97.5 0.0 copy-done.8
  97.5 0.3 convolution_multiply_fusion
  97.9 0.1 broadcast_in_dim.4
  97.9 0.1 reshape.27
  98.0 0.3 fusion.6
  98.4 2.7 convolution_bitcast_fusion
  101.0 0.0 copy-start.2
  101.0 0.0 copy-start.7
  101.0 0.0 copy-start.1
  101.0 0.0 reduce-scatter.2.cloned.1.call-update
  101.1 0.0 all-reduce.2.cloned.1.call-start
  101.1 0.8 copy-done.2
  102.0 0.8 copy.20
  102.8 0.0 copy-done.6
  102.8 0.8 copy.18
  103.6 0.0 copy-done.7
  103.6 0.8 copy.19
  104.4 93.0 %reduce-scatter.2.cloned.1.call-done = f32[128,384]{0,1:T(8,128)} async-done(((f32[2048,384]{0,1:T(8,128)}), f32[128,384]{0,1:T(8,128)}) %reduce-scatter.2.cloned.1.call-update) | async-done | bytes 196624 | tf_op jit(solution)/shard_map/reduce_scatter | solution.py:55
  197.3 0.0 all-reduce.2.cloned.1.call-update
  197.4 0.0 copy-done.1
  197.4 0.9 convolution_convert_fusion
  198.3 0.6 reshape.28
  198.8 0.0 copy-start.3
  198.8 0.0 copy-start.4
  198.8 0.0 copy-start.5
  198.9 1.9 copy.21
  200.8 337.3 %all-reduce.2.cloned.1.call-done = f32[128,384]{0,1:T(8,128)} async-done(((f32[128,384]{0,1:T(8,128)}), f32[128,384]{0,1:T(8,128)}) %all-reduce.2.cloned.1.call-update) | async-done | bytes 196624 | tf_op jit(solution)/shard_map/psum | solution.py:63
  538.0 0.0 copy-done.3
  538.1 0.0 copy-done.4
  538.1 0.0 copy-done.5
  538.1 1.1 divide_subtract_fusion
  539.1 0.8 copy.22
  539.9 0.8 copy.23
  540.8 0.8 copy.24
  (2 shorter events, 0.0 us)
Async XLA Ops:
  7.2 90.1 %copy-start = (f32[384,3]{0,1:T(4,128)S(1)}, f32[384,3]{0,1:T(4,128)}, u32[]{:S(2)}) copy-start(f32[384,3]{0,1:T(4,128)} %param.9) | copy-start | bytes 13828
  7.2 87.3 %all-gather.2.cloned.1.call-start = ((), (), s32[]{:S(2)}) async-start(), calls=%async_computation.1 | async-start | bytes 1671168 | tf_op jit(solution)/shard_map/all_gather | solution.py:36
  8.8 188.5 %reduce-scatter.2.cloned.1.call-start = ((), (), s32[]{:S(2)}) async-start(), calls=%async_computation.2 | async-start | bytes 3342336 | tf_op jit(solution)/shard_map/reduce_scatter | solution.py:55
  96.9 0.7 copy-start.8
  101.0 0.9 copy-start.2
  101.0 1.7 copy-start.6
  101.0 2.5 copy-start.7
  101.0 96.3 %copy-start.1 = (bf16[2048,384]{1,0:T(8,128)(2,1)S(1)}, bf16[2048,384]{1,0:T(8,128)(2,1)}, u32[]{:S(2)}) copy-start(bf16[2048,384]{1,0:T(8,128)(2,1)} %all-gather.2.cloned.1.call-done) | copy-start | bytes 4718596
  101.1 437.0 %all-reduce.2.cloned.1.call-start = ((), (), s32[]{:S(2)}) async-start(), calls=%async_computation.3 | async-start | bytes 393216 | tf_op jit(solution)/shard_map/psum | solution.py:63
  198.8 339.2 %copy-start.3 = (f32[128,384]{0,1:T(8,128)S(1)}, f32[128,384]{0,1:T(8,128)}, u32[]{:S(2)}) copy-start(f32[128,384]{0,1:T(8,128)} %copy.20) | copy-start | bytes 589828
  198.8 339.2 %copy-start.4 = (f32[128,384]{0,1:T(8,128)S(1)}, f32[128,384]{0,1:T(8,128)}, u32[]{:S(2)}) copy-start(f32[128,384]{0,1:T(8,128)} %copy.18) | copy-start | bytes 589828
  198.8 339.2 %copy-start.5 = (f32[128,384]{0,1:T(8,128)S(1)}, f32[128,384]{0,1:T(8,128)}, u32[]{:S(2)}) copy-start(f32[128,384]{0,1:T(8,128)} %copy.19) | copy-start | bytes 589828
Sparse Core Ops, SparseCore 0:
  10.7 83.8 all-gather.1
  101.2 96.1 reduce-scatter.1
  200.3 337.7 all-reduce.1
where the time goes:
time: 548 us
  waiting for transfers between devices  513 us (94%)
  between operations  13.9 us (3%)
  local copies, waits for them, and re-layouts  11.1 us (2%)
  matrix products  6.39 us (1%)
    psum x1, waiting for transfers between devices, per_device(): grad_total = lax.psum(grad_shard, 'dp')  337 us
    reduce_scatter x1, waiting for transfers between devices, per_device(): lax.psum_scatter(lax.dot_general(columns, dpre, (((0,), (0,)), ((), ())),...  93 us
    all_gather x1, waiting for transfers between devices, per_device(): lax.all_gather(low_weight, 'group', axis=0, tiled=True)  83 us
  transfers between devices with their start and end apart: 3, of which 3 were waited for; matrix products, arithmetic and copies ran while one was open for 2% of the time, Pallas kernels for 0%

commit v1 on v0

v1 whole, which is shorter than its diff:
```python
import functools
import math

import jax
import jax.numpy as jnp
from jax import lax
from jax.experimental import pallas as pl
from jax.experimental.pallas import tpu as pltpu
from jax.sharding import PartitionSpec as P

beta_one = 0.9
beta_two = 0.999
learn_rate = 0.01
epsilon = 1e-08
bias_steps = 10.0

AXES = ("dp", "group")
Z, YH, CORE, X, YL = 8, 2, 2, 4, 4
GROUP = X * YL
root = math.sqrt(2.0 / math.pi)
cubic = 0.044715


def index(z, yh, c, x, yl):
    return ((z * YH + yh) * CORE + c) * GROUP + x * YL + yl


def places():
    for z in range(Z):
        for yh in range(YH):
            for c in range(CORE):
                for x in range(X):
                    for yl in range(YL):
                        yield z, yh, c, x, yl


def groups(key):
    held = {}
    for place in places():
        held.setdefault(key(*place), []).append(index(*place))
    return [held[name] for name in sorted(held)]


OVER_GROUP = groups(lambda z, yh, c, x, yl: (z, yh, c))
OVER_X = groups(lambda z, yh, c, x, yl: (z, yh, c, yl))
OVER_Y = groups(lambda z, yh, c, x, yl: (z, c, x))
OVER_Z = groups(lambda z, yh, c, x, yl: (yh, c, x, yl))
SWAP = [(index(z, yh, c, x, yl), index(z, yh, 1 - c, x, yl)) for z, yh, c, x, yl in places()]


def swap_cores(value):
    return lax.ppermute(value, AXES, SWAP)


def exchange(value, members):
    return lax.all_to_all(value, AXES, 0, 0, tiled=True, axis_index_groups=members)


def join_halves(core, own_ref, other_ref, out_ref, rows):
    own_at = core * rows
    other_at = rows - own_at
    for block in range(own_ref.shape[0] // rows):
        span = pl.ds(block * rows, rows)
        base = 2 * rows * block
        out_ref[pl.ds(pl.multiple_of(base + own_at, rows), rows), :] = own_ref[span, :]
        out_ref[pl.ds(pl.multiple_of(base + other_at, rows), rows), :] = other_ref[span, :]


def core_index():
    return lax.rem(lax.axis_index("dp"), CORE)


def forward_kernel(
    own_ref, other_ref, rows_ref, labels_ref, head_ref, dpre_ref, keep_ref, send_ref, weight_ref, flip_ref
):
    core = core_index()
    positions, piles, channels = rows_ref.shape
    outputs = head_ref.shape[1]
    classes = head_ref.shape[0]
    count = positions * piles
    join_halves(core, own_ref, other_ref, weight_ref, own_ref.shape[0] // GROUP)
    rows = rows_ref[...].reshape(count, channels)
    pre = jnp.dot(rows, weight_ref[...], preferred_element_type=jnp.float32)
    square = pre * pre
    bend = jnp.tanh(root * (pre + cubic * (pre * square)))
    act = 0.5 * pre * (1.0 + bend)
    slope = 0.5 * (1.0 + bend) + 0.5 * pre * (1.0 - bend * bend) * (root * (1.0 + 3.0 * cubic * square))
    pooled = act[:piles]
    for position in range(1, positions):
        pooled = pooled + act[position * piles : (position + 1) * piles]
    pooled = pooled / positions
    heads = [head_ref[kind : kind + 1, :] for kind in range(classes)]
    logits = [jnp.sum(pooled * vector, axis=1, keepdims=True) for vector in heads]
    top = functools.reduce(jnp.maximum, logits)
    powers = [jnp.exp(value - top) for value in logits]
    total = functools.reduce(jnp.add, powers)
    across = lax.broadcasted_iota(jnp.int32, (piles, piles), 0) == lax.broadcasted_iota(
        jnp.int32, (piles, piles), 1
    )
    marks = jnp.sum(
        jnp.where(across, labels_ref[...].astype(jnp.float32), 0.0), axis=1, keepdims=True
    )
    dpooled = jnp.zeros((piles, outputs), jnp.float32)
    for kind in range(classes):
        dlogit = powers[kind] / total - jnp.where(marks == float(kind), 1.0, 0.0)
        dpooled = dpooled + dlogit * heads[kind]
    dact = dpooled / positions
    dpre = jnp.concatenate([dact] * positions, axis=0) * slope
    dpre_ref[...] = dpre.astype(jnp.bfloat16)
    flip_ref[...] = dpre.T.astype(jnp.bfloat16)
    half = outputs // 2
    keep_ref[...] = flip_ref[pl.ds(pl.multiple_of(core * half, half), half), :]
    other = flip_ref[pl.ds(pl.multiple_of((1 - core) * half, half), half), :]
    width = channels // GROUP
    for block in range(GROUP // 4):
        part = jnp.dot(
            other,
            rows_ref[:, :, 4 * width * block : 4 * width * (block + 1)].reshape(count, 4 * width),
            preferred_element_type=jnp.float32,
        ).astype(jnp.bfloat16)
        for at in range(4):
            send_ref[4 * block + at] = part[:, at * width : (at + 1) * width]


def backward_kernel(own_ref, other_ref, rows_ref, dpre_ref, keep_ref, input_ref, grad_ref, weight_ref):
    core = core_index()
    positions, piles, wide = rows_ref.shape
    join_halves(core, own_ref, other_ref, weight_ref, own_ref.shape[0] // 4)
    back = lax.dot_general(
        dpre_ref[...], weight_ref[...], (((1,), (1,)), ((), ())), preferred_element_type=jnp.float32
    )
    input_ref[...] = back.astype(jnp.bfloat16).reshape(positions, piles, wide)
    part = jnp.dot(
        keep_ref[...], rows_ref[...].reshape(positions * piles, wide), preferred_element_type=jnp.float32
    )
    width = wide // 4
    for at in range(4):
        grad_ref[at] = part[:, at * width : (at + 1) * width]


def adam_kernel(
    own_ref, other_ref, weight_ref, first_ref, second_ref, out_weight, out_first, out_second, flip_ref
):
    core = core_index()
    join_halves(core, own_ref, other_ref, flip_ref, own_ref.shape[0])
    grad = flip_ref[...].T
    new_first = beta_one * first_ref[...] + (1.0 - beta_one) * grad
    new_second = beta_two * second_ref[...] + (1.0 - beta_two) * grad * grad
    first_hat = new_first / (1.0 - beta_one**bias_steps)
    second_hat = new_second / (1.0 - beta_two**bias_steps)
    out_weight[...] = weight_ref[...] - learn_rate * first_hat / (jnp.sqrt(second_hat) + epsilon)
    out_first[...] = new_first
    out_second[...] = new_second


def per_device(features, labels, weight, head, moment_one, moment_two):
    piles, positions, channels = features.shape
    shard, outputs = weight.shape
    count = piles * positions
    half_rows = shard // 2
    half_outs = outputs // 2
    core = lax.rem(lax.axis_index("dp"), CORE)
    rows = features.transpose(1, 0, 2)

    half = lax.dynamic_slice_in_dim(weight, core * half_rows, half_rows, 0).astype(jnp.bfloat16)
    copies = jnp.broadcast_to(half[None], (GROUP, half_rows, outputs)).reshape(-1, outputs)
    own = exchange(copies, OVER_GROUP)
    other = swap_cores(own)

    vmem = pl.BlockSpec(memory_space=pltpu.VMEM)
    dpre, keep, send = pl.pallas_call(
        forward_kernel,
        out_shape=(
            jax.ShapeDtypeStruct((count, outputs), jnp.bfloat16),
            jax.ShapeDtypeStruct((half_outs, count), jnp.bfloat16),
            jax.ShapeDtypeStruct((GROUP, half_outs, shard), jnp.bfloat16),
        ),
        in_specs=[vmem] * 5,
        out_specs=(vmem, vmem, vmem),
        scratch_shapes=[
            pltpu.VMEM((channels, outputs), jnp.bfloat16),
            pltpu.VMEM((outputs, count), jnp.bfloat16),
        ],
        compiler_params=pltpu.CompilerParams(vmem_limit_bytes=32 << 20),
        cost_estimate=pl.CostEstimate(
            flops=3 * count * channels * outputs, bytes_accessed=4 << 20, transcendentals=count * outputs
        ),
        name="forward",
    )(own, other, rows, labels.reshape(1, piles), head.T)

    received = swap_cores(send)
    wide = 4 * shard
    input_grad, grad = pl.pallas_call(
        backward_kernel,
        grid=(channels // wide,),
        out_shape=(
            jax.ShapeDtypeStruct((positions, piles, channels), jnp.bfloat16),
            jax.ShapeDtypeStruct((GROUP, half_outs, shard), jnp.float32),
        ),
        in_specs=[
            pl.BlockSpec((4 * half_rows, outputs), lambda step: (step, 0)),
            pl.BlockSpec((4 * half_rows, outputs), lambda step: (step, 0)),
            pl.BlockSpec((positions, piles, wide), lambda step: (0, 0, step)),
            pl.BlockSpec((count, outputs), lambda step: (0, 0)),
            pl.BlockSpec((half_outs, count), lambda step: (0, 0)),
        ],
        out_specs=(
            pl.BlockSpec((positions, piles, wide), lambda step: (0, 0, step)),
            pl.BlockSpec((4, half_outs, shard), lambda step: (step, 0, 0)),
        ),
        scratch_shapes=[pltpu.VMEM((wide, outputs), jnp.bfloat16)],
        compiler_params=pltpu.CompilerParams(vmem_limit_bytes=32 << 20),
        cost_estimate=pl.CostEstimate(
            flops=3 * count * channels * outputs, bytes_accessed=6 << 20, transcendentals=0
        ),
        name="backward",
    )(own, other, rows, dpre, keep)

    def total(parts, members):
        return jnp.sum(parts.reshape(members, -1, half_outs, shard).astype(jnp.float32), axis=0)

    both = (grad + received.astype(jnp.float32)).astype(jnp.bfloat16)
    over_x = total(exchange(both, OVER_X), X).astype(jnp.bfloat16)
    over_y = total(exchange(jnp.concatenate([over_x] * YH, axis=0), OVER_Y), Z).astype(jnp.bfloat16)
    copies = jnp.broadcast_to(over_y, (Z, half_outs, shard))
    mine = total(exchange(copies, OVER_Z), Z)[0]
    theirs = swap_cores(mine)

    new_weight, new_first, new_second = pl.pallas_call(
        adam_kernel,
        out_shape=(jax.ShapeDtypeStruct((shard, outputs), jnp.float32),) * 3,
        in_specs=[vmem] * 5,
        out_specs=(vmem,) * 3,
        scratch_shapes=[pltpu.VMEM((outputs, shard), jnp.float32)],
        name="adam",
    )(mine, theirs, weight, moment_one, moment_two)
    return (input_grad.transpose(1, 0, 2), new_weight, new_first, new_second)


def solution(mesh):
    return jax.shard_map(
        per_device,
        mesh=mesh,
        in_specs=(
            P(("dp", "group"), None, None),
            P(("dp", "group")),
            P("group", None),
            P(),
            P("group", None),
            P("group", None),
        ),
        out_specs=(
            P(("dp", "group"), None, None),
            P("group", None),
            P("group", None),
            P("group", None),
        ),
        check_vma=False,
    )
```

time: 548 us -> 107 us (0.20)
  waiting for transfers between devices: 513 us -> 2.81 us
  blocking collectives: 0 us -> 82 us
  between operations: 13.9 us -> 0.75 us
  starting transfers between devices: 0.12 us -> 11.9 us
  local copies, waits for them, and re-layouts: 11.1 us -> 1.8 us
  Pallas kernels: 0 us -> 7.01 us
  matrix products: 6.39 us -> 0 us
    psum x1 -> x0, waiting for transfers between devices: 337 us -> none  [per_device(): grad_total = lax.psum(grad_shard, 'dp')]
    reduce_scatter x1 -> x0, waiting for transfers between devices: 93 us -> none  [per_device(): lax.psum_scatter(lax.dot_general(columns, dpre, (((0,), (0,)), ((), ())),...]
    all_gather x1 -> x0, waiting for transfers between devices: 83 us -> none  [per_device(): lax.all_gather(low_weight, 'group', axis=0, tiled=True)]
    all_to_all x0 -> x4, blocking collectives: none -> 82 us  [exchange(): lax.all_to_all(value, AXES, 0, 0, tiled=True, axis_index_groups=members)]
    ppermute x0 -> x3, starting transfers between devices: none -> 11.9 us  [swap_cores(): return lax.ppermute(value, AXES, SWAP)]
    unnamed x26 -> x10, local copies, waits for them, and re-layouts: 9.77 us -> 0.65 us
    pallas_call x0 -> x3, Pallas kernels: none -> 7.01 us  [the longest x1 2.86 us: per_device(): pl.pallas_call(backward_kernel, grid=(channels // wide,), out_shape=(jax....]
    dot_general x5 -> x0, matrix products: 6.39 us -> none  [the longest x1 2.66 us: per_device(): lax.dot_general(columns, dpre, (((0,), (0,)), ((), ())), preferred_elemen...]
  transfers between devices with their start and end apart: 3 -> 3, of which waited for: 3 -> 2; matrix products, arithmetic and copies ran while one was open for 2% -> 0% of each run, Pallas kernels for 0% -> 3%
where the time goes in v1:
time: 107 us
  blocking collectives  82 us (77%)
  starting transfers between devices  11.9 us (11%)
  Pallas kernels  7.01 us (7%)
  waiting for transfers between devices  2.81 us (3%)
  local copies, waits for them, and re-layouts  1.8 us (2%)
    all_to_all x4, blocking collectives, exchange(): lax.all_to_all(value, AXES, 0, 0, tiled=True, axis_index_groups=members)  82 us
    ppermute x3, starting transfers between devices, swap_cores(): return lax.ppermute(value, AXES, SWAP)  11.9 us
    pallas_call x1, Pallas kernels, per_device(): pl.pallas_call(backward_kernel, grid=(channels // wide,), out_shape=(jax....  2.86 us
    ppermute x3, waiting for transfers between devices, swap_cores(): return lax.ppermute(value, AXES, SWAP)  2.81 us
    pallas_call x1, Pallas kernels, per_device(): pl.pallas_call(adam_kernel, out_shape=(jax.ShapeDtypeStruct((shard, outpu...  2.25 us
  transfers between devices with their start and end apart: 3, of which 2 were waited for; matrix products, arithmetic and copies ran while one was open for 0% of the time, Pallas kernels for 3%

profile of v1, /device:TPU:1, one launch (start us, length us, event | category | flops | bytes accessed | tf_op | source)
XLA Modules:
  0.0 106.7 jit_solution(4163887419577268148)
XLA Ops:
  0.6 0.0 copy-start.1
  0.6 0.0 copy-start.2
  0.7 0.0 copy-start
  0.7 1.0 dynamic-slice_convert_fusion
  1.7 0.1 broadcast_in_dim.4
  1.8 29.4 %all_to_all.23 = bf16[16,64,384]{2,1,0:T(8,128)(2,1)S(1)} all-to-all(bf16[16,64,384]{2,1,0:T(8,128)(2,1)S(1)} %broadcast_in_dim.4), channel_id=1, replica_groups={{0,1,2,3,4,5,6,7,8,9,10,11,12,13,14,15},{16,17,18,19,20,21,22,23,24,25,..., dimensions={0} | all-to-all | bytes 1572864 | tf_op jit(solution)/shard_map/all_to_all | solution.py:56
  31.1 3.4 %collective-permute-start = (bf16[1024,384]{1,0:T(8,128)(2,1)S(1)}, bf16[1024,384]{1,0:T(8,128)(2,1)S(1)}, u32[]{:S(2)}, u32[]{:S(2)}) collective-permute-start(bf16[1024,384]{1,0:T(8,128)(2,1)S(1)} %bitcast.6), channel_id=1, source_target_pairs={{0,16},{1,17},{2,18},{3,19},{4,20},{5,21},{6,22},{7,23},{8,24},{9,... | collective-permute-start | bytes 2359304 | tf_op jit(solution)/shard_map/ppermute | solution.py:52
  34.6 1.9 %collective-permute-done.other_ref = bf16[1024,384]{1,0:T(8,128)(2,1)S(1)} collective-permute-done((bf16[1024,384]{1,0:T(8,128)(2,1)S(1)}, bf16[1024,384]{1,0:T(8,128)(2,1)S(1)}, u32[]{:S(2)}, u32[]{:S(2)}) %collective-permute-start) | collective-permute-done | bytes 786464 | tf_op jit(solution)/shard_map/ppermute | solution.py:52
  36.4 0.0 copy-done.1
  36.4 0.0 copy-done.2
  36.4 0.0 copy-done
  36.5 1.9 %forward.1 = (bf16[320,384]{1,0:T(8,128)(2,1)S(1)}, bf16[192,320]{1,0:T(8,128)(2,1)S(1)}, bf16[16,192,128]{2,1,0:T(8,128)(2,1)S(1)}) custom-call(bf16[1024,384]{1,0:T(8,128)(2,1)S(1)} %bitcast.7, bf16[1024,384]{1,0:T(8,128)(2,1)S(1)} %collective-permute-done.other_ref, bf16[5,64,2048]{2,1,0:T(8,128)(2,1)S(1)} %bitcast.9, s32[1,64]{1,0:T(1,128)S(1)} %bitcast.12, ...), custom_call_target="tpu_custom_call" | custom-call | flops 754974720 | bytes 4194304 | tf_op jit(solution)/shard_map/forward/pallas_call | solution.py:171
  38.4 2.3 %collective-permute-start.1 = (bf16[16,192,128]{2,1,0:T(8,128)(2,1)S(1)}, bf16[16,192,128]{2,1,0:T(8,128)(2,1)S(1)}, u32[]{:S(2)}, u32[]{:S(2)}) collective-permute-start(bf16[16,192,128]{2,1,0:T(8,128)(2,1)S(1)} %get-tuple-element.16), channel_id=1, source_target_pairs={{0,16},{1,17},{2,18},{3,19},{4,20},{5,21},{6,22},{7,23},{8,24},{9,... | collective-permute-start | bytes 2359304 | tf_op jit(solution)/shard_map/ppermute | solution.py:52
  40.7 2.9 %backward.1 = (bf16[5,64,2048]{2,1,0:T(8,128)(2,1)}, f32[16,192,128]{2,1,0:T(8,128)S(1)}) custom-call(bf16[1024,384]{1,0:T(8,128)(2,1)S(1)} %bitcast.8, bf16[1024,384]{1,0:T(8,128)(2,1)S(1)} %collective-permute-done.other_ref, bf16[5,64,2048]{2,1,0:T(8,128)(2,1)S(1)} %bitcast.10, bf16[320,384]{1,0:T(8,128)(2,1)S(1)} %get-tuple-element.12.dpre_ref, ...), custom_call_target="tpu_custom_call" | custom-call | flops 754974720 | bytes 6291456 | tf_op jit(solution)/shard_map/backward/pallas_call | solution.py:193
  43.5 0.0 collective-permute-done.1
  43.5 0.2 add_convert_fusion
  43.7 14.4 %all_to_all.24 = bf16[16,192,128]{2,1,0:T(8,128)(2,1)S(1)} all-to-all(bf16[16,192,128]{2,1,0:T(8,128)(2,1)S(1)} %add_convert_fusion), channel_id=1, replica_groups={{0,4,8,12},{1,5,9,13},{2,6,10,14},{3,7,11,15},{16,20,24,28},{17,21,25,2..., dimensions={0} | all-to-all | bytes 1572864 | tf_op jit(solution)/shard_map/all_to_all | solution.py:56
  58.1 0.2 reduce_sum.33
  58.3 17.0 %all_to_all.25 = bf16[8,192,128]{2,1,0:T(8,128)(2,1)S(1)} all-to-all(bf16[8,192,128]{2,1,0:T(8,128)(2,1)S(1)} %pad_maximum_fusion), channel_id=1, replica_groups={{0,1,2,3,32,33,34,35},{4,5,6,7,36,37,38,39},{8,9,10,11,40,41,42,43},{12..., dimensions={0} | all-to-all | bytes 786432 | tf_op jit(solution)/shard_map/all_to_all | solution.py:56
  75.3 0.1 reduce_sum.34
  75.4 0.1 broadcast_in_dim.5
  75.4 21.2 %all_to_all.26 = bf16[8,192,128]{2,1,0:T(8,128)(2,1)S(1)} all-to-all(bf16[8,192,128]{2,1,0:T(8,128)(2,1)S(1)} %broadcast_in_dim.5), channel_id=1, replica_groups={{0,64,128,192,256,320,384,448},{1,65,129,193,257,321,385,449},{2,66,130..., dimensions={0} | all-to-all | bytes 786432 | tf_op jit(solution)/shard_map/all_to_all | solution.py:56
  96.6 0.1 convert_reduce_fusion.own_ref
  96.7 0.0 copy-start.3
  96.7 6.2 %collective-permute-start.2 = (f32[192,128]{1,0:T(8,128)S(1)}, f32[192,128]{1,0:T(8,128)S(1)}, u32[]{:S(2)}, u32[]{:S(2)}) collective-permute-start(f32[192,128]{1,0:T(8,128)S(1)} %convert_reduce_fusion.own_ref), channel_id=1, source_target_pairs={{0,16},{1,17},{2,18},{3,19},{4,20},{5,21},{6,22},{7,23},{8,24},{9,... | collective-permute-start | bytes 294920 | tf_op jit(solution)/shard_map/ppermute | solution.py:52
  102.9 0.9 collective-permute-done.2.other_ref
  103.8 0.0 copy-done.3
  103.8 0.0 copy-start.4
  103.8 0.6 copy-done.4
  104.5 2.2 %adam.1 = (f32[128,384]{1,0:T(8,128)}, f32[128,384]{1,0:T(8,128)}, f32[128,384]{1,0:T(8,128)}) custom-call(f32[192,128]{1,0:T(8,128)} %copy-done.3, f32[192,128]{1,0:T(8,128)} %copy-done.4, f32[128,384]{1,0:T(8,128)} %weight_ref.1, f32[128,384]{1,0:T(8,128)} %first_ref.1, f32[128,384]{1,0:T(8,128)} %second_ref.1), custom_call_target="tpu_custom_call" | custom-call | tf_op jit(solution)/shard_map/adam/pallas_call | solution.py:229
  (1 shorter events, 0.0 us)
Async XLA Ops:
  0.6 35.8 %copy-start.1 = (f32[384,3]{0,1:T(4,128)S(1)}, f32[384,3]{0,1:T(4,128)}, u32[]{:S(2)}) copy-start(f32[384,3]{0,1:T(4,128)} %param.9) | copy-start | bytes 13828
  0.6 35.8 %copy-start.2 = (s32[64]{0:T(128)S(1)}, s32[64]{0:T(128)}, u32[]{:S(2)}) copy-start(s32[64]{0:T(128)} %param.7) | copy-start | bytes 772
  0.7 35.8 %copy-start = (bf16[64,5,2048]{2,0,1:T(8,128)(2,1)S(1)}, bf16[64,5,2048]{2,0,1:T(8,128)(2,1)}, u32[]{:S(2)}) copy-start(bf16[64,5,2048]{2,0,1:T(8,128)(2,1)} %param.6) | copy-start | bytes 3932164
  31.1 5.3 %collective-permute-start = (bf16[1024,384]{1,0:T(8,128)(2,1)S(1)}, bf16[1024,384]{1,0:T(8,128)(2,1)S(1)}, u32[]{:S(2)}, u32[]{:S(2)}) collective-permute-start(bf16[1024,384]{1,0:T(8,128)(2,1)S(1)} %bitcast.6), channel_id=1, source_target_pairs={{0,16},{1,17},{2,18},{3,19},{4,20},{5,21},{6,22},{7,23},{8,24},{9,... | collective-permute-start | bytes 2359304 | tf_op jit(solution)/shard_map/ppermute | solution.py:52
  38.4 5.1 %collective-permute-start.1 = (bf16[16,192,128]{2,1,0:T(8,128)(2,1)S(1)}, bf16[16,192,128]{2,1,0:T(8,128)(2,1)S(1)}, u32[]{:S(2)}, u32[]{:S(2)}) collective-permute-start(bf16[16,192,128]{2,1,0:T(8,128)(2,1)S(1)} %get-tuple-element.16), channel_id=1, source_target_pairs={{0,16},{1,17},{2,18},{3,19},{4,20},{5,21},{6,22},{7,23},{8,24},{9,... | collective-permute-start | bytes 2359304 | tf_op jit(solution)/shard_map/ppermute | solution.py:52
  96.7 7.2 %copy-start.3 = (f32[192,128]{1,0:T(8,128)}, f32[192,128]{1,0:T(8,128)S(1)}, u32[]{:S(2)}) copy-start(f32[192,128]{1,0:T(8,128)S(1)} %convert_reduce_fusion.own_ref) | copy-start | bytes 294916
  96.7 7.2 %collective-permute-start.2 = (f32[192,128]{1,0:T(8,128)S(1)}, f32[192,128]{1,0:T(8,128)S(1)}, u32[]{:S(2)}, u32[]{:S(2)}) collective-permute-start(f32[192,128]{1,0:T(8,128)S(1)} %convert_reduce_fusion.own_ref), channel_id=1, source_target_pairs={{0,16},{1,17},{2,18},{3,19},{4,20},{5,21},{6,22},{7,23},{8,24},{9,... | collective-permute-start | bytes 294920 | tf_op jit(solution)/shard_map/ppermute | solution.py:52
  103.8 0.6 copy-start.4

commit v2 on v1

--- a/solution.py
+++ b/solution.py
@@ -16,6 +16,7 @@
 
 AXES = ("dp", "group")
 Z, YH, CORE, X, YL = 8, 2, 2, 4, 4
+Y = YH * YL
 GROUP = X * YL
 root = math.sqrt(2.0 / math.pi)
 cubic = 0.044715
@@ -34,17 +35,20 @@
                         yield z, yh, c, x, yl
 
 
-def groups(key):
+def groups(key, order):
     held = {}
     for place in places():
-        held.setdefault(key(*place), []).append(index(*place))
-    return [held[name] for name in sorted(held)]
-
-
-OVER_GROUP = groups(lambda z, yh, c, x, yl: (z, yh, c))
-OVER_X = groups(lambda z, yh, c, x, yl: (z, yh, c, yl))
-OVER_Y = groups(lambda z, yh, c, x, yl: (z, c, x))
-OVER_Z = groups(lambda z, yh, c, x, yl: (yh, c, x, yl))
+        held.setdefault(key(*place), []).append((order(*place), index(*place)))
+    return [[at for _, at in sorted(held[name])] for name in sorted(held)]
+
+
+def line(yh, yl, c):
+    return (yh * YL + yl + (Y - 2 * c)) % Y // YL
+
+
+OVER_GROUP = groups(lambda z, yh, c, x, yl: (z, c, line(yh, yl, c)), lambda z, yh, c, x, yl: (x, yl))
+OVER_Z = groups(lambda z, yh, c, x, yl: (yh, c, x, yl), lambda z, yh, c, x, yl: z)
+OVER_REST = groups(lambda z, yh, c, x, yl: (z, x, yl), lambda z, yh, c, x, yl: (yh, c))
 SWAP = [(index(z, yh, c, x, yl), index(z, yh, 1 - c, x, yl)) for z, yh, c, x, yl in places()]
 
 
@@ -71,7 +75,7 @@
 
 
 def forward_kernel(
-    own_ref, other_ref, rows_ref, labels_ref, head_ref, dpre_ref, keep_ref, send_ref, weight_ref, flip_ref
+    _, own_ref, other_ref, rows_ref, labels_ref, head_ref, dpre_ref, keep_ref, send_ref, weight_ref, flip_ref
 ):
     core = core_index()
     positions, piles, channels = rows_ref.shape
@@ -138,12 +142,16 @@
         grad_ref[at] = part[:, at * width : (at + 1) * width]
 
 
-def adam_kernel(
-    own_ref, other_ref, weight_ref, first_ref, second_ref, out_weight, out_first, out_second, flip_ref
-):
-    core = core_index()
-    join_halves(core, own_ref, other_ref, flip_ref, own_ref.shape[0])
-    grad = flip_ref[...].T
+def stage_kernel(_, weight_ref, first_ref, second_ref, out_weight, out_first, out_second):
+    out_weight[...] = weight_ref[...]
+    out_first[...] = first_ref[...]
+    out_second[...] = second_ref[...]
+
+
+def adam_kernel(parts_ref, weight_ref, first_ref, second_ref, out_weight, out_first, out_second):
+    parts = [parts_ref[at].astype(jnp.float32) for at in range(YH * CORE)]
+    halves = [functools.reduce(jnp.add, parts[core::CORE]) for core in range(CORE)]
+    grad = jnp.concatenate(halves, axis=0).T
     new_first = beta_one * first_ref[...] + (1.0 - beta_one) * grad
     new_second = beta_two * second_ref[...] + (1.0 - beta_two) * grad * grad
     first_hat = new_first / (1.0 - beta_one**bias_steps)
@@ -168,6 +176,15 @@
     other = swap_cores(own)
 
     vmem = pl.BlockSpec(memory_space=pltpu.VMEM)
+    anywhere = pl.BlockSpec(memory_space=pl.ANY)
+    staged = pl.pallas_call(
+        stage_kernel,
+        out_shape=(jax.ShapeDtypeStruct((shard, outputs), jnp.float32),) * 3,
+        in_specs=[anywhere] + [vmem] * 3,
+        out_specs=(vmem,) * 3,
+        cost_estimate=pl.CostEstimate(flops=0, bytes_accessed=2 << 20, transcendentals=0),
+        name="stage",
+    )(own, weight, moment_one, moment_two)
     dpre, keep, send = pl.pallas_call(
         forward_kernel,
         out_shape=(
@@ -175,7 +192,7 @@
             jax.ShapeDtypeStruct((half_outs, count), jnp.bfloat16),
             jax.ShapeDtypeStruct((GROUP, half_outs, shard), jnp.bfloat16),
         ),
-        in_specs=[vmem] * 5,
+        in_specs=[anywhere] + [vmem] * 5,
         out_specs=(vmem, vmem, vmem),
         scratch_shapes=[
             pltpu.VMEM((channels, outputs), jnp.bfloat16),
@@ -186,7 +203,7 @@
             flops=3 * count * channels * outputs, bytes_accessed=4 << 20, transcendentals=count * outputs
         ),
         name="forward",
-    )(own, other, rows, labels.reshape(1, piles), head.T)
+    )(staged[0], own, other, rows, labels.reshape(1, piles), head.T)
 
     received = swap_cores(send)
     wide = 4 * shard
@@ -220,20 +237,19 @@
         return jnp.sum(parts.reshape(members, -1, half_outs, shard).astype(jnp.float32), axis=0)
 
     both = (grad + received.astype(jnp.float32)).astype(jnp.bfloat16)
-    over_x = total(exchange(both, OVER_X), X).astype(jnp.bfloat16)
-    over_y = total(exchange(jnp.concatenate([over_x] * YH, axis=0), OVER_Y), Z).astype(jnp.bfloat16)
-    copies = jnp.broadcast_to(over_y, (Z, half_outs, shard))
-    mine = total(exchange(copies, OVER_Z), Z)[0]
-    theirs = swap_cores(mine)
+    over_group = total(exchange(both, OVER_GROUP), GROUP).astype(jnp.bfloat16)
+    copies = jnp.broadcast_to(over_group, (Z, half_outs, shard))
+    over_z = total(exchange(copies, OVER_Z), Z).astype(jnp.bfloat16)
+    copies = jnp.broadcast_to(over_z, (YH * CORE, half_outs, shard))
+    parts = exchange(copies, OVER_REST)
 
     new_weight, new_first, new_second = pl.pallas_call(
         adam_kernel,
         out_shape=(jax.ShapeDtypeStruct((shard, outputs), jnp.float32),) * 3,
-        in_specs=[vmem] * 5,
+        in_specs=[vmem] * 4,
         out_specs=(vmem,) * 3,
-        scratch_shapes=[pltpu.VMEM((outputs, shard), jnp.float32)],
         name="adam",
-    )(mine, theirs, weight, moment_one, moment_two)
+    )(parts, *staged)
     return (input_grad.transpose(1, 0, 2), new_weight, new_first, new_second)
 
 

time: 107 us -> 106 us (level)
  starting transfers between devices: 11.9 us -> 4.06 us
  blocking collectives: 82 us -> 87.5 us
  waiting for transfers between devices: 2.81 us -> 0.27 us
  Pallas kernels: 7.01 us -> 8.96 us
  local copies, waits for them, and re-layouts: 1.8 us -> 3.16 us
    ppermute x3 -> x2, starting transfers between devices: 11.9 us -> 4.06 us  [swap_cores(): return lax.ppermute(value, AXES, SWAP)]
    all_to_all x4, blocking collectives: 82 us -> 87.5 us  [exchange(): lax.all_to_all(value, AXES, 0, 0, tiled=True, axis_index_groups=members)]
    ppermute x3 -> x2, waiting for transfers between devices: 2.81 us -> 0.27 us  [swap_cores(): return lax.ppermute(value, AXES, SWAP)]
    pallas_call x0 -> x1, Pallas kernels: none -> 1.98 us  [per_device(): pl.pallas_call(stage_kernel, out_shape=(jax.ShapeDtypeStruct((shard, outp...]
    unnamed x10 -> x12, local copies, waits for them, and re-layouts: 0.65 us -> 2.08 us
  transfers between devices with their start and end apart: 3 -> 2, of which waited for: 2 -> 1; matrix products, arithmetic and copies ran while one was open for 0% -> 0% of each run, Pallas kernels for 3% -> 5%
where the time goes in v2:
time: 106 us; the launch traced here: 105 us
  blocking collectives  87.5 us (83%)
  Pallas kernels  8.96 us (8%)
  starting transfers between devices  4.06 us (4%)
  local copies, waits for them, and re-layouts  3.16 us (3%)
    all_to_all x4, blocking collectives, exchange(): lax.all_to_all(value, AXES, 0, 0, tiled=True, axis_index_groups=members)  87.5 us
    ppermute x2, starting transfers between devices, swap_cores(): return lax.ppermute(value, AXES, SWAP)  4.06 us
    pallas_call x1, Pallas kernels, per_device(): pl.pallas_call(backward_kernel, grid=(channels // wide,), out_shape=(jax....  2.86 us
    pallas_call x1, Pallas kernels, per_device(): pl.pallas_call(adam_kernel, out_shape=(jax.ShapeDtypeStruct((shard, outpu...  2.23 us
  transfers between devices with their start and end apart: 2, of which 1 were waited for; matrix products, arithmetic and copies ran while one was open for 0% of the time, Pallas kernels for 5%

profile of v2, /device:TPU:1, one launch (start us, length us, event | category | flops | bytes accessed | tf_op | source)
XLA Modules:
  0.0 105.1 jit_solution(15394822046625421026)
XLA Ops:
  0.6 0.9 dynamic-slice_convert_fusion
  1.5 0.1 broadcast_in_dim.6
  1.6 0.0 copy-start.2
  1.7 0.0 copy-start.4
  1.7 0.0 copy-start.5
  1.7 28.0 %all_to_all.23 = bf16[16,64,384]{2,1,0:T(8,128)(2,1)S(1)} all-to-all(bf16[16,64,384]{2,1,0:T(8,128)(2,1)S(1)} %broadcast_in_dim.6), channel_id=1, replica_groups={{0,1,2,3,4,5,6,7,8,9,10,11,12,13,14,15},{32,33,34,35,36,37,38,39,40,41,..., dimensions={0} | all-to-all | bytes 1572864 | tf_op jit(solution)/shard_map/all_to_all | solution.py:60
  29.6 0.0 copy-start
  29.6 1.9 %collective-permute-start = (bf16[1024,384]{1,0:T(8,128)(2,1)S(1)}, bf16[1024,384]{1,0:T(8,128)(2,1)S(1)}, u32[]{:S(2)}, u32[]{:S(2)}) collective-permute-start(bf16[1024,384]{1,0:T(8,128)(2,1)S(1)} %bitcast.5), channel_id=1, source_target_pairs={{0,16},{1,17},{2,18},{3,19},{4,20},{5,21},{6,22},{7,23},{8,24},{9,... | collective-permute-start | bytes 2359304 | tf_op jit(solution)/shard_map/ppermute | solution.py:56
  31.6 0.0 copy-done
  31.6 2.0 %stage.1 = (f32[128,384]{1,0:T(8,128)}, f32[128,384]{1,0:T(8,128)}, f32[128,384]{1,0:T(8,128)}) custom-call(bf16[1024,384]{1,0:T(8,128)(2,1)} %bitcast.6, f32[128,384]{1,0:T(8,128)} %weight_ref.1, f32[128,384]{1,0:T(8,128)} %first_ref.1, f32[128,384]{1,0:T(8,128)} %second_ref.1), custom_call_target="tpu_custom_call" | custom-call | bytes 2097152 | tf_op jit(solution)/shard_map/stage/pallas_call | solution.py:180
  33.5 0.3 collective-permute-done.other_ref
  33.8 0.0 copy-done.2
  33.8 0.0 copy-done.4
  33.8 0.0 copy-done.5
  33.8 0.0 copy-start.1
  33.8 1.1 %copy-done.1 = bf16[16,64,384]{2,1,0:T(8,128)(2,1)S(1)} copy-done((bf16[16,64,384]{2,1,0:T(8,128)(2,1)S(1)}, bf16[16,64,384]{2,1,0:T(8,128)(2,1)}, u32[]{:S(2)}) %copy-start.1) | copy-done | bytes 786456
  35.0 0.0 copy-start.3
  35.0 0.9 copy-done.3
  35.9 1.9 %forward.1 = (bf16[320,384]{1,0:T(8,128)(2,1)S(1)}, bf16[192,320]{1,0:T(8,128)(2,1)S(1)}, bf16[16,192,128]{2,1,0:T(8,128)(2,1)S(1)}) custom-call(f32[128,384]{1,0:T(8,128)S(1)} %copy-done.3, bf16[1024,384]{1,0:T(8,128)(2,1)S(1)} %bitcast.7, bf16[1024,384]{1,0:T(8,128)(2,1)S(1)} %collective-permute-done.other_ref, bf16[5,64,2048]{2,1,0:T(8,128)(2,1)S(1)} %bitcast.9, ...), custom_call_target="tpu_custom_call" | custom-call | flops 754974720 | bytes 4194304 | tf_op jit(solution)/shard_map/forward/pallas_call | solution.py:188
  37.8 2.1 %collective-permute-start.1 = (bf16[16,192,128]{2,1,0:T(8,128)(2,1)S(1)}, bf16[16,192,128]{2,1,0:T(8,128)(2,1)S(1)}, u32[]{:S(2)}, u32[]{:S(2)}) collective-permute-start(bf16[16,192,128]{2,1,0:T(8,128)(2,1)S(1)} %get-tuple-element.20), channel_id=1, source_target_pairs={{0,16},{1,17},{2,18},{3,19},{4,20},{5,21},{6,22},{7,23},{8,24},{9,... | collective-permute-start | bytes 2359304 | tf_op jit(solution)/shard_map/ppermute | solution.py:56
  40.0 2.9 %backward.1 = (bf16[5,64,2048]{2,1,0:T(8,128)(2,1)}, f32[16,192,128]{2,1,0:T(8,128)S(1)}) custom-call(bf16[1024,384]{1,0:T(8,128)(2,1)S(1)} %bitcast.8, bf16[1024,384]{1,0:T(8,128)(2,1)S(1)} %collective-permute-done.other_ref, bf16[5,64,2048]{2,1,0:T(8,128)(2,1)S(1)} %bitcast.10, bf16[320,384]{1,0:T(8,128)(2,1)S(1)} %get-tuple-element.16.dpre_ref, ...), custom_call_target="tpu_custom_call" | custom-call | flops 754974720 | bytes 6291456 | tf_op jit(solution)/shard_map/backward/pallas_call | solution.py:210
  42.8 0.0 collective-permute-done.1
  42.8 0.2 add_convert_fusion
  43.0 22.1 %all_to_all.24 = bf16[16,192,128]{2,1,0:T(8,128)(2,1)S(1)} all-to-all(bf16[16,192,128]{2,1,0:T(8,128)(2,1)S(1)} %add_convert_fusion), channel_id=1, replica_groups={{0,1,2,3,4,5,6,7,8,9,10,11,12,13,14,15},{32,33,34,35,36,37,38,39,40,41,..., dimensions={0} | all-to-all | bytes 1572864 | tf_op jit(solution)/shard_map/all_to_all | solution.py:60
  65.1 0.1 reduce_sum.24
  65.2 0.1 broadcast_in_dim.7
  65.3 23.6 %all_to_all.25 = bf16[8,192,128]{2,1,0:T(8,128)(2,1)S(1)} all-to-all(bf16[8,192,128]{2,1,0:T(8,128)(2,1)S(1)} %broadcast_in_dim.7), channel_id=1, replica_groups={{0,64,128,192,256,320,384,448},{1,65,129,193,257,321,385,449},{2,66,130..., dimensions={0} | all-to-all | bytes 786432 | tf_op jit(solution)/shard_map/all_to_all | solution.py:60
  88.9 0.1 reduce_sum.25
  89.0 13.8 %all_to_all.26.parts_ref = bf16[4,192,128]{2,1,0:T(8,128)(2,1)} all-to-all(bf16[4,192,128]{2,1,0:T(8,128)(2,1)S(1)} %broadcast_in_dim.8), channel_id=1, replica_groups={{0,16,32,48},{1,17,33,49},{2,18,34,50},{3,19,35,51},{4,20,36,52},{5,21,..., dimensions={0} | all-to-all | bytes 393216 | tf_op jit(solution)/shard_map/all_to_all | solution.py:60
  102.8 2.2 %adam.1 = (f32[128,384]{1,0:T(8,128)}, f32[128,384]{1,0:T(8,128)}, f32[128,384]{1,0:T(8,128)}) custom-call(bf16[4,192,128]{2,1,0:T(8,128)(2,1)} %all_to_all.26.parts_ref, f32[128,384]{1,0:T(8,128)} %get-tuple-element.15._.weight_ref, f32[128,384]{1,0:T(8,128)} %get-tuple-element.21.first_ref, f32[128,384]{1,0:T(8,128)} %get-tuple-element.22.second_ref), custom_call_target="tpu_custom_call" | custom-call | tf_op jit(solution)/shard_map/adam/pallas_call | solution.py:246
  (1 shorter events, 0.0 us)
Async XLA Ops:
  1.6 32.2 %copy-start.2 = (bf16[64,5,2048]{2,0,1:T(8,128)(2,1)S(1)}, bf16[64,5,2048]{2,0,1:T(8,128)(2,1)}, u32[]{:S(2)}) copy-start(bf16[64,5,2048]{2,0,1:T(8,128)(2,1)} %param.6) | copy-start | bytes 3932164
  1.7 32.2 %copy-start.4 = (f32[384,3]{0,1:T(4,128)S(1)}, f32[384,3]{0,1:T(4,128)}, u32[]{:S(2)}) copy-start(f32[384,3]{0,1:T(4,128)} %param.9) | copy-start | bytes 13828
  1.7 32.1 %copy-start.5 = (s32[64]{0:T(128)S(1)}, s32[64]{0:T(128)}, u32[]{:S(2)}) copy-start(s32[64]{0:T(128)} %param.7) | copy-start | bytes 772
  29.6 1.9 %copy-start = (bf16[16,64,384]{2,1,0:T(8,128)(2,1)}, bf16[16,64,384]{2,1,0:T(8,128)(2,1)S(1)}, u32[]{:S(2)}) copy-start(bf16[16,64,384]{2,1,0:T(8,128)(2,1)S(1)} %all_to_all.23) | copy-start | bytes 2359300
  29.6 4.2 %collective-permute-start = (bf16[1024,384]{1,0:T(8,128)(2,1)S(1)}, bf16[1024,384]{1,0:T(8,128)(2,1)S(1)}, u32[]{:S(2)}, u32[]{:S(2)}) collective-permute-start(bf16[1024,384]{1,0:T(8,128)(2,1)S(1)} %bitcast.5), channel_id=1, source_target_pairs={{0,16},{1,17},{2,18},{3,19},{4,20},{5,21},{6,22},{7,23},{8,24},{9,... | collective-permute-start | bytes 2359304 | tf_op jit(solution)/shard_map/ppermute | solution.py:56
  33.8 1.1 %copy-start.1 = (bf16[16,64,384]{2,1,0:T(8,128)(2,1)S(1)}, bf16[16,64,384]{2,1,0:T(8,128)(2,1)}, u32[]{:S(2)}) copy-start(bf16[16,64,384]{2,1,0:T(8,128)(2,1)} %copy-done) | copy-start | bytes 2359300
  35.0 0.9 copy-start.3
  37.8 5.0 %collective-permute-start.1 = (bf16[16,192,128]{2,1,0:T(8,128)(2,1)S(1)}, bf16[16,192,128]{2,1,0:T(8,128)(2,1)S(1)}, u32[]{:S(2)}, u32[]{:S(2)}) collective-permute-start(bf16[16,192,128]{2,1,0:T(8,128)(2,1)S(1)} %get-tuple-element.20), channel_id=1, source_target_pairs={{0,16},{1,17},{2,18},{3,19},{4,20},{5,21},{6,22},{7,23},{8,24},{9,... | collective-permute-start | bytes 2359304 | tf_op jit(solution)/shard_map/ppermute | solution.py:56

commit v3 on v2

--- a/solution.py
+++ b/solution.py
@@ -16,8 +16,8 @@
 
 AXES = ("dp", "group")
 Z, YH, CORE, X, YL = 8, 2, 2, 4, 4
-Y = YH * YL
 GROUP = X * YL
+PARTS = 4
 root = math.sqrt(2.0 / math.pi)
 cubic = 0.044715
 
@@ -42,13 +42,14 @@
     return [[at for _, at in sorted(held[name])] for name in sorted(held)]
 
 
-def line(yh, yl, c):
-    return (yh * YL + yl + (Y - 2 * c)) % Y // YL
-
-
-OVER_GROUP = groups(lambda z, yh, c, x, yl: (z, c, line(yh, yl, c)), lambda z, yh, c, x, yl: (x, yl))
-OVER_Z = groups(lambda z, yh, c, x, yl: (yh, c, x, yl), lambda z, yh, c, x, yl: z)
-OVER_REST = groups(lambda z, yh, c, x, yl: (z, x, yl), lambda z, yh, c, x, yl: (yh, c))
+def run(at, c):
+    return (at + 8 - 2 * c) % 8 // 4
+
+
+OVER_GROUP = groups(lambda z, yh, c, x, yl: (z, c, run(yh * YL + yl, c)), lambda z, yh, c, x, yl: (x, yl))
+OVER_XZ = groups(lambda z, yh, c, x, yl: (yh, yl, c, run(z, c)), lambda z, yh, c, x, yl: (x, z % PARTS))
+OVER_Y = groups(lambda z, yh, c, x, yl: (z, c, x), lambda z, yh, c, x, yl: (yh, yl))
+OVER_ZC = groups(lambda z, yh, c, x, yl: (yh, x, yl), lambda z, yh, c, x, yl: (c, z % PARTS, z // PARTS))
 SWAP = [(index(z, yh, c, x, yl), index(z, yh, 1 - c, x, yl)) for z, yh, c, x, yl in places()]
 
 
@@ -75,7 +76,7 @@
 
 
 def forward_kernel(
-    _, own_ref, other_ref, rows_ref, labels_ref, head_ref, dpre_ref, keep_ref, send_ref, weight_ref, flip_ref
+    _, own_ref, other_ref, rows_ref, labels_ref, head_ref, weight_ref, dpre_ref, keep_ref, send_ref, flip_ref
 ):
     core = core_index()
     positions, piles, channels = rows_ref.shape
@@ -115,31 +116,39 @@
     half = outputs // 2
     keep_ref[...] = flip_ref[pl.ds(pl.multiple_of(core * half, half), half), :]
     other = flip_ref[pl.ds(pl.multiple_of((1 - core) * half, half), half), :]
-    width = channels // GROUP
-    for block in range(GROUP // 4):
-        part = jnp.dot(
-            other,
-            rows_ref[:, :, 4 * width * block : 4 * width * (block + 1)].reshape(count, 4 * width),
-            preferred_element_type=jnp.float32,
-        ).astype(jnp.bfloat16)
-        for at in range(4):
-            send_ref[4 * block + at] = part[:, at * width : (at + 1) * width]
-
-
-def backward_kernel(own_ref, other_ref, rows_ref, dpre_ref, keep_ref, input_ref, grad_ref, weight_ref):
-    core = core_index()
-    positions, piles, wide = rows_ref.shape
-    join_halves(core, own_ref, other_ref, weight_ref, own_ref.shape[0] // 4)
-    back = lax.dot_general(
-        dpre_ref[...], weight_ref[...], (((1,), (1,)), ((), ())), preferred_element_type=jnp.float32
-    )
-    input_ref[...] = back.astype(jnp.bfloat16).reshape(positions, piles, wide)
-    part = jnp.dot(
-        keep_ref[...], rows_ref[...].reshape(positions * piles, wide), preferred_element_type=jnp.float32
-    )
-    width = wide // 4
-    for at in range(4):
-        grad_ref[at] = part[:, at * width : (at + 1) * width]
+    gradient(other, rows_ref, send_ref)
+
+
+def gradient(left, rows_ref, out_ref):
+    positions, piles, channels = rows_ref.shape
+    wide = channels // X
+    width = wide // YL
+    deep = left.shape[0] // PARTS
+    for x in range(X):
+        rows = rows_ref[:, :, x * wide : (x + 1) * wide].reshape(positions * piles, wide)
+        product = jnp.dot(left, rows, preferred_element_type=jnp.float32).astype(out_ref.dtype)
+        for part in range(PARTS):
+            for yl in range(YL):
+                out_ref[x, part, yl] = product[part * deep : (part + 1) * deep, yl * width : (yl + 1) * width]
+
+
+def backward_kernel(weight_ref, rows_ref, dpre_ref, keep_ref, input_ref, grad_ref, held_ref, sems):
+    positions, piles, channels = rows_ref.shape
+    wide = channels // X
+    copies = []
+    for x in range(X):
+        span = pl.ds(x * wide, wide)
+        back = lax.dot_general(
+            dpre_ref[...], weight_ref[span, :], (((1,), (1,)), ((), ())), preferred_element_type=jnp.float32
+        )
+        held_ref[:, :, span] = back.astype(jnp.bfloat16).reshape(positions, piles, wide)
+        copies.append(
+            pltpu.make_async_copy(held_ref.at[:, :, span], input_ref.at[:, :, span], sems.at[x])
+        )
+        copies[-1].start()
+    gradient(keep_ref[...], rows_ref, grad_ref)
+    for copy in copies:
+        copy.wait()
 
 
 def stage_kernel(_, weight_ref, first_ref, second_ref, out_weight, out_first, out_second):
@@ -149,9 +158,9 @@
 
 
 def adam_kernel(parts_ref, weight_ref, first_ref, second_ref, out_weight, out_first, out_second):
-    parts = [parts_ref[at].astype(jnp.float32) for at in range(YH * CORE)]
-    halves = [functools.reduce(jnp.add, parts[core::CORE]) for core in range(CORE)]
-    grad = jnp.concatenate(halves, axis=0).T
+    parts = [parts_ref[at].astype(jnp.float32) for at in range(parts_ref.shape[0])]
+    sums = [parts[at] + parts[at + 1] for at in range(0, len(parts), 2)]
+    grad = jnp.concatenate(sums, axis=0).T
     new_first = beta_one * first_ref[...] + (1.0 - beta_one) * grad
     new_second = beta_two * second_ref[...] + (1.0 - beta_two) * grad * grad
     first_hat = new_first / (1.0 - beta_one**bias_steps)
@@ -177,28 +186,31 @@
 
     vmem = pl.BlockSpec(memory_space=pltpu.VMEM)
     anywhere = pl.BlockSpec(memory_space=pl.ANY)
+    params = pltpu.CompilerParams(vmem_limit_bytes=16 << 20)
     staged = pl.pallas_call(
         stage_kernel,
         out_shape=(jax.ShapeDtypeStruct((shard, outputs), jnp.float32),) * 3,
         in_specs=[anywhere] + [vmem] * 3,
         out_specs=(vmem,) * 3,
+        compiler_params=params,
         cost_estimate=pl.CostEstimate(flops=0, bytes_accessed=2 << 20, transcendentals=0),
         name="stage",
     )(own, weight, moment_one, moment_two)
-    dpre, keep, send = pl.pallas_call(
+
+    deep = half_outs // PARTS
+    chunks = (X, PARTS, YL, deep, shard)
+    joined, dpre, keep, send = pl.pallas_call(
         forward_kernel,
         out_shape=(
+            jax.ShapeDtypeStruct((channels, outputs), jnp.bfloat16),
             jax.ShapeDtypeStruct((count, outputs), jnp.bfloat16),
             jax.ShapeDtypeStruct((half_outs, count), jnp.bfloat16),
-            jax.ShapeDtypeStruct((GROUP, half_outs, shard), jnp.bfloat16),
+            jax.ShapeDtypeStruct(chunks, jnp.bfloat16),
         ),
         in_specs=[anywhere] + [vmem] * 5,
-        out_specs=(vmem, vmem, vmem),
-        scratch_shapes=[
-            pltpu.VMEM((channels, outputs), jnp.bfloat16),
-            pltpu.VMEM((outputs, count), jnp.bfloat16),
-        ],
-        compiler_params=pltpu.CompilerParams(vmem_limit_bytes=32 << 20),
+        out_specs=(vmem,) * 4,
+        scratch_shapes=[pltpu.VMEM((outputs, count), jnp.bfloat16)],
+        compiler_params=params,
         cost_estimate=pl.CostEstimate(
             flops=3 * count * channels * outputs, bytes_accessed=4 << 20, transcendentals=count * outputs
         ),
@@ -206,48 +218,40 @@
     )(staged[0], own, other, rows, labels.reshape(1, piles), head.T)
 
     received = swap_cores(send)
-    wide = 4 * shard
     input_grad, grad = pl.pallas_call(
         backward_kernel,
-        grid=(channels // wide,),
         out_shape=(
             jax.ShapeDtypeStruct((positions, piles, channels), jnp.bfloat16),
-            jax.ShapeDtypeStruct((GROUP, half_outs, shard), jnp.float32),
-        ),
-        in_specs=[
-            pl.BlockSpec((4 * half_rows, outputs), lambda step: (step, 0)),
-            pl.BlockSpec((4 * half_rows, outputs), lambda step: (step, 0)),
-            pl.BlockSpec((positions, piles, wide), lambda step: (0, 0, step)),
-            pl.BlockSpec((count, outputs), lambda step: (0, 0)),
-            pl.BlockSpec((half_outs, count), lambda step: (0, 0)),
+            jax.ShapeDtypeStruct(chunks, jnp.float32),
+        ),
+        in_specs=[vmem] * 4,
+        out_specs=(anywhere, vmem),
+        scratch_shapes=[
+            pltpu.VMEM((positions, piles, channels), jnp.bfloat16),
+            pltpu.SemaphoreType.DMA((X,)),
         ],
-        out_specs=(
-            pl.BlockSpec((positions, piles, wide), lambda step: (0, 0, step)),
-            pl.BlockSpec((4, half_outs, shard), lambda step: (step, 0, 0)),
-        ),
-        scratch_shapes=[pltpu.VMEM((wide, outputs), jnp.bfloat16)],
-        compiler_params=pltpu.CompilerParams(vmem_limit_bytes=32 << 20),
+        compiler_params=params,
         cost_estimate=pl.CostEstimate(
             flops=3 * count * channels * outputs, bytes_accessed=6 << 20, transcendentals=0
         ),
         name="backward",
-    )(own, other, rows, dpre, keep)
+    )(joined, rows, dpre, keep)
 
     def total(parts, members):
-        return jnp.sum(parts.reshape(members, -1, half_outs, shard).astype(jnp.float32), axis=0)
-
-    both = (grad + received.astype(jnp.float32)).astype(jnp.bfloat16)
-    over_group = total(exchange(both, OVER_GROUP), GROUP).astype(jnp.bfloat16)
-    copies = jnp.broadcast_to(over_group, (Z, half_outs, shard))
-    over_z = total(exchange(copies, OVER_Z), Z).astype(jnp.bfloat16)
-    copies = jnp.broadcast_to(over_z, (YH * CORE, half_outs, shard))
-    parts = exchange(copies, OVER_REST)
+        parts = parts.reshape(members, -1, deep, shard).astype(jnp.float32)
+        return jnp.sum(parts, axis=0).astype(jnp.bfloat16)
+
+    both = (grad + received.astype(jnp.float32)).astype(jnp.bfloat16).reshape(-1, YL, deep, shard)
+    over_xz = total(exchange(both, OVER_XZ), X * PARTS)
+    over_y = total(exchange(jnp.concatenate([over_xz] * YH, axis=0), OVER_Y), YH * YL)
+    parts = exchange(jnp.broadcast_to(over_y, (Z * CORE, deep, shard)), OVER_ZC)
 
     new_weight, new_first, new_second = pl.pallas_call(
         adam_kernel,
         out_shape=(jax.ShapeDtypeStruct((shard, outputs), jnp.float32),) * 3,
         in_specs=[vmem] * 4,
         out_specs=(vmem,) * 3,
+        compiler_params=params,
         name="adam",
     )(parts, *staged)
     return (input_grad.transpose(1, 0, 2), new_weight, new_first, new_second)

time: 106 us -> 96.4 us (0.909)
  blocking collectives: 87.5 us -> 82.6 us
  Pallas kernels: 8.96 us -> 4.62 us
  waiting for transfers between devices: 0.27 us -> 2.65 us
  local copies, waits for them, and re-layouts: 3.16 us -> 1.12 us
    all_to_all x4, blocking collectives: 87.5 us -> 82.6 us  [exchange(): lax.all_to_all(value, AXES, 0, 0, tiled=True, axis_index_groups=members)]
    ppermute x2, waiting for transfers between devices: 0.27 us -> 2.65 us  [swap_cores(): return lax.ppermute(value, AXES, SWAP)]
    unnamed x12, local copies, waits for them, and re-layouts: 2.08 us -> 0.03 us
    pallas_call x1, Pallas kernels: 1.98 us -> 0.04 us  [per_device(): pl.pallas_call(stage_kernel, out_shape=(jax.ShapeDtypeStruct((shard, outp...]
    pallas_call x1, Pallas kernels: 2.23 us -> 1.01 us  [per_device(): pl.pallas_call(adam_kernel, out_shape=(jax.ShapeDtypeStruct((shard, outpu...]
    pallas_call x2, Pallas kernels: 4.76 us -> 3.57 us  [the longest x1 1.93 us: per_device(): pl.pallas_call(forward_kernel, out_shape=(jax.ShapeDtypeStruct((channels,...]
  transfers between devices with their start and end apart: 2 -> 2, of which waited for: 1 -> 2; matrix products, arithmetic and copies ran while one was open for 0% -> 0% of each run, Pallas kernels for 5% -> 2%
where the time goes in v3:
time: 96.4 us; the launch traced here: 96.1 us
  blocking collectives  82.6 us (86%)
  Pallas kernels  4.62 us (5%)
  starting transfers between devices  3.95 us (4%)
  waiting for transfers between devices  2.65 us (3%)
  local copies, waits for them, and re-layouts  1.12 us (1%)
    all_to_all x4, blocking collectives, exchange(): lax.all_to_all(value, AXES, 0, 0, tiled=True, axis_index_groups=members)  82.6 us
    ppermute x2, starting transfers between devices, swap_cores(): return lax.ppermute(value, AXES, SWAP)  3.95 us
    ppermute x2, waiting for transfers between devices, swap_cores(): return lax.ppermute(value, AXES, SWAP)  2.65 us
    pallas_call x1, Pallas kernels, per_device(): pl.pallas_call(forward_kernel, out_shape=(jax.ShapeDtypeStruct((channels,...  1.93 us
  transfers between devices with their start and end apart: 2, of which 2 were waited for; matrix products, arithmetic and copies ran while one was open for 0% of the time, Pallas kernels for 2%

profile of v3, /device:TPU:1, one launch (start us, length us, event | category | flops | bytes accessed | tf_op | source)
XLA Modules:
  0.0 96.1 jit_solution(15069127464456289666)
XLA Ops:
  0.6 0.0 copy-start.1
  0.6 0.0 copy-start.3
  0.7 0.0 copy-start.2
  0.7 1.0 %dynamic-slice_convert_fusion = bf16[64,384]{1,0:T(8,128)(2,1)S(1)} fusion(f32[128,384]{1,0:T(8,128)} %weight_ref.1, s32[]{:T(128)S(6)} %select_n.3), kind=kLoop, calls=%fused_computation.2 | loop fusion | bytes 98308 | tf_op jit(solution)/shard_map/convert_element_type | solution.py:182
  1.6 0.1 broadcast_in_dim.4
  1.7 0.0 copy-start
  1.7 0.0 copy-start.4
  1.8 0.0 copy-start.5
  1.8 28.0 %all_to_all.23 = bf16[16,64,384]{2,1,0:T(8,128)(2,1)S(1)} all-to-all(bf16[16,64,384]{2,1,0:T(8,128)(2,1)S(1)} %broadcast_in_dim.4), channel_id=1, replica_groups={{0,1,2,3,4,5,6,7,8,9,10,11,12,13,14,15},{32,33,34,35,36,37,38,39,40,41,..., dimensions={0} | all-to-all | bytes 1572864 | tf_op jit(solution)/shard_map/all_to_all | solution.py:61
  29.7 1.9 %collective-permute-start = (bf16[1024,384]{1,0:T(8,128)(2,1)S(1)}, bf16[1024,384]{1,0:T(8,128)(2,1)S(1)}, u32[]{:S(2)}, u32[]{:S(2)}) collective-permute-start(bf16[1024,384]{1,0:T(8,128)(2,1)S(1)} %bitcast.6), channel_id=1, source_target_pairs={{0,16},{1,17},{2,18},{3,19},{4,20},{5,21},{6,22},{7,23},{8,24},{9,... | collective-permute-start | bytes 2359304 | tf_op jit(solution)/shard_map/ppermute | solution.py:57
  31.6 0.0 copy-done.1
  31.7 0.0 copy-done.3
  31.7 0.0 copy-done.2
  31.7 2.2 %collective-permute-done.other_ref = bf16[1024,384]{1,0:T(8,128)(2,1)S(1)} collective-permute-done((bf16[1024,384]{1,0:T(8,128)(2,1)S(1)}, bf16[1024,384]{1,0:T(8,128)(2,1)S(1)}, u32[]{:S(2)}, u32[]{:S(2)}) %collective-permute-start) | collective-permute-done | bytes 786464 | tf_op jit(solution)/shard_map/ppermute | solution.py:57
  33.9 0.0 copy-done
  33.9 0.0 copy-done.4
  33.9 0.0 copy-done.5
  33.9 1.9 %forward.1 = (bf16[2048,384]{1,0:T(8,128)(2,1)S(1)}, bf16[320,384]{1,0:T(8,128)(2,1)S(1)}, bf16[192,320]{1,0:T(8,128)(2,1)S(1)}, bf16[4,4,4,48,128]{4,3,2,1,0:T(8,128)(2,1)S(1)}) custom-call(f32[128,384]{1,0:T(8,128)S(1)} %get-tuple-element.16._.weight_ref, bf16[1024,384]{1,0:T(8,128)(2,1)S(1)} %bitcast.8, ...), custom_call_target="tpu_custom_call" | custom-call | flops 754974720 | bytes 4194304 | tf_op jit(solution)/shard_map/forward/pallas_call | solution.py:202
  35.8 2.0 %collective-permute-start.1 = (bf16[4,4,4,48,128]{4,3,2,1,0:T(8,128)(2,1)S(1)}, bf16[4,4,4,48,128]{4,3,2,1,0:T(8,128)(2,1)S(1)}, u32[]{:S(2)}, u32[]{:S(2)}) collective-permute-start(bf16[4,4,4,48,128]{4,3,2,1,0:T(8,128)(2,1)S(1)} %get-tuple-element.22), channel_id=1, source_target_pairs={{0,16},{1,17},{2,18},{3,19},{4,20},{5,21},{6,22},{7,23},{8,24},{9,... | collective-permute-start | bytes 2359304 | tf_op jit(solution)/shard_map/ppermute | solution.py:57
  37.9 1.6 %backward.1 = (bf16[5,64,2048]{2,1,0:T(8,128)(2,1)}, f32[4,4,4,48,128]{4,3,2,1,0:T(8,128)S(1)}) custom-call(bf16[2048,384]{1,0:T(8,128)(2,1)S(1)} %get-tuple-element.17.weight_ref, bf16[5,64,2048]{2,1,0:T(8,128)(2,1)S(1)} %bitcast.10, bf16[320,384]{1,0:T(8,128)(2,1)S(1)} %get-tuple-element.18.dpre_ref, bf16[192,320]{1,0:T(8,128)(2,1)S(1)} %get-tuple-element.19.keep_ref), custom_call_target="tpu_custom_call" | custom-call | flops 754974720 | bytes 6291456 | tf_op jit(solution)/shard_map/backward/pallas_call | solution.py:221
  39.5 0.5 collective-permute-done.1
  40.0 0.2 add_convert_fusion
  40.3 29.6 %all_to_all.24 = bf16[16,4,48,128]{3,2,1,0:T(8,128)(2,1)S(1)} all-to-all(bf16[16,4,48,128]{3,2,1,0:T(8,128)(2,1)S(1)} %bitcast.13), channel_id=1, replica_groups={{0,64,128,192,4,68,132,196,8,72,136,200,12,76,140,204},{256,320,384,448..., dimensions={0} | all-to-all | bytes 1572864 | tf_op jit(solution)/shard_map/all_to_all | solution.py:61
  69.9 0.1 reduce_sum.24
  70.0 10.7 %all_to_all.25 = bf16[8,48,128]{2,1,0:T(8,128)(2,1)S(1)} all-to-all(bf16[8,48,128]{2,1,0:T(8,128)(2,1)S(1)} %pad_maximum_fusion), channel_id=1, replica_groups={{0,1,2,3,32,33,34,35},{4,5,6,7,36,37,38,39},{8,9,10,11,40,41,42,43},{12..., dimensions={0} | all-to-all | bytes 196608 | tf_op jit(solution)/shard_map/all_to_all | solution.py:61
  80.8 14.3 %all_to_all.26.parts_ref = bf16[16,48,128]{2,1,0:T(8,128)(2,1)S(1)} all-to-all(bf16[16,48,128]{2,1,0:T(8,128)(2,1)S(1)} %broadcast_in_dim.5), channel_id=1, replica_groups={{0,256,64,320,128,384,192,448,16,272,80,336,144,400,208,464},{1,257,65,..., dimensions={0} | all-to-all | bytes 393216 | tf_op jit(solution)/shard_map/all_to_all | solution.py:61
  95.1 1.0 %adam.1 = (f32[128,384]{1,0:T(8,128)}, f32[128,384]{1,0:T(8,128)}, f32[128,384]{1,0:T(8,128)}) custom-call(bf16[16,48,128]{2,1,0:T(8,128)(2,1)S(1)} %all_to_all.26.parts_ref, f32[128,384]{1,0:T(8,128)S(1)} %get-tuple-element.16._.weight_ref, f32[128,384]{1,0:T(8,128)S(1)} %get-tuple-element.23.first_ref, f32[128,384]{1,0:T(8,128)S(1)} %get-tuple-element.24.second_ref), custom_call_target="tpu_custom_call" | custom-call | tf_op jit(solution)/shard_map/adam/pallas_call | solution.py:249
  (4 shorter events, 0.1 us)
Async XLA Ops:
  0.6 31.0 %copy-start.1 = (f32[128,384]{1,0:T(8,128)S(1)}, f32[128,384]{1,0:T(8,128)}, u32[]{:S(2)}) copy-start(f32[128,384]{1,0:T(8,128)} %weight_ref.1) | copy-start | bytes 589828
  0.6 31.0 %copy-start.3 = (f32[128,384]{1,0:T(8,128)S(1)}, f32[128,384]{1,0:T(8,128)}, u32[]{:S(2)}) copy-start(f32[128,384]{1,0:T(8,128)} %second_ref.1) | copy-start | bytes 589828
  0.7 31.0 %copy-start.2 = (f32[128,384]{1,0:T(8,128)S(1)}, f32[128,384]{1,0:T(8,128)}, u32[]{:S(2)}) copy-start(f32[128,384]{1,0:T(8,128)} %first_ref.1) | copy-start | bytes 589828
  1.7 32.2 %copy-start = (bf16[64,5,2048]{2,0,1:T(8,128)(2,1)S(1)}, bf16[64,5,2048]{2,0,1:T(8,128)(2,1)}, u32[]{:S(2)}) copy-start(bf16[64,5,2048]{2,0,1:T(8,128)(2,1)} %param.6) | copy-start | bytes 3932164
  1.7 32.2 %copy-start.4 = (f32[384,3]{0,1:T(4,128)S(1)}, f32[384,3]{0,1:T(4,128)}, u32[]{:S(2)}) copy-start(f32[384,3]{0,1:T(4,128)} %param.9) | copy-start | bytes 13828
  1.8 32.1 %copy-start.5 = (s32[64]{0:T(128)S(1)}, s32[64]{0:T(128)}, u32[]{:S(2)}) copy-start(s32[64]{0:T(128)} %param.7) | copy-start | bytes 772
  29.7 4.2 %collective-permute-start = (bf16[1024,384]{1,0:T(8,128)(2,1)S(1)}, bf16[1024,384]{1,0:T(8,128)(2,1)S(1)}, u32[]{:S(2)}, u32[]{:S(2)}) collective-permute-start(bf16[1024,384]{1,0:T(8,128)(2,1)S(1)} %bitcast.6), channel_id=1, source_target_pairs={{0,16},{1,17},{2,18},{3,19},{4,20},{5,21},{6,22},{7,23},{8,24},{9,... | collective-permute-start | bytes 2359304 | tf_op jit(solution)/shard_map/ppermute | solution.py:57
  35.8 4.2 %collective-permute-start.1 = (bf16[4,4,4,48,128]{4,3,2,1,0:T(8,128)(2,1)S(1)}, bf16[4,4,4,48,128]{4,3,2,1,0:T(8,128)(2,1)S(1)}, u32[]{:S(2)}, u32[]{:S(2)}) collective-permute-start(bf16[4,4,4,48,128]{4,3,2,1,0:T(8,128)(2,1)S(1)} %get-tuple-element.22), channel_id=1, source_target_pairs={{0,16},{1,17},{2,18},{3,19},{4,20},{5,21},{6,22},{7,23},{8,24},{9,... | collective-permute-start | bytes 2359304 | tf_op jit(solution)/shard_map/ppermute | solution.py:57

commit v4 on v3

--- a/solution.py
+++ b/solution.py
@@ -17,7 +17,7 @@
 AXES = ("dp", "group")
 Z, YH, CORE, X, YL = 8, 2, 2, 4, 4
 GROUP = X * YL
-PARTS = 4
+PAIR = 2
 root = math.sqrt(2.0 / math.pi)
 cubic = 0.044715
 
@@ -42,15 +42,14 @@
     return [[at for _, at in sorted(held[name])] for name in sorted(held)]
 
 
-def run(at, c):
-    return (at + 8 - 2 * c) % 8 // 4
-
-
-OVER_GROUP = groups(lambda z, yh, c, x, yl: (z, c, run(yh * YL + yl, c)), lambda z, yh, c, x, yl: (x, yl))
-OVER_XZ = groups(lambda z, yh, c, x, yl: (yh, yl, c, run(z, c)), lambda z, yh, c, x, yl: (x, z % PARTS))
-OVER_Y = groups(lambda z, yh, c, x, yl: (z, c, x), lambda z, yh, c, x, yl: (yh, yl))
-OVER_ZC = groups(lambda z, yh, c, x, yl: (yh, x, yl), lambda z, yh, c, x, yl: (c, z % PARTS, z // PARTS))
+OVER_XY = groups(lambda z, yh, c, x, yl: (z, yh, c, yl // PAIR), lambda z, yh, c, x, yl: (x, yl))
+OVER_XYZ = groups(
+    lambda z, yh, c, x, yl: (z // PAIR, yh, c, yl // PAIR), lambda z, yh, c, x, yl: (x, yl % PAIR, z % PAIR)
+)
+OVER_Y = groups(lambda z, yh, c, x, yl: (z, c, x, yl % PAIR), lambda z, yh, c, x, yl: (yh, yl))
+OVER_Z = groups(lambda z, yh, c, x, yl: (yh, c, x, yl), lambda z, yh, c, x, yl: (z % PAIR, z))
 SWAP = [(index(z, yh, c, x, yl), index(z, yh, 1 - c, x, yl)) for z, yh, c, x, yl in places()]
+CROSS = [(index(z, yh, c, x, yl), index(z, yh, c, x, (yl + PAIR) % YL)) for z, yh, c, x, yl in places()]
 
 
 def swap_cores(value):
@@ -61,12 +60,12 @@
     return lax.all_to_all(value, AXES, 0, 0, tiled=True, axis_index_groups=members)
 
 
-def join_halves(core, own_ref, other_ref, out_ref, rows):
+def join_halves(core, own_ref, other_ref, out_ref, rows, places_of):
     own_at = core * rows
     other_at = rows - own_at
-    for block in range(own_ref.shape[0] // rows):
+    for block, place in enumerate(places_of):
         span = pl.ds(block * rows, rows)
-        base = 2 * rows * block
+        base = 2 * rows * place
         out_ref[pl.ds(pl.multiple_of(base + own_at, rows), rows), :] = own_ref[span, :]
         out_ref[pl.ds(pl.multiple_of(base + other_at, rows), rows), :] = other_ref[span, :]
 
@@ -83,7 +82,14 @@
     outputs = head_ref.shape[1]
     classes = head_ref.shape[0]
     count = positions * piles
-    join_halves(core, own_ref, other_ref, weight_ref, own_ref.shape[0] // GROUP)
+    near = lax.rem(lax.axis_index("group"), YL) // PAIR
+    shards = [
+        x * YL + (near if turn == 0 else 1 - near) * PAIR + odd
+        for x in range(X)
+        for odd in range(PAIR)
+        for turn in range(YL // PAIR)
+    ]
+    join_halves(core, own_ref, other_ref, weight_ref, own_ref.shape[0] // GROUP, shards)
     rows = rows_ref[...].reshape(count, channels)
     pre = jnp.dot(rows, weight_ref[...], preferred_element_type=jnp.float32)
     square = pre * pre
@@ -123,13 +129,15 @@
     positions, piles, channels = rows_ref.shape
     wide = channels // X
     width = wide // YL
-    deep = left.shape[0] // PARTS
+    deep = left.shape[0] // PAIR
     for x in range(X):
         rows = rows_ref[:, :, x * wide : (x + 1) * wide].reshape(positions * piles, wide)
         product = jnp.dot(left, rows, preferred_element_type=jnp.float32).astype(out_ref.dtype)
-        for part in range(PARTS):
+        for part in range(PAIR):
             for yl in range(YL):
-                out_ref[x, part, yl] = product[part * deep : (part + 1) * deep, yl * width : (yl + 1) * width]
+                out_ref[x, yl % PAIR, part, yl // PAIR] = product[
+                    part * deep : (part + 1) * deep, yl * width : (yl + 1) * width
+                ]
 
 
 def backward_kernel(weight_ref, rows_ref, dpre_ref, keep_ref, input_ref, grad_ref, held_ref, sems):
@@ -157,10 +165,11 @@
     out_second[...] = second_ref[...]
 
 
-def adam_kernel(parts_ref, weight_ref, first_ref, second_ref, out_weight, out_first, out_second):
-    parts = [parts_ref[at].astype(jnp.float32) for at in range(parts_ref.shape[0])]
-    sums = [parts[at] + parts[at + 1] for at in range(0, len(parts), 2)]
-    grad = jnp.concatenate(sums, axis=0).T
+def adam_kernel(
+    own_ref, other_ref, weight_ref, first_ref, second_ref, out_weight, out_first, out_second, flip_ref
+):
+    join_halves(core_index(), own_ref, other_ref, flip_ref, own_ref.shape[0], [0])
+    grad = flip_ref[...].T
     new_first = beta_one * first_ref[...] + (1.0 - beta_one) * grad
     new_second = beta_two * second_ref[...] + (1.0 - beta_two) * grad * grad
     first_hat = new_first / (1.0 - beta_one**bias_steps)
@@ -180,8 +189,9 @@
     rows = features.transpose(1, 0, 2)
 
     half = lax.dynamic_slice_in_dim(weight, core * half_rows, half_rows, 0).astype(jnp.bfloat16)
-    copies = jnp.broadcast_to(half[None], (GROUP, half_rows, outputs)).reshape(-1, outputs)
-    own = exchange(copies, OVER_GROUP)
+    pair = jnp.concatenate([half, lax.ppermute(half, AXES, CROSS)], axis=0)
+    copies = jnp.broadcast_to(pair[None], (X * PAIR, PAIR * half_rows, outputs))
+    own = exchange(copies, OVER_XY).reshape(-1, outputs)
     other = swap_cores(own)
 
     vmem = pl.BlockSpec(memory_space=pltpu.VMEM)
@@ -197,8 +207,8 @@
         name="stage",
     )(own, weight, moment_one, moment_two)
 
-    deep = half_outs // PARTS
-    chunks = (X, PARTS, YL, deep, shard)
+    deep = half_outs // PAIR
+    chunks = (X, PAIR, PAIR, YL // PAIR, deep, shard)
     joined, dpre, keep, send = pl.pallas_call(
         forward_kernel,
         out_shape=(
@@ -237,23 +247,23 @@
         name="backward",
     )(joined, rows, dpre, keep)
 
-    def total(parts, members):
-        parts = parts.reshape(members, -1, deep, shard).astype(jnp.float32)
-        return jnp.sum(parts, axis=0).astype(jnp.bfloat16)
-
-    both = (grad + received.astype(jnp.float32)).astype(jnp.bfloat16).reshape(-1, YL, deep, shard)
-    over_xz = total(exchange(both, OVER_XZ), X * PARTS)
-    over_y = total(exchange(jnp.concatenate([over_xz] * YH, axis=0), OVER_Y), YH * YL)
-    parts = exchange(jnp.broadcast_to(over_y, (Z * CORE, deep, shard)), OVER_ZC)
+    both = (grad + received.astype(jnp.float32)).astype(jnp.bfloat16).reshape(GROUP, -1, deep, shard)
+    over_xyz = jnp.sum(exchange(both, OVER_XYZ).astype(jnp.float32), axis=0).astype(jnp.bfloat16)
+    copies = jnp.concatenate([over_xyz] * YH, axis=0)
+    over_y = jnp.sum(exchange(copies, OVER_Y).astype(jnp.float32), axis=0).astype(jnp.bfloat16)
+    parts = exchange(jnp.broadcast_to(over_y, (Z, deep, shard)), OVER_Z)
+    mine = jnp.sum(parts.reshape(PAIR, Z // PAIR, deep, shard).astype(jnp.float32), axis=1)
+    mine = mine.reshape(half_outs, shard)
 
     new_weight, new_first, new_second = pl.pallas_call(
         adam_kernel,
         out_shape=(jax.ShapeDtypeStruct((shard, outputs), jnp.float32),) * 3,
-        in_specs=[vmem] * 4,
+        in_specs=[vmem] * 5,
         out_specs=(vmem,) * 3,
+        scratch_shapes=[pltpu.VMEM((outputs, shard), jnp.float32)],
         compiler_params=params,
         name="adam",
-    )(parts, *staged)
+    )(mine, swap_cores(mine), *staged)
     return (input_grad.transpose(1, 0, 2), new_weight, new_first, new_second)
 
 

time: 96.4 us -> 92.7 us (0.962)
  blocking collectives: 82.6 us -> 59 us
  starting transfers between devices: 3.95 us -> 21.8 us
  waiting for transfers between devices: 2.65 us -> 4.44 us
    all_to_all x4, blocking collectives: 82.6 us -> 59 us  [exchange(): lax.all_to_all(value, AXES, 0, 0, tiled=True, axis_index_groups=members)]
    ppermute x2 -> x3, starting transfers between devices: 3.95 us -> 16.8 us  [swap_cores(): return lax.ppermute(value, AXES, SWAP)]
    ppermute x0 -> x1, starting transfers between devices: none -> 5.03 us  [per_device(): pair = jnp.concatenate([half, lax.ppermute(half, AXES, CROSS)], axis=0)]
    ppermute x0 -> x1, waiting for transfers between devices: none -> 1.46 us  [per_device(): pair = jnp.concatenate([half, lax.ppermute(half, AXES, CROSS)], axis=0)]
    ppermute x2 -> x3, waiting for transfers between devices: 2.65 us -> 2.97 us  [swap_cores(): return lax.ppermute(value, AXES, SWAP)]
  transfers between devices with their start and end apart: 2 -> 4, of which waited for: 2 -> 4; matrix products, arithmetic and copies ran while one was open for 0% -> 0% of each run, Pallas kernels for 2% -> 2%
where the time goes in v4:
time: 92.7 us; the launch traced here: 92.3 us
  blocking collectives  59 us (64%)
  starting transfers between devices  21.8 us (24%)
  Pallas kernels  4.74 us (5%)
  waiting for transfers between devices  4.44 us (5%)
  local copies, waits for them, and re-layouts  1.09 us (1%)
    all_to_all x4, blocking collectives, exchange(): lax.all_to_all(value, AXES, 0, 0, tiled=True, axis_index_groups=members)  59 us
    ppermute x3, starting transfers between devices, swap_cores(): return lax.ppermute(value, AXES, SWAP)  16.8 us
    ppermute x1, starting transfers between devices, per_device(): pair = jnp.concatenate([half, lax.ppermute(half, AXES, CROSS)], axis=0)  5.03 us
    ppermute x3, waiting for transfers between devices, swap_cores(): return lax.ppermute(value, AXES, SWAP)  2.97 us
    pallas_call x1, Pallas kernels, per_device(): pl.pallas_call(forward_kernel, out_shape=(jax.ShapeDtypeStruct((channels,...  2.03 us
  transfers between devices with their start and end apart: 4, of which 4 were waited for; matrix products, arithmetic and copies ran while one was open for 0% of the time, Pallas kernels for 2%

profile of v4, /device:TPU:1, one launch (start us, length us, event | category | flops | bytes accessed | tf_op | source)
XLA Modules:
  0.0 92.3 jit_solution(14124024421889982185)
XLA Ops:
  0.6 0.0 copy-start.1
  0.6 0.0 copy-start.3
  0.7 0.0 copy-start.2
  0.7 1.0 %dynamic-slice_convert_fusion = bf16[64,384]{1,0:T(8,128)(2,1)S(1)} fusion(f32[128,384]{1,0:T(8,128)} %weight_ref.1, s32[]{:T(128)S(6)} %select_n.3), kind=kLoop, calls=%fused_computation.4 | loop fusion | bytes 98308 | tf_op jit(solution)/shard_map/convert_element_type | solution.py:191
  1.6 5.0 %collective-permute-start = (bf16[64,384]{1,0:T(8,128)(2,1)S(1)}, bf16[64,384]{1,0:T(8,128)(2,1)S(1)}, u32[]{:S(2)}, u32[]{:S(2)}) collective-permute-start(bf16[64,384]{1,0:T(8,128)(2,1)S(1)} %dynamic-slice_convert_fusion), channel_id=1, source_target_pairs={{0,2},{1,3},{2,0},{3,1},{4,6},{5,7},{6,4},{7,5},{8,10},{9,11},{10,... | collective-permute-start | bytes 147464 | tf_op jit(solution)/shard_map/ppermute | solution.py:192
  6.7 1.5 %collective-permute-done = bf16[64,384]{1,0:T(8,128)(2,1)S(1)} collective-permute-done((bf16[64,384]{1,0:T(8,128)(2,1)S(1)}, bf16[64,384]{1,0:T(8,128)(2,1)S(1)}, u32[]{:S(2)}, u32[]{:S(2)}) %collective-permute-start) | collective-permute-done | bytes 49184 | tf_op jit(solution)/shard_map/ppermute | solution.py:192
  8.2 0.1 broadcast_in_dim.4
  8.2 0.0 copy-start
  8.2 0.0 copy-start.4
  8.3 0.0 copy-start.5
  8.3 14.0 %all_to_all.20 = bf16[8,128,384]{2,1,0:T(8,128)(2,1)S(1)} all-to-all(bf16[8,128,384]{2,1,0:T(8,128)(2,1)S(1)} %broadcast_in_dim.4), channel_id=1, replica_groups={{0,1,4,5,8,9,12,13},{2,3,6,7,10,11,14,15},{16,17,20,21,24,25,28,29},{18..., dimensions={0} | all-to-all | bytes 1572864 | tf_op jit(solution)/shard_map/all_to_all | solution.py:60
  22.3 7.8 %collective-permute-start.1 = (bf16[1024,384]{1,0:T(8,128)(2,1)S(1)}, bf16[1024,384]{1,0:T(8,128)(2,1)S(1)}, u32[]{:S(2)}, u32[]{:S(2)}) collective-permute-start(bf16[1024,384]{1,0:T(8,128)(2,1)S(1)} %bitcast.10), channel_id=1, source_target_pairs={{0,16},{1,17},{2,18},{3,19},{4,20},{5,21},{6,22},{7,23},{8,24},{9,... | collective-permute-start | bytes 2359304 | tf_op jit(solution)/shard_map/ppermute | solution.py:56
  30.1 0.0 copy-done.1
  30.1 0.0 copy-done.3
  30.1 0.0 copy-done.2
  30.1 1.8 %collective-permute-done.1.other_ref = bf16[1024,384]{1,0:T(8,128)(2,1)S(1)} collective-permute-done((bf16[1024,384]{1,0:T(8,128)(2,1)S(1)}, bf16[1024,384]{1,0:T(8,128)(2,1)S(1)}, u32[]{:S(2)}, u32[]{:S(2)}) %collective-permute-start.1) | collective-permute-done | bytes 786464 | tf_op jit(solution)/shard_map/ppermute | solution.py:56
  32.0 0.0 copy-done
  32.0 0.0 copy-done.4
  32.0 0.0 copy-done.5
  32.0 2.0 %forward.1 = (bf16[2048,384]{1,0:T(8,128)(2,1)S(1)}, bf16[320,384]{1,0:T(8,128)(2,1)S(1)}, bf16[192,320]{1,0:T(8,128)(2,1)S(1)}, bf16[4,2,2,2,96,128]{5,4,3,2,1,0:T(8,128)(2,1)S(1)}) custom-call(f32[128,384]{1,0:T(8,128)S(1)} %get-tuple-element.16._.weight_ref, bf16[1024,384]{1,0:T(8,128)(2,1)S(1)} %bitcast.12, ...), custom_call_target="tpu_custom_call" | custom-call | flops 754974720 | bytes 4194304 | tf_op jit(solution)/shard_map/forward/pallas_call | solution.py:212
  34.0 2.3 %collective-permute-start.2 = (bf16[4,2,2,2,96,128]{5,4,3,2,1,0:T(8,128)(2,1)S(1)}, bf16[4,2,2,2,96,128]{5,4,3,2,1,0:T(8,128)(2,1)S(1)}, u32[]{:S(2)}, u32[]{:S(2)}) collective-permute-start(bf16[4,2,2,2,96,128]{5,4,3,2,1,0:T(8,128)(2,1)S(1)} %get-tuple-element.22), channel_id=1, source_target_pairs={{0,16},{1,17},{2,18},{3,19},{4,20},{5,21},{6,22},{7,23},{8,24},{9,... | collective-permute-start | bytes 2359304 | tf_op jit(solution)/shard_map/ppermute | solution.py:56
  36.3 1.6 %backward.1 = (bf16[5,64,2048]{2,1,0:T(8,128)(2,1)}, f32[4,2,2,2,96,128]{5,4,3,2,1,0:T(8,128)S(1)}) custom-call(bf16[2048,384]{1,0:T(8,128)(2,1)S(1)} %get-tuple-element.17.weight_ref, bf16[5,64,2048]{2,1,0:T(8,128)(2,1)S(1)} %bitcast.14, bf16[320,384]{1,0:T(8,128)(2,1)S(1)} %get-tuple-element.18.dpre_ref, bf16[192,320]{1,0:T(8,128)(2,1)S(1)} %get-tuple-element.19.keep_ref), custom_call_target="tpu_custom_call" | custom-call | flops 754974720 | bytes 6291456 | tf_op jit(solution)/shard_map/backward/pallas_call | solution.py:231
  37.9 0.2 collective-permute-done.2
  38.2 0.2 add_convert_fusion
  38.4 15.4 %all_to_all.21 = bf16[16,2,96,128]{3,2,1,0:T(8,128)(2,1)S(1)} all-to-all(bf16[16,2,96,128]{3,2,1,0:T(8,128)(2,1)S(1)} %bitcast.19), channel_id=1, replica_groups={{0,64,1,65,4,68,5,69,8,72,9,73,12,76,13,77},{2,66,3,67,6,70,7,71,10,74,..., dimensions={0} | all-to-all | bytes 1572864 | tf_op jit(solution)/shard_map/all_to_all | solution.py:60
  53.8 0.1 reduce_sum.33
  53.9 13.3 %all_to_all.22 = bf16[4,96,128]{2,1,0:T(8,128)(2,1)S(1)} all-to-all(bf16[4,96,128]{2,1,0:T(8,128)(2,1)S(1)} %pad_maximum_fusion.1), channel_id=1, replica_groups={{0,2,32,34},{1,3,33,35},{4,6,36,38},{5,7,37,39},{8,10,40,42},{9,11,41,4..., dimensions={0} | all-to-all | bytes 196608 | tf_op jit(solution)/shard_map/all_to_all | solution.py:60
  67.3 16.4 %all_to_all.23 = bf16[8,96,128]{2,1,0:T(8,128)(2,1)S(1)} all-to-all(bf16[8,96,128]{2,1,0:T(8,128)(2,1)S(1)} %broadcast_in_dim.10), channel_id=1, replica_groups={{0,128,256,384,64,192,320,448},{1,129,257,385,65,193,321,449},{2,130,25..., dimensions={0} | all-to-all | bytes 393216 | tf_op jit(solution)/shard_map/all_to_all | solution.py:60
  83.7 6.7 %collective-permute-start.3 = (f32[192,128]{1,0:T(8,128)S(1)}, f32[192,128]{1,0:T(8,128)S(1)}, u32[]{:S(2)}, u32[]{:S(2)}) collective-permute-start(f32[192,128]{1,0:T(8,128)S(1)} %bitcast.15), channel_id=1, source_target_pairs={{0,16},{1,17},{2,18},{3,19},{4,20},{5,21},{6,22},{7,23},{8,24},{9,... | collective-permute-start | bytes 294920 | tf_op jit(solution)/shard_map/ppermute | solution.py:56
  90.4 0.9 collective-permute-done.3.other_ref
  91.3 1.0 %adam.1 = (f32[128,384]{1,0:T(8,128)}, f32[128,384]{1,0:T(8,128)}, f32[128,384]{1,0:T(8,128)}) custom-call(f32[192,128]{1,0:T(8,128)S(1)} %bitcast.16, f32[192,128]{1,0:T(8,128)S(1)} %collective-permute-done.3.other_ref, f32[128,384]{1,0:T(8,128)S(1)} %get-tuple-element.16._.weight_ref, f32[128,384]{1,0:T(8,128)S(1)} %get-tuple-element.23.first_ref, ...), custom_call_target="tpu_custom_call" | custom-call | tf_op jit(solution)/shard_map/adam/pallas_call | solution.py:258
  (6 shorter events, 0.1 us)
Async XLA Ops:
  0.6 29.4 %copy-start.1 = (f32[128,384]{1,0:T(8,128)S(1)}, f32[128,384]{1,0:T(8,128)}, u32[]{:S(2)}) copy-start(f32[128,384]{1,0:T(8,128)} %weight_ref.1) | copy-start | bytes 589828
  0.6 29.4 %copy-start.3 = (f32[128,384]{1,0:T(8,128)S(1)}, f32[128,384]{1,0:T(8,128)}, u32[]{:S(2)}) copy-start(f32[128,384]{1,0:T(8,128)} %second_ref.1) | copy-start | bytes 589828
  0.7 29.4 %copy-start.2 = (f32[128,384]{1,0:T(8,128)S(1)}, f32[128,384]{1,0:T(8,128)}, u32[]{:S(2)}) copy-start(f32[128,384]{1,0:T(8,128)} %first_ref.1) | copy-start | bytes 589828
  1.6 6.5 %collective-permute-start = (bf16[64,384]{1,0:T(8,128)(2,1)S(1)}, bf16[64,384]{1,0:T(8,128)(2,1)S(1)}, u32[]{:S(2)}, u32[]{:S(2)}) collective-permute-start(bf16[64,384]{1,0:T(8,128)(2,1)S(1)} %dynamic-slice_convert_fusion), channel_id=1, source_target_pairs={{0,2},{1,3},{2,0},{3,1},{4,6},{5,7},{6,4},{7,5},{8,10},{9,11},{10,... | collective-permute-start | bytes 147464 | tf_op jit(solution)/shard_map/ppermute | solution.py:192
  8.2 23.7 %copy-start = (bf16[64,5,2048]{2,0,1:T(8,128)(2,1)S(1)}, bf16[64,5,2048]{2,0,1:T(8,128)(2,1)}, u32[]{:S(2)}) copy-start(bf16[64,5,2048]{2,0,1:T(8,128)(2,1)} %param.6) | copy-start | bytes 3932164
  8.2 23.7 %copy-start.4 = (f32[384,3]{0,1:T(4,128)S(1)}, f32[384,3]{0,1:T(4,128)}, u32[]{:S(2)}) copy-start(f32[384,3]{0,1:T(4,128)} %param.9) | copy-start | bytes 13828
  8.3 23.7 %copy-start.5 = (s32[64]{0:T(128)S(1)}, s32[64]{0:T(128)}, u32[]{:S(2)}) copy-start(s32[64]{0:T(128)} %param.7) | copy-start | bytes 772
  22.3 9.7 %collective-permute-start.1 = (bf16[1024,384]{1,0:T(8,128)(2,1)S(1)}, bf16[1024,384]{1,0:T(8,128)(2,1)S(1)}, u32[]{:S(2)}, u32[]{:S(2)}) collective-permute-start(bf16[1024,384]{1,0:T(8,128)(2,1)S(1)} %bitcast.10), channel_id=1, source_target_pairs={{0,16},{1,17},{2,18},{3,19},{4,20},{5,21},{6,22},{7,23},{8,24},{9,... | collective-permute-start | bytes 2359304 | tf_op jit(solution)/shard_map/ppermute | solution.py:56
  34.0 4.2 %collective-permute-start.2 = (bf16[4,2,2,2,96,128]{5,4,3,2,1,0:T(8,128)(2,1)S(1)}, bf16[4,2,2,2,96,128]{5,4,3,2,1,0:T(8,128)(2,1)S(1)}, u32[]{:S(2)}, u32[]{:S(2)}) collective-permute-start(bf16[4,2,2,2,96,128]{5,4,3,2,1,0:T(8,128)(2,1)S(1)} %get-tuple-element.22), channel_id=1, source_target_pairs={{0,16},{1,17},{2,18},{3,19},{4,20},{5,21},{6,22},{7,23},{8,24},{9,... | collective-permute-start | bytes 2359304 | tf_op jit(solution)/shard_map/ppermute | solution.py:56
  83.7 7.7 %collective-permute-start.3 = (f32[192,128]{1,0:T(8,128)S(1)}, f32[192,128]{1,0:T(8,128)S(1)}, u32[]{:S(2)}, u32[]{:S(2)}) collective-permute-start(f32[192,128]{1,0:T(8,128)S(1)} %bitcast.15), channel_id=1, source_target_pairs={{0,16},{1,17},{2,18},{3,19},{4,20},{5,21},{6,22},{7,23},{8,24},{9,... | collective-permute-start | bytes 294920 | tf_op jit(solution)/shard_map/ppermute | solution.py:56

commit v5 on v4

v5 whole, which is shorter than its diff:
```python
import functools
import math

import jax
import jax.numpy as jnp
from jax import lax
from jax.experimental import pallas as pl
from jax.experimental.pallas import tpu as pltpu
from jax.sharding import PartitionSpec as P

beta_one = 0.9
beta_two = 0.999
learn_rate = 0.01
epsilon = 1e-08
bias_steps = 10.0

AXES = ("dp", "group")
Z, YH, CORE, X, YL = 8, 2, 2, 4, 4
GROUP = X * YL
PAIR = 2
root = math.sqrt(2.0 / math.pi)
cubic = 0.044715


def index(z, yh, c, x, yl):
    return ((z * YH + yh) * CORE + c) * GROUP + x * YL + yl


def places():
    for z in range(Z):
        for yh in range(YH):
            for c in range(CORE):
                for x in range(X):
                    for yl in range(YL):
                        yield z, yh, c, x, yl


def groups(key, order):
    held = {}
    for place in places():
        held.setdefault(key(*place), []).append((order(*place), index(*place)))
    return [[at for _, at in sorted(held[name])] for name in sorted(held)]


OVER_XY = groups(lambda z, yh, c, x, yl: (z, yh, c, yl // PAIR), lambda z, yh, c, x, yl: (x, yl))
OVER_XYZ = groups(
    lambda z, yh, c, x, yl: (z // PAIR, yh, c, yl // PAIR), lambda z, yh, c, x, yl: (x, yl % PAIR, z % PAIR)
)
OVER_Y = groups(lambda z, yh, c, x, yl: (z, c, x, yl % PAIR), lambda z, yh, c, x, yl: (yh, yl))
OVER_Z = groups(lambda z, yh, c, x, yl: (yh, c, x, yl), lambda z, yh, c, x, yl: (z % PAIR, z))
SWAP = [(index(z, yh, c, x, yl), index(z, yh, 1 - c, x, yl)) for z, yh, c, x, yl in places()]


def beside(yh, yl):
    at = (yh * YL + yl + (1 if yl % PAIR else -1)) % (YH * YL)
    return at // YL, at % YL


CROSS = [(index(z, yh, c, x, yl), index(z, *beside(yh, yl)[:1], c, x, beside(yh, yl)[1])) for z, yh, c, x, yl in places()]


def swap_cores(value):
    return lax.ppermute(value, AXES, SWAP)


def exchange(value, members):
    return lax.all_to_all(value, AXES, 0, 0, tiled=True, axis_index_groups=members)


def core_index():
    return lax.rem(lax.axis_index("dp"), CORE)


def gelu_parts(pre):
    square = pre * pre
    bend = jnp.tanh(root * (pre + cubic * (pre * square)))
    act = 0.5 * pre * (1.0 + bend)
    slope = 0.5 * (1.0 + bend) + 0.5 * pre * (1.0 - bend * bend) * (root * (1.0 + 3.0 * cubic * square))
    return act, slope


def product(rows_ref, weight_ref):
    positions, piles, channels = rows_ref.shape
    return lax.dot_general(
        rows_ref[...].reshape(positions * piles, channels),
        weight_ref[...],
        (((1,), (1,)), ((), ())),
        preferred_element_type=jnp.float32,
    )


def head_half(head_ref, half):
    count = head_ref.shape[1] // 2
    whole = head_ref[...]
    chosen = jnp.where(half == 0, whole[:, :count], whole[:, count:])
    return [chosen[kind : kind + 1, :] for kind in range(head_ref.shape[0])]


def in_lanes(columns):
    lane = lax.broadcasted_iota(jnp.int32, (columns[0].shape[0], 128), 1)
    held = jnp.zeros(lane.shape, jnp.float32)
    for at, column in enumerate(columns):
        held = jnp.where(lane == at, column, held)
    return held


def spread(dlogits, heads, positions):
    dpooled = functools.reduce(jnp.add, [column * vector for column, vector in zip(dlogits, heads)])
    return jnp.concatenate([dpooled / positions] * positions, axis=0)


def prepare_kernel(weight_ref, out_ref, flip_ref):
    half = out_ref.shape[0]
    flip_ref[...] = weight_ref[...].T
    out_ref[...] = flip_ref[pl.ds(pl.multiple_of(core_index() * half, half), half), :].astype(jnp.bfloat16)


def forward_kernel(
    _, blocks_ref, rows_ref, others_ref, labels_ref, head_ref, weight_ref, slope_ref, logits_ref
):
    positions, piles, channels = rows_ref.shape
    width = channels // GROUP
    near = lax.rem(lax.axis_index("group"), YL) // PAIR
    for block in range(GROUP):
        yl = near * PAIR + block // 2 % PAIR
        shard = block // YL * YL + (yl if block % 2 == 0 else YL - 1 - yl)
        weight_ref[:, pl.ds(pl.multiple_of(shard * width, width), width)] = blocks_ref[block]
    heads = head_half(head_ref, core_index())
    across = lax.broadcasted_iota(jnp.int32, (piles, piles), 0) == lax.broadcasted_iota(
        jnp.int32, (piles, piles), 1
    )
    marks = jnp.sum(
        jnp.where(across, labels_ref[...].astype(jnp.float32), 0.0), axis=1, keepdims=True
    )
    for side, side_ref in enumerate((rows_ref, others_ref)):
        act, slope = gelu_parts(product(side_ref, weight_ref))
        slope_ref[side] = slope
        pooled = functools.reduce(
            jnp.add, [act[position * piles : (position + 1) * piles] for position in range(positions)]
        )
        pooled = pooled / positions
        logits = [jnp.sum(pooled * vector, axis=1, keepdims=True) for vector in heads]
        logits_ref[side] = in_lanes(logits + [marks] if side == 0 else logits)


def gradient_kernel(
    logits_ref, received_ref, slope_ref, rows_ref, others_ref, head_ref, grad_ref, dpre_ref, dlogits_ref
):
    positions, piles, channels = rows_ref.shape
    count = positions * piles
    classes = head_ref.shape[0]
    heads = head_half(head_ref, core_index())
    lefts = []
    for side in range(CORE):
        mine, theirs = logits_ref[side], received_ref[1 - side]
        marks = (mine if side == 0 else theirs)[:, classes : classes + 1]
        logits = [mine[:, kind : kind + 1] + theirs[:, kind : kind + 1] for kind in range(classes)]
        top = functools.reduce(jnp.maximum, logits)
        powers = [jnp.exp(value - top) for value in logits]
        total = functools.reduce(jnp.add, powers)
        dlogits = [
            powers[kind] / total - jnp.where(marks == float(kind), 1.0, 0.0) for kind in range(classes)
        ]
        dpre = spread(dlogits, heads, positions) * slope_ref[side]
        if side == 0:
            dpre_ref[...] = dpre.astype(jnp.bfloat16)
            dlogits_ref[...] = in_lanes(dlogits)
        lefts.append(dpre.T.astype(jnp.bfloat16))
    wide = channels // X
    width = wide // YL
    deep = lefts[0].shape[0] // PAIR
    for x in range(X):
        parts = [
            jnp.dot(
                left,
                side_ref[:, :, x * wide : (x + 1) * wide].reshape(count, wide),
                preferred_element_type=jnp.float32,
            )
            for left, side_ref in zip(lefts, (rows_ref, others_ref))
        ]
        total = (parts[0] + parts[1]).astype(jnp.bfloat16)
        for part in range(PAIR):
            for yl in range(YL):
                grad_ref[x, yl % PAIR, part, yl // PAIR] = total[
                    part * deep : (part + 1) * deep, yl * width : (yl + 1) * width
                ]


def input_kernel(
    _, weight_ref, other_ref, rows_ref, dpre_ref, dlogits_ref, head_ref, input_ref, held_ref, sems
):
    positions, piles, channels = rows_ref.shape
    heads = head_half(head_ref, 1 - core_index())
    slope = gelu_parts(product(rows_ref, other_ref))[1]
    dlogits = [dlogits_ref[:, kind : kind + 1] for kind in range(head_ref.shape[0])]
    rest = (spread(dlogits, heads, positions) * slope).astype(jnp.bfloat16)
    wide = channels // X
    copies = []
    for x in range(X):
        span = pl.ds(x * wide, wide)
        back = jnp.dot(dpre_ref[...], weight_ref[:, span], preferred_element_type=jnp.float32)
        back = back + jnp.dot(rest, other_ref[:, span], preferred_element_type=jnp.float32)
        held_ref[:, :, span] = back.astype(jnp.bfloat16).reshape(positions, piles, wide)
        copies.append(
            pltpu.make_async_copy(held_ref.at[:, :, span], input_ref.at[:, :, span], sems.at[x])
        )
        copies[-1].start()
    for copy in copies:
        copy.wait()


def stage_kernel(_, weight_ref, first_ref, second_ref, out_weight, out_first, out_second):
    out_weight[...] = weight_ref[...]
    out_first[...] = first_ref[...]
    out_second[...] = second_ref[...]


def adam_kernel(
    _, own_ref, other_ref, weight_ref, first_ref, second_ref, out_weight, out_first, out_second, flip_ref
):
    half = own_ref.shape[0]
    core = core_index()
    flip_ref[pl.ds(pl.multiple_of(core * half, half), half), :] = own_ref[...]
    flip_ref[pl.ds(pl.multiple_of((1 - core) * half, half), half), :] = other_ref[...]
    grad = flip_ref[...].T
    new_first = beta_one * first_ref[...] + (1.0 - beta_one) * grad
    new_second = beta_two * second_ref[...] + (1.0 - beta_two) * grad * grad
    first_hat = new_first / (1.0 - beta_one**bias_steps)
    second_hat = new_second / (1.0 - beta_two**bias_steps)
    out_weight[...] = weight_ref[...] - learn_rate * first_hat / (jnp.sqrt(second_hat) + epsilon)
    out_first[...] = new_first
    out_second[...] = new_second


def per_device(features, labels, weight, head, moment_one, moment_two):
    piles, positions, channels = features.shape
    shard, outputs = weight.shape
    count = piles * positions
    half_outs = outputs // 2
    deep = half_outs // PAIR
    rows = features.transpose(1, 0, 2)
    flat_head = head.T
    vmem = pl.BlockSpec(memory_space=pltpu.VMEM)
    anywhere = pl.BlockSpec(memory_space=pl.ANY)
    params = pltpu.CompilerParams(vmem_limit_bytes=16 << 20)

    half = pl.pallas_call(
        prepare_kernel,
        out_shape=jax.ShapeDtypeStruct((half_outs, shard), jnp.bfloat16),
        in_specs=[vmem],
        out_specs=vmem,
        scratch_shapes=[pltpu.VMEM((outputs, shard), jnp.float32)],
        compiler_params=params,
        name="prepare",
    )(weight)
    pair = jnp.stack([half, lax.ppermute(half, AXES, CROSS)])
    sent_rows, half = lax.optimization_barrier((rows, half))
    other_rows = swap_cores(sent_rows)
    staged = pl.pallas_call(
        stage_kernel,
        out_shape=(jax.ShapeDtypeStruct((shard, outputs), jnp.float32),) * 3,
        in_specs=[anywhere] + [vmem] * 3,
        out_specs=(vmem,) * 3,
        compiler_params=params,
        cost_estimate=pl.CostEstimate(flops=0, bytes_accessed=2 << 20, transcendentals=0),
        name="stage",
    )(half, weight, moment_one, moment_two)
    copies = jnp.broadcast_to(pair, (X * PAIR, PAIR, half_outs, shard))
    blocks = exchange(copies, OVER_XY).reshape(GROUP, half_outs, shard)

    flops = 2 * count * channels * outputs
    weight_half, slope, logits = pl.pallas_call(
        forward_kernel,
        out_shape=(
            jax.ShapeDtypeStruct((half_outs, channels), jnp.bfloat16),
            jax.ShapeDtypeStruct((CORE, count, half_outs), jnp.float32),
            jax.ShapeDtypeStruct((CORE, piles, 128), jnp.float32),
        ),
        in_specs=[anywhere] + [vmem] * 5,
        out_specs=(vmem,) * 3,
        compiler_params=params,
        cost_estimate=pl.CostEstimate(
            flops=flops, bytes_accessed=4 << 20, transcendentals=count * outputs
        ),
        name="forward",
    )(staged[0], blocks, rows, other_rows, labels.reshape(1, piles), flat_head)

    received = swap_cores(logits)
    other_half = swap_cores(weight_half)
    grad, dpre, dlogits = pl.pallas_call(
        gradient_kernel,
        out_shape=(
            jax.ShapeDtypeStruct((X, PAIR, PAIR, YL // PAIR, deep, shard), jnp.bfloat16),
            jax.ShapeDtypeStruct((count, half_outs), jnp.bfloat16),
            jax.ShapeDtypeStruct((piles, 128), jnp.float32),
        ),
        in_specs=[vmem] * 6,
        out_specs=(vmem,) * 3,
        compiler_params=params,
        cost_estimate=pl.CostEstimate(flops=flops, bytes_accessed=4 << 20, transcendentals=0),
        name="gradient",
    )(logits, received, slope, rows, other_rows, flat_head)

    both = grad.reshape(GROUP, -1, deep, shard)
    over_xyz = jnp.sum(exchange(both, OVER_XYZ).astype(jnp.float32), axis=0).astype(jnp.bfloat16)
    copies = jnp.concatenate([over_xyz] * YH, axis=0)
    over_y = jnp.sum(exchange(copies, OVER_Y).astype(jnp.float32), axis=0).astype(jnp.bfloat16)
    parts = exchange(jnp.broadcast_to(over_y, (Z, deep, shard)), OVER_Z)
    mine = jnp.sum(parts.reshape(PAIR, Z // PAIR, deep, shard).astype(jnp.float32), axis=1)
    mine = mine.reshape(half_outs, shard)

    theirs = swap_cores(mine)
    input_grad = pl.pallas_call(
        input_kernel,
        out_shape=jax.ShapeDtypeStruct((positions, piles, channels), jnp.bfloat16),
        in_specs=[anywhere] + [vmem] * 6,
        out_specs=anywhere,
        scratch_shapes=[
            pltpu.VMEM((positions, piles, channels), jnp.bfloat16),
            pltpu.SemaphoreType.DMA((X,)),
        ],
        compiler_params=params,
        cost_estimate=pl.CostEstimate(
            flops=flops, bytes_accessed=4 << 20, transcendentals=count * outputs
        ),
        name="input_grad",
    )(mine, weight_half, other_half, rows, dpre, dlogits, flat_head)

    new_weight, new_first, new_second = pl.pallas_call(
        adam_kernel,
        out_shape=(jax.ShapeDtypeStruct((shard, outputs), jnp.float32),) * 3,
        in_specs=[anywhere] + [vmem] * 5,
        out_specs=(vmem,) * 3,
        scratch_shapes=[pltpu.VMEM((outputs, shard), jnp.float32)],
        compiler_params=params,
        name="adam",
    )(input_grad, mine, theirs, *staged)
    return (input_grad.transpose(1, 0, 2), new_weight, new_first, new_second)


def solution(mesh):
    return jax.shard_map(
        per_device,
        mesh=mesh,
        in_specs=(
            P(("dp", "group"), None, None),
            P(("dp", "group")),
            P("group", None),
            P(),
            P("group", None),
            P("group", None),
        ),
        out_specs=(
            P(("dp", "group"), None, None),
            P("group", None),
            P("group", None),
            P("group", None),
        ),
        check_vma=False,
    )
```

time: 92.7 us -> 97.4 us (1.051)
  blocking collectives: 59 us -> 28.3 us
  starting transfers between devices: 21.8 us -> 35.9 us
  local copies, waits for them, and re-layouts: 1.09 us -> 9.95 us
  waiting for transfers between devices: 4.44 us -> 12.4 us
  Pallas kernels: 4.74 us -> 8 us
    all_to_all x4 -> x2, blocking collectives: 59 us -> 28.3 us  [exchange(): lax.all_to_all(value, AXES, 0, 0, tiled=True, axis_index_groups=members)]
    all_to_all x0 -> x2, waiting for transfers between devices: none -> 10.1 us  [exchange(): lax.all_to_all(value, AXES, 0, 0, tiled=True, axis_index_groups=members)]
    unnamed x12 -> x34, local copies, waits for them, and re-layouts: 0.03 us -> 8.89 us
    all_to_all x0 -> x2, starting transfers between devices: none -> 8.56 us  [exchange(): lax.all_to_all(value, AXES, 0, 0, tiled=True, axis_index_groups=members)]
    ppermute x3 -> x4, starting transfers between devices: 16.8 us -> 21.4 us  [swap_cores(): return lax.ppermute(value, AXES, SWAP)]
    pallas_call x2 -> x4, Pallas kernels: 3.67 us -> 6.93 us  [the longest x1 2.85 us: per_device(): pl.pallas_call(input_kernel, out_shape=jax.ShapeDtypeStruct((positions, p...]
    ppermute x3 -> x4, waiting for transfers between devices: 2.97 us -> 0.89 us  [swap_cores(): return lax.ppermute(value, AXES, SWAP)]
    reduce_sum x1, other arithmetic: 0.11 us -> 1.25 us  [per_device(): jnp.sum(exchange(both, OVER_XYZ).astype(jnp.float32), axis=0)]
  transfers between devices with their start and end apart: 4 -> 7, of which waited for: 4 -> 3; matrix products, arithmetic and copies ran while one was open for 0% -> 1% of each run, Pallas kernels for 2% -> 3%
where the time goes in v5:
time: 97.4 us; the launch traced here: 96.7 us
  starting transfers between devices  35.9 us (37%)
  blocking collectives  28.3 us (29%)
  waiting for transfers between devices  12.4 us (13%)
  local copies, waits for them, and re-layouts  9.95 us (10%)
  Pallas kernels  8 us (8%)
  other arithmetic  1.31 us (1%)
    all_to_all x2, blocking collectives, exchange(): lax.all_to_all(value, AXES, 0, 0, tiled=True, axis_index_groups=members)  28.3 us
    ppermute x4, starting transfers between devices, swap_cores(): return lax.ppermute(value, AXES, SWAP)  21.4 us
    all_to_all x2, waiting for transfers between devices, exchange(): lax.all_to_all(value, AXES, 0, 0, tiled=True, axis_index_groups=members)  10.1 us
    unnamed x34, local copies, waits for them, and re-layouts  8.89 us
    all_to_all x2, starting transfers between devices, exchange(): lax.all_to_all(value, AXES, 0, 0, tiled=True, axis_index_groups=members)  8.56 us
    ppermute x1, starting transfers between devices, per_device(): pair = jnp.stack([half, lax.ppermute(half, AXES, CROSS)])  5.93 us
    pallas_call x1, Pallas kernels, per_device(): pl.pallas_call(input_kernel, out_shape=jax.ShapeDtypeStruct((positions, p...  2.85 us
    pallas_call x1, Pallas kernels, per_device(): pl.pallas_call(gradient_kernel, out_shape=(jax.ShapeDtypeStruct((X, PAIR,...  2.37 us
  transfers between devices with their start and end apart: 7, of which 3 were waited for; matrix products, arithmetic and copies ran while one was open for 1% of the time, Pallas kernels for 3%

profile of v5, /device:TPU:1, one launch (start us, length us, event | category | flops | bytes accessed | tf_op | source)
XLA Modules:
  0.0 96.7 jit_solution(10364222748845360668)
XLA Ops:
  0.6 0.0 copy-start.4
  0.6 0.9 copy-done.4
  1.6 0.1 prepare.1._
  1.7 5.9 %collective-permute-start = (bf16[192,128]{1,0:T(8,128)(2,1)S(1)}, bf16[192,128]{1,0:T(8,128)(2,1)S(1)}, u32[]{:S(2)}, u32[]{:S(2)}) collective-permute-start(bf16[192,128]{1,0:T(8,128)(2,1)S(1)} %prepare.1._), channel_id=1, source_target_pairs={{0,35},{1,2},{2,1},{3,32},{4,39},{5,6},{6,5},{7,36},{8,43},{9,10},... | collective-permute-start | bytes 147464 | tf_op jit(solution)/shard_map/ppermute | solution.py:256
  7.6 1.5 %collective-permute-done = bf16[192,128]{1,0:T(8,128)(2,1)S(1)} collective-permute-done((bf16[192,128]{1,0:T(8,128)(2,1)S(1)}, bf16[192,128]{1,0:T(8,128)(2,1)S(1)}, u32[]{:S(2)}, u32[]{:S(2)}) %collective-permute-start) | collective-permute-done | bytes 49184 | tf_op jit(solution)/shard_map/ppermute | solution.py:256
  9.1 1.0 %broadcast_in_dim.6 = bf16[8,2,192,128]{3,2,1,0:T(8,128)(2,1)} broadcast(bf16[2,192,128]{2,1,0:T(8,128)(2,1)S(1)} %pad_maximum_fusion), dimensions={1,2,3} | broadcast | bytes 884736 | tf_op jit(solution)/shard_map/broadcast_in_dim | solution.py:268
  10.2 4.2 %all-to-all-start = ((bf16[8,2,192,128]{3,2,1,0:T(8,128)(2,1)}), bf16[8,2,192,128]{3,2,1,0:T(8,128)(2,1)S(1)}, u32[]{:S(2)}, u32[]{:S(2)}) async-start(bf16[8,2,192,128]{3,2,1,0:T(8,128)(2,1)} %broadcast_in_dim.6), calls=%async_computation | async-start | bytes 1572864 | tf_op jit(solution)/shard_map/all_to_all | solution.py:67
  14.3 0.0 copy-done
  14.3 8.1 %collective-permute-start.1 = (bf16[5,64,2048]{2,1,0:T(8,128)(2,1)S(1)}, bf16[5,64,2048]{2,1,0:T(8,128)(2,1)S(1)}, u32[]{:S(2)}, u32[]{:S(2)}) collective-permute-start(bf16[5,64,2048]{2,1,0:T(8,128)(2,1)S(1)} %bitcast.12), channel_id=1, source_target_pairs={{0,16},{1,17},{2,18},{3,19},{4,20},{5,21},{6,22},{7,23},{8,24},{9,... | collective-permute-start | bytes 3932168 | tf_op jit(solution)/shard_map/ppermute | solution.py:63
  22.4 0.0 copy-start.5
  22.4 0.9 copy-done.5
  23.4 0.9 copy-done.13
  24.3 0.9 copy-done.14
  25.3 0.0 copy-start.6
  25.3 0.7 copy-done.6
  25.9 0.7 copy-done.9
  26.6 0.7 copy-done.11
  27.3 0.0 collective-permute-done.1.others_ref
  27.3 0.0 all-to-all-done
  27.3 0.0 copy-done.15
  27.3 0.0 copy-done.16
  27.3 0.0 copy-start.7
  27.3 0.9 copy-done.7
  28.2 1.6 %forward.1 = (bf16[192,2048]{1,0:T(8,128)(2,1)S(1)}, f32[2,320,192]{2,1,0:T(8,128)S(1)}, f32[2,64,128]{2,1,0:T(8,128)S(1)}) custom-call(f32[128,384]{1,0:T(8,128)S(1)} %copy-done.7, bf16[16,192,128]{2,1,0:T(8,128)(2,1)S(1)} %bitcast.17, bf16[5,64,2048]{2,1,0:T(8,128)(2,1)S(1)} %bitcast.13, bf16[5,64,2048]{2,1,0:T(8,128)(2,1)S(1)} %collective-permute-done.1.others_ref, ...), custom_call_target="tpu_custom_call" | custom-call | flops 503316480 | bytes 4194304 | tf_op jit(solution)/shard_map/forward/pallas_call | solution.py:272
  29.8 0.0 copy-start.2
  29.8 0.9 copy-done.2
  30.7 5.1 %collective-permute-start.2 = (f32[2,64,128]{2,1,0:T(8,128)S(1)}, f32[2,64,128]{2,1,0:T(8,128)S(1)}, u32[]{:S(2)}, u32[]{:S(2)}) collective-permute-start(f32[2,64,128]{2,1,0:T(8,128)S(1)} %get-tuple-element.21.logits_ref), channel_id=1, source_target_pairs={{0,16},{1,17},{2,18},{3,19},{4,20},{5,21},{6,22},{7,23},{8,24},{9,... | collective-permute-start | bytes 196616 | tf_op jit(solution)/shard_map/ppermute | solution.py:63
  35.9 0.9 collective-permute-done.2.received_ref
  36.8 2.4 %gradient.1 = (bf16[4,2,2,2,96,128]{5,4,3,2,1,0:T(8,128)(2,1)}, bf16[320,192]{1,0:T(8,128)(2,1)S(1)}, f32[64,128]{1,0:T(8,128)S(1)}) custom-call(f32[2,64,128]{2,1,0:T(8,128)S(1)} %get-tuple-element.21.logits_ref, f32[2,64,128]{2,1,0:T(8,128)S(1)} %collective-permute-done.2.received_ref, f32[2,320,192]{2,1,0:T(8,128)S(1)} %get-tuple-element.22.slope_ref, ...), custom_call_target="tpu_custom_call" | custom-call | flops 503316480 | bytes 4194304 | tf_op jit(solution)/shard_map/gradient/pallas_call | solution.py:290
  39.1 4.4 %all-to-all-start.1 = ((bf16[16,2,96,128]{3,2,1,0:T(8,128)(2,1)}), bf16[16,2,96,128]{3,2,1,0:T(8,128)(2,1)}, u32[]{:S(2)}, u32[]{:S(2)}) async-start(bf16[16,2,96,128]{3,2,1,0:T(8,128)(2,1)} %bitcast.6), calls=%async_computation.1 | async-start | bytes 1572864 | tf_op jit(solution)/shard_map/all_to_all | solution.py:67
  43.6 2.3 %collective-permute-start.3 = (bf16[192,2048]{1,0:T(8,128)(2,1)S(1)}, bf16[192,2048]{1,0:T(8,128)(2,1)S(1)}, u32[]{:S(2)}, u32[]{:S(2)}) collective-permute-start(bf16[192,2048]{1,0:T(8,128)(2,1)S(1)} %copy-done.3), channel_id=1, source_target_pairs={{0,16},{1,17},{2,18},{3,19},{4,20},{5,21},{6,22},{7,23},{8,24},{9,... | collective-permute-start | bytes 2359304 | tf_op jit(solution)/shard_map/ppermute | solution.py:63
  45.8 10.1 %all-to-all-done.1 = bf16[16,2,96,128]{3,2,1,0:T(8,128)(2,1)} async-done(((bf16[16,2,96,128]{3,2,1,0:T(8,128)(2,1)}), bf16[16,2,96,128]{3,2,1,0:T(8,128)(2,1)}, u32[]{:S(2)}, u32[]{:S(2)}) %all-to-all-start.1) | async-done | bytes 786464 | tf_op jit(solution)/shard_map/all_to_all | solution.py:67
  55.9 1.2 %reduce_sum.33 = bf16[2,96,128]{2,1,0:T(8,128)(2,1)S(1)} reduce(bf16[16,2,96,128]{3,2,1,0:T(8,128)(2,1)} %all-to-all-done.1, bf16[]{:T(256)} %constant.3.clone.1), dimensions={0}, to_apply=%region_0.0 | reduce | flops 368640 | bytes 835586 | tf_op jit(solution)/shard_map/reduce_sum | solution.py:305
  57.1 11.3 %all_to_all.20 = bf16[4,96,128]{2,1,0:T(8,128)(2,1)S(1)} all-to-all(bf16[4,96,128]{2,1,0:T(8,128)(2,1)S(1)} %pad_maximum_fusion.1), channel_id=1, replica_groups={{0,2,32,34},{1,3,33,35},{4,6,36,38},{5,7,37,39},{8,10,40,42},{9,11,41,4..., dimensions={0} | all-to-all | bytes 196608 | tf_op jit(solution)/shard_map/all_to_all | solution.py:67
  68.5 16.9 %all_to_all.21 = bf16[8,96,128]{2,1,0:T(8,128)(2,1)S(1)} all-to-all(bf16[8,96,128]{2,1,0:T(8,128)(2,1)S(1)} %broadcast_in_dim.7), channel_id=1, replica_groups={{0,128,256,384,64,192,320,448},{1,129,257,385,65,193,321,449},{2,130,25..., dimensions={0} | all-to-all | bytes 393216 | tf_op jit(solution)/shard_map/all_to_all | solution.py:67
  85.5 5.9 %collective-permute-start.4 = (f32[192,128]{1,0:T(8,128)S(1)}, f32[192,128]{1,0:T(8,128)S(1)}, u32[]{:S(2)}, u32[]{:S(2)}) collective-permute-start(f32[192,128]{1,0:T(8,128)S(1)} %bitcast.18), channel_id=1, source_target_pairs={{0,16},{1,17},{2,18},{3,19},{4,20},{5,21},{6,22},{7,23},{8,24},{9,... | collective-permute-start | bytes 294920 | tf_op jit(solution)/shard_map/ppermute | solution.py:63
  91.4 0.0 collective-permute-done.3.other_ref
  91.4 0.0 copy-start.8
  91.4 0.0 copy-start.10
  91.4 0.0 copy-start.12
  91.4 2.9 %input_grad.1._ = bf16[5,64,2048]{2,1,0:T(8,128)(2,1)} custom-call(f32[192,128]{1,0:T(8,128)S(1)} %bitcast.19, bf16[192,2048]{1,0:T(8,128)(2,1)S(1)} %copy-done.3, bf16[192,2048]{1,0:T(8,128)(2,1)S(1)} %collective-permute-done.3.other_ref, bf16[5,64,2048]{2,1,0:T(8,128)(2,1)S(1)} %bitcast.15, bf16[320,192]{1,0:T(8,128)(2,1)S(1)} %get-tuple-element.25.dpre_ref, ...), custom_call_target="tpu_custom_call" | custom-call | flops 503316480 | bytes 4194304 | tf_op jit(solution)/shard_map/input_grad/pallas_call | solution.py:313
  94.3 0.0 collective-permute-done.4.other_ref
  94.3 0.0 copy-done.8
  94.3 0.0 copy-done.10
  94.3 0.0 copy-done.12
  94.3 0.0 copy-start.1
  94.3 1.3 %copy-done.1 = bf16[5,64,2048]{2,1,0:T(8,128)(2,1)S(1)} copy-done((bf16[5,64,2048]{2,1,0:T(8,128)(2,1)S(1)}, bf16[5,64,2048]{2,1,0:T(8,128)(2,1)}, u32[]{:S(2)}) %copy-start.1) | copy-done | bytes 1310744
  95.6 1.0 %adam.1 = (f32[128,384]{1,0:T(8,128)}, f32[128,384]{1,0:T(8,128)}, f32[128,384]{1,0:T(8,128)}) custom-call(bf16[5,64,2048]{2,1,0:T(8,128)(2,1)S(1)} %copy-done.1, f32[192,128]{1,0:T(8,128)S(1)} %bitcast.20, f32[192,128]{1,0:T(8,128)S(1)} %collective-permute-done.4.other_ref, f32[128,384]{1,0:T(8,128)S(1)} %copy-done.8, f32[128,384]{1,0:T(8,128)S(1)} %copy-done.10, ...), custom_call_target="tpu_custom_call" | custom-call | tf_op jit(solution)/shard_map/adam/pallas_call | solution.py:329
  (15 shorter events, 0.1 us)
Async XLA Ops:
  0.6 0.9 copy-start.4
  1.7 7.4 %collective-permute-start = (bf16[192,128]{1,0:T(8,128)(2,1)S(1)}, bf16[192,128]{1,0:T(8,128)(2,1)S(1)}, u32[]{:S(2)}, u32[]{:S(2)}) collective-permute-start(bf16[192,128]{1,0:T(8,128)(2,1)S(1)} %prepare.1._), channel_id=1, source_target_pairs={{0,35},{1,2},{2,1},{3,32},{4,39},{5,6},{6,5},{7,36},{8,43},{9,10},... | collective-permute-start | bytes 147464 | tf_op jit(solution)/shard_map/ppermute | solution.py:256
  9.1 5.2 %copy-start = (bf16[64,5,2048]{2,0,1:T(8,128)(2,1)S(1)}, bf16[64,5,2048]{2,0,1:T(8,128)(2,1)}, u32[]{:S(2)}) copy-start(bf16[64,5,2048]{2,0,1:T(8,128)(2,1)} %param.6) | copy-start | bytes 3932164
  10.2 17.1 %copy-start.15 = (f32[384,3]{0,1:T(4,128)S(1)}, f32[384,3]{0,1:T(4,128)}, u32[]{:S(2)}) copy-start(f32[384,3]{0,1:T(4,128)} %param.9) | copy-start | bytes 13828
  10.2 17.2 %copy-start.16 = (s32[64]{0:T(128)S(1)}, s32[64]{0:T(128)}, u32[]{:S(2)}) copy-start(s32[64]{0:T(128)} %param.7) | copy-start | bytes 772
  10.2 17.1 %all-to-all-start = ((bf16[8,2,192,128]{3,2,1,0:T(8,128)(2,1)}), bf16[8,2,192,128]{3,2,1,0:T(8,128)(2,1)S(1)}, u32[]{:S(2)}, u32[]{:S(2)}) async-start(bf16[8,2,192,128]{3,2,1,0:T(8,128)(2,1)} %broadcast_in_dim.6), calls=%async_computation | async-start | bytes 1572864 | tf_op jit(solution)/shard_map/all_to_all | solution.py:67
  14.3 13.0 %collective-permute-start.1 = (bf16[5,64,2048]{2,1,0:T(8,128)(2,1)S(1)}, bf16[5,64,2048]{2,1,0:T(8,128)(2,1)S(1)}, u32[]{:S(2)}, u32[]{:S(2)}) collective-permute-start(bf16[5,64,2048]{2,1,0:T(8,128)(2,1)S(1)} %bitcast.12), channel_id=1, source_target_pairs={{0,16},{1,17},{2,18},{3,19},{4,20},{5,21},{6,22},{7,23},{8,24},{9,... | collective-permute-start | bytes 3932168 | tf_op jit(solution)/shard_map/ppermute | solution.py:63
  22.4 0.9 copy-start.5
  23.4 0.9 copy-start.13
  24.3 0.9 copy-start.14
  25.3 0.7 copy-start.6
  25.9 0.7 copy-start.9
  26.6 0.7 copy-start.11
  27.3 0.9 copy-start.7
  29.8 0.9 copy-start.2
  30.7 6.0 %collective-permute-start.2 = (f32[2,64,128]{2,1,0:T(8,128)S(1)}, f32[2,64,128]{2,1,0:T(8,128)S(1)}, u32[]{:S(2)}, u32[]{:S(2)}) collective-permute-start(f32[2,64,128]{2,1,0:T(8,128)S(1)} %get-tuple-element.21.logits_ref), channel_id=1, source_target_pairs={{0,16},{1,17},{2,18},{3,19},{4,20},{5,21},{6,22},{7,23},{8,24},{9,... | collective-permute-start | bytes 196616 | tf_op jit(solution)/shard_map/ppermute | solution.py:63
  39.1 4.4 %copy-start.3 = (bf16[192,2048]{1,0:T(8,128)(2,1)S(1)}, bf16[192,2048]{1,0:T(8,128)(2,1)}, u32[]{:S(2)}) copy-start(bf16[192,2048]{1,0:T(8,128)(2,1)} %copy-done.2) | copy-start | bytes 2359300
  39.1 16.7 %all-to-all-start.1 = ((bf16[16,2,96,128]{3,2,1,0:T(8,128)(2,1)}), bf16[16,2,96,128]{3,2,1,0:T(8,128)(2,1)}, u32[]{:S(2)}, u32[]{:S(2)}) async-start(bf16[16,2,96,128]{3,2,1,0:T(8,128)(2,1)} %bitcast.6), calls=%async_computation.1 | async-start | bytes 1572864 | tf_op jit(solution)/shard_map/all_to_all | solution.py:67
  43.6 47.8 %collective-permute-start.3 = (bf16[192,2048]{1,0:T(8,128)(2,1)S(1)}, bf16[192,2048]{1,0:T(8,128)(2,1)S(1)}, u32[]{:S(2)}, u32[]{:S(2)}) collective-permute-start(bf16[192,2048]{1,0:T(8,128)(2,1)S(1)} %copy-done.3), channel_id=1, source_target_pairs={{0,16},{1,17},{2,18},{3,19},{4,20},{5,21},{6,22},{7,23},{8,24},{9,... | collective-permute-start | bytes 2359304 | tf_op jit(solution)/shard_map/ppermute | solution.py:63
  85.5 8.8 %collective-permute-start.4 = (f32[192,128]{1,0:T(8,128)S(1)}, f32[192,128]{1,0:T(8,128)S(1)}, u32[]{:S(2)}, u32[]{:S(2)}) collective-permute-start(f32[192,128]{1,0:T(8,128)S(1)} %bitcast.18), channel_id=1, source_target_pairs={{0,16},{1,17},{2,18},{3,19},{4,20},{5,21},{6,22},{7,23},{8,24},{9,... | collective-permute-start | bytes 294920 | tf_op jit(solution)/shard_map/ppermute | solution.py:63
  91.4 2.9 %copy-start.8 = (f32[128,384]{1,0:T(8,128)S(1)}, f32[128,384]{1,0:T(8,128)}, u32[]{:S(2)}) copy-start(f32[128,384]{1,0:T(8,128)} %copy-done.6) | copy-start | bytes 589828
  91.4 2.9 %copy-start.10 = (f32[128,384]{1,0:T(8,128)S(1)}, f32[128,384]{1,0:T(8,128)}, u32[]{:S(2)}) copy-start(f32[128,384]{1,0:T(8,128)} %copy-done.9) | copy-start | bytes 589828
  91.4 2.9 %copy-start.12 = (f32[128,384]{1,0:T(8,128)S(1)}, f32[128,384]{1,0:T(8,128)}, u32[]{:S(2)}) copy-start(f32[128,384]{1,0:T(8,128)} %copy-done.11) | copy-start | bytes 589828
  94.3 1.3 %copy-start.1 = (bf16[5,64,2048]{2,1,0:T(8,128)(2,1)S(1)}, bf16[5,64,2048]{2,1,0:T(8,128)(2,1)}, u32[]{:S(2)}) copy-start(bf16[5,64,2048]{2,1,0:T(8,128)(2,1)} %input_grad.1._) | copy-start | bytes 3932164

commit v6 on v5

--- a/solution.py
+++ b/solution.py
@@ -115,16 +115,20 @@
     out_ref[...] = flip_ref[pl.ds(pl.multiple_of(core_index() * half, half), half), :].astype(jnp.bfloat16)
 
 
-def forward_kernel(
-    _, blocks_ref, rows_ref, others_ref, labels_ref, head_ref, weight_ref, slope_ref, logits_ref
-):
-    positions, piles, channels = rows_ref.shape
-    width = channels // GROUP
+def assemble(blocks_ref, weight_ref):
+    width = blocks_ref.shape[2]
     near = lax.rem(lax.axis_index("group"), YL) // PAIR
     for block in range(GROUP):
         yl = near * PAIR + block // 2 % PAIR
         shard = block // YL * YL + (yl if block % 2 == 0 else YL - 1 - yl)
         weight_ref[:, pl.ds(pl.multiple_of(shard * width, width), width)] = blocks_ref[block]
+
+
+def forward_kernel(
+    blocks_ref, rows_ref, others_ref, labels_ref, head_ref, slope_ref, logits_ref, weight_ref
+):
+    positions, piles, channels = rows_ref.shape
+    assemble(blocks_ref, weight_ref)
     heads = head_half(head_ref, core_index())
     across = lax.broadcasted_iota(jnp.int32, (piles, piles), 0) == lax.broadcasted_iota(
         jnp.int32, (piles, piles), 1
@@ -186,10 +190,21 @@
                 ]
 
 
+def sum_kernel(parts_ref, out_ref):
+    count, rows = parts_ref.shape[:2]
+    total = parts_ref[0].astype(jnp.float32)
+    for at in range(1, count):
+        total = total + parts_ref[at].astype(jnp.float32)
+    for copy in range(out_ref.shape[0] // rows):
+        out_ref[copy * rows : (copy + 1) * rows] = total.astype(jnp.bfloat16)
+
+
 def input_kernel(
-    _, weight_ref, other_ref, rows_ref, dpre_ref, dlogits_ref, head_ref, input_ref, held_ref, sems
+    blocks_ref, others_ref, rows_ref, dpre_ref, dlogits_ref, head_ref, input_ref, weight_ref, other_ref, held_ref, sems
 ):
     positions, piles, channels = rows_ref.shape
+    assemble(blocks_ref, weight_ref)
+    assemble(others_ref, other_ref)
     heads = head_half(head_ref, 1 - core_index())
     slope = gelu_parts(product(rows_ref, other_ref))[1]
     dlogits = [dlogits_ref[:, kind : kind + 1] for kind in range(head_ref.shape[0])]
@@ -209,14 +224,8 @@
         copy.wait()
 
 
-def stage_kernel(_, weight_ref, first_ref, second_ref, out_weight, out_first, out_second):
-    out_weight[...] = weight_ref[...]
-    out_first[...] = first_ref[...]
-    out_second[...] = second_ref[...]
-
-
 def adam_kernel(
-    _, own_ref, other_ref, weight_ref, first_ref, second_ref, out_weight, out_first, out_second, flip_ref
+    own_ref, other_ref, weight_ref, first_ref, second_ref, out_weight, out_first, out_second, flip_ref
 ):
     half = own_ref.shape[0]
     core = core_index()
@@ -254,39 +263,29 @@
         name="prepare",
     )(weight)
     pair = jnp.stack([half, lax.ppermute(half, AXES, CROSS)])
-    sent_rows, half = lax.optimization_barrier((rows, half))
+    sent_rows, pair = lax.optimization_barrier((rows, pair))
     other_rows = swap_cores(sent_rows)
-    staged = pl.pallas_call(
-        stage_kernel,
-        out_shape=(jax.ShapeDtypeStruct((shard, outputs), jnp.float32),) * 3,
-        in_specs=[anywhere] + [vmem] * 3,
-        out_specs=(vmem,) * 3,
-        compiler_params=params,
-        cost_estimate=pl.CostEstimate(flops=0, bytes_accessed=2 << 20, transcendentals=0),
-        name="stage",
-    )(half, weight, moment_one, moment_two)
     copies = jnp.broadcast_to(pair, (X * PAIR, PAIR, half_outs, shard))
     blocks = exchange(copies, OVER_XY).reshape(GROUP, half_outs, shard)
 
     flops = 2 * count * channels * outputs
-    weight_half, slope, logits = pl.pallas_call(
+    slope, logits = pl.pallas_call(
         forward_kernel,
         out_shape=(
-            jax.ShapeDtypeStruct((half_outs, channels), jnp.bfloat16),
             jax.ShapeDtypeStruct((CORE, count, half_outs), jnp.float32),
             jax.ShapeDtypeStruct((CORE, piles, 128), jnp.float32),
         ),
-        in_specs=[anywhere] + [vmem] * 5,
-        out_specs=(vmem,) * 3,
+        in_specs=[vmem] * 5,
+        out_specs=(vmem,) * 2,
+        scratch_shapes=[pltpu.VMEM((half_outs, channels), jnp.bfloat16)],
         compiler_params=params,
         cost_estimate=pl.CostEstimate(
             flops=flops, bytes_accessed=4 << 20, transcendentals=count * outputs
         ),
         name="forward",
-    )(staged[0], blocks, rows, other_rows, labels.reshape(1, piles), flat_head)
+    )(blocks, rows, other_rows, labels.reshape(1, piles), flat_head)
 
     received = swap_cores(logits)
-    other_half = swap_cores(weight_half)
     grad, dpre, dlogits = pl.pallas_call(
         gradient_kernel,
         out_shape=(
@@ -302,39 +301,49 @@
     )(logits, received, slope, rows, other_rows, flat_head)
 
     both = grad.reshape(GROUP, -1, deep, shard)
-    over_xyz = jnp.sum(exchange(both, OVER_XYZ).astype(jnp.float32), axis=0).astype(jnp.bfloat16)
-    copies = jnp.concatenate([over_xyz] * YH, axis=0)
+    parts = exchange(both, OVER_XYZ)
+    other_blocks = swap_cores(blocks)
+    input_grad = pl.pallas_call(
+        input_kernel,
+        out_shape=jax.ShapeDtypeStruct((positions, piles, channels), jnp.bfloat16),
+        in_specs=[vmem] * 6,
+        out_specs=anywhere,
+        scratch_shapes=[
+            pltpu.VMEM((half_outs, channels), jnp.bfloat16),
+            pltpu.VMEM((half_outs, channels), jnp.bfloat16),
+            pltpu.VMEM((positions, piles, channels), jnp.bfloat16),
+            pltpu.SemaphoreType.DMA((X,)),
+        ],
+        compiler_params=params,
+        cost_estimate=pl.CostEstimate(
+            flops=flops, bytes_accessed=4 << 20, transcendentals=count * outputs
+        ),
+        name="input_grad",
+    )(blocks, other_blocks, rows, dpre, dlogits, flat_head)
+    parts, input_grad = lax.optimization_barrier((parts, input_grad))
+    copies = pl.pallas_call(
+        sum_kernel,
+        out_shape=jax.ShapeDtypeStruct((YH * parts.shape[1], deep, shard), jnp.bfloat16),
+        in_specs=[vmem],
+        out_specs=vmem,
+        compiler_params=params,
+        name="sum",
+    )(parts)
     over_y = jnp.sum(exchange(copies, OVER_Y).astype(jnp.float32), axis=0).astype(jnp.bfloat16)
     parts = exchange(jnp.broadcast_to(over_y, (Z, deep, shard)), OVER_Z)
     mine = jnp.sum(parts.reshape(PAIR, Z // PAIR, deep, shard).astype(jnp.float32), axis=1)
     mine = mine.reshape(half_outs, shard)
 
     theirs = swap_cores(mine)
-    input_grad = pl.pallas_call(
-        input_kernel,
-        out_shape=jax.ShapeDtypeStruct((positions, piles, channels), jnp.bfloat16),
-        in_specs=[anywhere] + [vmem] * 6,
-        out_specs=anywhere,
-        scratch_shapes=[
-            pltpu.VMEM((positions, piles, channels), jnp.bfloat16),
-            pltpu.SemaphoreType.DMA((X,)),
-        ],
-        compiler_params=params,
-        cost_estimate=pl.CostEstimate(
-            flops=flops, bytes_accessed=4 << 20, transcendentals=count * outputs
-        ),
-        name="input_grad",
-    )(mine, weight_half, other_half, rows, dpre, dlogits, flat_head)
-
     new_weight, new_first, new_second = pl.pallas_call(
         adam_kernel,
         out_shape=(jax.ShapeDtypeStruct((shard, outputs), jnp.float32),) * 3,
-        in_specs=[anywhere] + [vmem] * 5,
+        in_specs=[vmem] * 5,
         out_specs=(vmem,) * 3,
         scratch_shapes=[pltpu.VMEM((outputs, shard), jnp.float32)],
         compiler_params=params,
         name="adam",
-    )(input_grad, mine, theirs, *staged)
+    )(mine, theirs, weight, moment_one, moment_two)
     return (input_grad.transpose(1, 0, 2), new_weight, new_first, new_second)
 
 

time: 97.4 us -> 91.1 us (0.935)
  local copies, waits for them, and re-layouts: 9.95 us -> 3.58 us
  starting transfers between devices: 35.9 us -> 37.8 us
  other arithmetic: 1.31 us -> 0.05 us
    unnamed x34 -> x20, local copies, waits for them, and re-layouts: 8.89 us -> 2.52 us
    ppermute x4, waiting for transfers between devices: 0.89 us -> 6.35 us  [swap_cores(): return lax.ppermute(value, AXES, SWAP)]
    all_to_all x2, waiting for transfers between devices: 10.1 us -> 4.83 us  [exchange(): lax.all_to_all(value, AXES, 0, 0, tiled=True, axis_index_groups=members)]
    ppermute x4, starting transfers between devices: 21.4 us -> 24.1 us  [swap_cores(): return lax.ppermute(value, AXES, SWAP)]
    reduce_sum x1 -> x0, other arithmetic: 1.25 us -> none  [per_device(): jnp.sum(exchange(both, OVER_XYZ).astype(jnp.float32), axis=0)]
  transfers between devices with their start and end apart: 7 -> 7, of which waited for: 3 -> 6; matrix products, arithmetic and copies ran while one was open for 1% -> 0% of each run, Pallas kernels for 3% -> 4%
where the time goes in v6:
time: 91.1 us; the launch traced here: 90.6 us
  starting transfers between devices  37.8 us (41%)
  blocking collectives  28.2 us (31%)
  waiting for transfers between devices  12.6 us (14%)
  Pallas kernels  7.51 us (8%)
  local copies, waits for them, and re-layouts  3.58 us (4%)
    all_to_all x2, blocking collectives, exchange(): lax.all_to_all(value, AXES, 0, 0, tiled=True, axis_index_groups=members)  28.2 us
    ppermute x4, starting transfers between devices, swap_cores(): return lax.ppermute(value, AXES, SWAP)  24.1 us
    all_to_all x2, starting transfers between devices, exchange(): lax.all_to_all(value, AXES, 0, 0, tiled=True, axis_index_groups=members)  7.76 us
    ppermute x4, waiting for transfers between devices, swap_cores(): return lax.ppermute(value, AXES, SWAP)  6.35 us
    ppermute x1, starting transfers between devices, per_device(): pair = jnp.stack([half, lax.ppermute(half, AXES, CROSS)])  5.93 us
    all_to_all x2, waiting for transfers between devices, exchange(): lax.all_to_all(value, AXES, 0, 0, tiled=True, axis_index_groups=members)  4.83 us
    pallas_call x1, Pallas kernels, per_device(): pl.pallas_call(input_kernel, out_shape=jax.ShapeDtypeStruct((positions, p...  3.22 us
    unnamed x20, local copies, waits for them, and re-layouts  2.52 us
  transfers between devices with their start and end apart: 7, of which 6 were waited for; matrix products, arithmetic and copies ran while one was open for 0% of the time, Pallas kernels for 4%

profile of v6, /device:TPU:1, one launch (start us, length us, event | category | flops | bytes accessed | tf_op | source)
XLA Modules:
  0.0 90.6 jit_solution(1732404902092270064)
XLA Ops:
  0.6 0.0 copy-start.2
  0.6 0.9 %copy-done.2 = f32[128,384]{1,0:T(8,128)S(1)} copy-done((f32[128,384]{1,0:T(8,128)S(1)}, f32[128,384]{1,0:T(8,128)}, u32[]{:S(2)}) %copy-start.2) | copy-done | bytes 196632
  1.6 0.1 prepare.1
  1.7 5.9 %collective-permute-start = (bf16[192,128]{1,0:T(8,128)(2,1)S(1)}, bf16[192,128]{1,0:T(8,128)(2,1)S(1)}, u32[]{:S(2)}, u32[]{:S(2)}) collective-permute-start(bf16[192,128]{1,0:T(8,128)(2,1)S(1)} %prepare.1), channel_id=1, source_target_pairs={{0,35},{1,2},{2,1},{3,32},{4,39},{5,6},{6,5},{7,36},{8,43},{9,10},... | collective-permute-start | bytes 147464 | tf_op jit(solution)/shard_map/ppermute | solution.py:265
  7.6 1.5 %collective-permute-done = bf16[192,128]{1,0:T(8,128)(2,1)S(1)} collective-permute-done((bf16[192,128]{1,0:T(8,128)(2,1)S(1)}, bf16[192,128]{1,0:T(8,128)(2,1)S(1)}, u32[]{:S(2)}, u32[]{:S(2)}) %collective-permute-start) | collective-permute-done | bytes 49184 | tf_op jit(solution)/shard_map/ppermute | solution.py:265
  9.1 0.0 copy-start
  9.1 0.0 copy-start.8
  9.1 0.0 copy-start.9
  9.1 1.0 %broadcast_in_dim.6 = bf16[8,2,192,128]{3,2,1,0:T(8,128)(2,1)} broadcast(bf16[2,192,128]{2,1,0:T(8,128)(2,1)S(1)} %pad_maximum_fusion), dimensions={1,2,3} | broadcast | bytes 884736 | tf_op jit(solution)/shard_map/broadcast_in_dim | solution.py:268
  10.2 4.0 %all-to-all-start = ((bf16[8,2,192,128]{3,2,1,0:T(8,128)(2,1)}), bf16[8,2,192,128]{3,2,1,0:T(8,128)(2,1)S(1)}, u32[]{:S(2)}, u32[]{:S(2)}) async-start(bf16[8,2,192,128]{3,2,1,0:T(8,128)(2,1)} %broadcast_in_dim.6), calls=%async_computation | async-start | bytes 1572864 | tf_op jit(solution)/shard_map/all_to_all | solution.py:67
  14.2 0.0 copy-done
  14.2 8.1 %collective-permute-start.1 = (bf16[5,64,2048]{2,1,0:T(8,128)(2,1)S(1)}, bf16[5,64,2048]{2,1,0:T(8,128)(2,1)S(1)}, u32[]{:S(2)}, u32[]{:S(2)}) collective-permute-start(bf16[5,64,2048]{2,1,0:T(8,128)(2,1)S(1)} %bitcast.12), channel_id=1, source_target_pairs={{0,16},{1,17},{2,18},{3,19},{4,20},{5,21},{6,22},{7,23},{8,24},{9,... | collective-permute-start | bytes 3932168 | tf_op jit(solution)/shard_map/ppermute | solution.py:63
  22.3 2.6 %collective-permute-done.1.others_ref = bf16[5,64,2048]{2,1,0:T(8,128)(2,1)S(1)} collective-permute-done((bf16[5,64,2048]{2,1,0:T(8,128)(2,1)S(1)}, bf16[5,64,2048]{2,1,0:T(8,128)(2,1)S(1)}, u32[]{:S(2)}, u32[]{:S(2)}) %collective-permute-start.1) | collective-permute-done | bytes 1310752 | tf_op jit(solution)/shard_map/ppermute | solution.py:63
  24.9 0.0 all-to-all-done
  24.9 0.0 copy-done.8
  24.9 0.0 copy-done.9
  25.0 1.5 %forward.1 = (f32[2,320,192]{2,1,0:T(8,128)S(1)}, f32[2,64,128]{2,1,0:T(8,128)S(1)}) custom-call(bf16[16,192,128]{2,1,0:T(8,128)(2,1)S(1)} %bitcast.16, bf16[5,64,2048]{2,1,0:T(8,128)(2,1)S(1)} %bitcast.13, bf16[5,64,2048]{2,1,0:T(8,128)(2,1)S(1)} %collective-permute-done.1.others_ref, s32[1,64]{1,0:T(1,128)S(1)} %bitcast.26, f32[3,384]{1,0:T(4,128)S(1)} %bitcast.23), custom_call_target="tpu_custom_call" | custom-call | flops 503316480 | bytes 4194304 | tf_op jit(solution)/shard_map/forward/pallas_call | solution.py:272
  26.5 7.4 %collective-permute-start.2 = (f32[2,64,128]{2,1,0:T(8,128)S(1)}, f32[2,64,128]{2,1,0:T(8,128)S(1)}, u32[]{:S(2)}, u32[]{:S(2)}) collective-permute-start(f32[2,64,128]{2,1,0:T(8,128)S(1)} %get-tuple-element.18.logits_ref), channel_id=1, source_target_pairs={{0,16},{1,17},{2,18},{3,19},{4,20},{5,21},{6,22},{7,23},{8,24},{9,... | collective-permute-start | bytes 196616 | tf_op jit(solution)/shard_map/ppermute | solution.py:63
  33.9 0.9 collective-permute-done.2.received_ref
  34.8 1.5 %gradient.1 = (bf16[4,2,2,2,96,128]{5,4,3,2,1,0:T(8,128)(2,1)S(1)}, bf16[320,192]{1,0:T(8,128)(2,1)S(1)}, f32[64,128]{1,0:T(8,128)S(1)}) custom-call(f32[2,64,128]{2,1,0:T(8,128)S(1)} %get-tuple-element.18.logits_ref, f32[2,64,128]{2,1,0:T(8,128)S(1)} %collective-permute-done.2.received_ref, f32[2,320,192]{2,1,0:T(8,128)S(1)} %get-tuple-element.19.slope_ref, ...), custom_call_target="tpu_custom_call" | custom-call | flops 503316480 | bytes 4194304 | tf_op jit(solution)/shard_map/gradient/pallas_call | solution.py:289
  36.3 0.0 copy-start.1
  36.3 0.9 copy-done.1
  37.2 0.0 copy-start.6
  37.2 0.7 copy-done.6
  37.8 0.0 copy-start.7
  37.8 3.7 %all-to-all-start.1 = ((bf16[16,2,96,128]{3,2,1,0:T(8,128)(2,1)}), bf16[16,2,96,128]{3,2,1,0:T(8,128)(2,1)S(1)}, u32[]{:S(2)}, u32[]{:S(2)}) async-start(bf16[16,2,96,128]{3,2,1,0:T(8,128)(2,1)} %bitcast.19), calls=%async_computation.1 | async-start | bytes 1572864 | tf_op jit(solution)/shard_map/all_to_all | solution.py:67
  41.6 2.3 %collective-permute-start.3 = (bf16[16,192,128]{2,1,0:T(8,128)(2,1)S(1)}, bf16[16,192,128]{2,1,0:T(8,128)(2,1)S(1)}, u32[]{:S(2)}, u32[]{:S(2)}) collective-permute-start(bf16[16,192,128]{2,1,0:T(8,128)(2,1)S(1)} %bitcast.17), channel_id=1, source_target_pairs={{0,16},{1,17},{2,18},{3,19},{4,20},{5,21},{6,22},{7,23},{8,24},{9,... | collective-permute-start | bytes 2359304 | tf_op jit(solution)/shard_map/ppermute | solution.py:63
  43.9 1.9 %collective-permute-done.3.others_ref = bf16[16,192,128]{2,1,0:T(8,128)(2,1)S(1)} collective-permute-done((bf16[16,192,128]{2,1,0:T(8,128)(2,1)S(1)}, bf16[16,192,128]{2,1,0:T(8,128)(2,1)S(1)}, u32[]{:S(2)}, u32[]{:S(2)}) %collective-permute-start.3) | collective-permute-done | bytes 786464 | tf_op jit(solution)/shard_map/ppermute | solution.py:63
  45.8 0.0 copy-done.7
  45.8 3.2 %input_grad.1 = bf16[5,64,2048]{2,1,0:T(8,128)(2,1)} custom-call(bf16[16,192,128]{2,1,0:T(8,128)(2,1)S(1)} %bitcast.18, bf16[16,192,128]{2,1,0:T(8,128)(2,1)S(1)} %collective-permute-done.3.others_ref, bf16[5,64,2048]{2,1,0:T(8,128)(2,1)S(1)} %bitcast.15, bf16[320,192]{1,0:T(8,128)(2,1)S(1)} %copy-done.7, f32[64,128]{1,0:T(8,128)S(1)} %get-tuple-element.22.dlogits_ref, ...), custom_call_target="tpu_custom_call" | custom-call | flops 503316480 | bytes 4194304 | tf_op jit(solution)/shard_map/input_grad/pallas_call | solution.py:306
  49.0 0.0 copy-start.3
  49.0 0.0 copy-start.4
  49.0 0.0 copy-start.5
  49.0 4.8 %all-to-all-done.1.parts_ref = bf16[16,2,96,128]{3,2,1,0:T(8,128)(2,1)S(1)} async-done(((bf16[16,2,96,128]{3,2,1,0:T(8,128)(2,1)}), bf16[16,2,96,128]{3,2,1,0:T(8,128)(2,1)S(1)}, u32[]{:S(2)}, u32[]{:S(2)}) %all-to-all-start.1) | async-done | bytes 786464 | tf_op jit(solution)/shard_map/all_to_all | solution.py:67
  53.9 0.1 sum.1
  54.0 12.0 %all_to_all.20 = bf16[4,96,128]{2,1,0:T(8,128)(2,1)S(1)} all-to-all(bf16[4,96,128]{2,1,0:T(8,128)(2,1)S(1)} %sum.1), channel_id=1, replica_groups={{0,2,32,34},{1,3,33,35},{4,6,36,38},{5,7,37,39},{8,10,40,42},{9,11,41,4..., dimensions={0} | all-to-all | bytes 196608 | tf_op jit(solution)/shard_map/all_to_all | solution.py:67
  66.0 16.3 %all_to_all.21 = bf16[8,96,128]{2,1,0:T(8,128)(2,1)S(1)} all-to-all(bf16[8,96,128]{2,1,0:T(8,128)(2,1)S(1)} %broadcast_in_dim.7), channel_id=1, replica_groups={{0,128,256,384,64,192,320,448},{1,129,257,385,65,193,321,449},{2,130,25..., dimensions={0} | all-to-all | bytes 393216 | tf_op jit(solution)/shard_map/all_to_all | solution.py:67
  82.3 6.3 %collective-permute-start.4 = (f32[192,128]{1,0:T(8,128)S(1)}, f32[192,128]{1,0:T(8,128)S(1)}, u32[]{:S(2)}, u32[]{:S(2)}) collective-permute-start(f32[192,128]{1,0:T(8,128)S(1)} %bitcast.20), channel_id=1, source_target_pairs={{0,16},{1,17},{2,18},{3,19},{4,20},{5,21},{6,22},{7,23},{8,24},{9,... | collective-permute-start | bytes 294920 | tf_op jit(solution)/shard_map/ppermute | solution.py:63
  88.6 0.9 %collective-permute-done.4.other_ref = f32[192,128]{1,0:T(8,128)S(1)} collective-permute-done((f32[192,128]{1,0:T(8,128)S(1)}, f32[192,128]{1,0:T(8,128)S(1)}, u32[]{:S(2)}, u32[]{:S(2)}) %collective-permute-start.4) | collective-permute-done | bytes 98336 | tf_op jit(solution)/shard_map/ppermute | solution.py:63
  89.5 0.0 copy-done.3
  89.5 0.0 copy-done.4
  89.5 0.0 copy-done.5
  89.5 1.0 %adam.1 = (f32[128,384]{1,0:T(8,128)}, f32[128,384]{1,0:T(8,128)}, f32[128,384]{1,0:T(8,128)}) custom-call(f32[192,128]{1,0:T(8,128)S(1)} %bitcast.21, f32[192,128]{1,0:T(8,128)S(1)} %collective-permute-done.4.other_ref, f32[128,384]{1,0:T(8,128)S(1)} %copy-done.3, f32[128,384]{1,0:T(8,128)S(1)} %copy-done.4, f32[128,384]{1,0:T(8,128)S(1)} %copy-done.5), custom_call_target="tpu_custom_call" | custom-call | tf_op jit(solution)/shard_map/adam/pallas_call | solution.py:338
  (4 shorter events, 0.1 us)
Async XLA Ops:
  0.6 0.9 %copy-start.2 = (f32[128,384]{1,0:T(8,128)S(1)}, f32[128,384]{1,0:T(8,128)}, u32[]{:S(2)}) copy-start(f32[128,384]{1,0:T(8,128)} %weight_ref.3) | copy-start | bytes 589828
  1.7 7.4 %collective-permute-start = (bf16[192,128]{1,0:T(8,128)(2,1)S(1)}, bf16[192,128]{1,0:T(8,128)(2,1)S(1)}, u32[]{:S(2)}, u32[]{:S(2)}) collective-permute-start(bf16[192,128]{1,0:T(8,128)(2,1)S(1)} %prepare.1), channel_id=1, source_target_pairs={{0,35},{1,2},{2,1},{3,32},{4,39},{5,6},{6,5},{7,36},{8,43},{9,10},... | collective-permute-start | bytes 147464 | tf_op jit(solution)/shard_map/ppermute | solution.py:265
  9.1 5.1 %copy-start = (bf16[64,5,2048]{2,0,1:T(8,128)(2,1)S(1)}, bf16[64,5,2048]{2,0,1:T(8,128)(2,1)}, u32[]{:S(2)}) copy-start(bf16[64,5,2048]{2,0,1:T(8,128)(2,1)} %param.6) | copy-start | bytes 3932164
  9.1 15.8 %copy-start.8 = (f32[384,3]{0,1:T(4,128)S(1)}, f32[384,3]{0,1:T(4,128)}, u32[]{:S(2)}) copy-start(f32[384,3]{0,1:T(4,128)} %param.9) | copy-start | bytes 13828
  9.1 15.8 %copy-start.9 = (s32[64]{0:T(128)S(1)}, s32[64]{0:T(128)}, u32[]{:S(2)}) copy-start(s32[64]{0:T(128)} %param.7) | copy-start | bytes 772
  10.2 14.8 %all-to-all-start = ((bf16[8,2,192,128]{3,2,1,0:T(8,128)(2,1)}), bf16[8,2,192,128]{3,2,1,0:T(8,128)(2,1)S(1)}, u32[]{:S(2)}, u32[]{:S(2)}) async-start(bf16[8,2,192,128]{3,2,1,0:T(8,128)(2,1)} %broadcast_in_dim.6), calls=%async_computation | async-start | bytes 1572864 | tf_op jit(solution)/shard_map/all_to_all | solution.py:67
  14.2 10.8 %collective-permute-start.1 = (bf16[5,64,2048]{2,1,0:T(8,128)(2,1)S(1)}, bf16[5,64,2048]{2,1,0:T(8,128)(2,1)S(1)}, u32[]{:S(2)}, u32[]{:S(2)}) collective-permute-start(bf16[5,64,2048]{2,1,0:T(8,128)(2,1)S(1)} %bitcast.12), channel_id=1, source_target_pairs={{0,16},{1,17},{2,18},{3,19},{4,20},{5,21},{6,22},{7,23},{8,24},{9,... | collective-permute-start | bytes 3932168 | tf_op jit(solution)/shard_map/ppermute | solution.py:63
  26.5 8.3 %collective-permute-start.2 = (f32[2,64,128]{2,1,0:T(8,128)S(1)}, f32[2,64,128]{2,1,0:T(8,128)S(1)}, u32[]{:S(2)}, u32[]{:S(2)}) collective-permute-start(f32[2,64,128]{2,1,0:T(8,128)S(1)} %get-tuple-element.18.logits_ref), channel_id=1, source_target_pairs={{0,16},{1,17},{2,18},{3,19},{4,20},{5,21},{6,22},{7,23},{8,24},{9,... | collective-permute-start | bytes 196616 | tf_op jit(solution)/shard_map/ppermute | solution.py:63
  36.3 0.9 copy-start.1
  37.2 0.7 copy-start.6
  37.8 7.9 %copy-start.7 = (bf16[320,192]{1,0:T(8,128)(2,1)S(1)}, bf16[320,192]{1,0:T(8,128)(2,1)}, u32[]{:S(2)}) copy-start(bf16[320,192]{1,0:T(8,128)(2,1)} %copy-done.6) | copy-start | bytes 368644
  37.8 16.0 %all-to-all-start.1 = ((bf16[16,2,96,128]{3,2,1,0:T(8,128)(2,1)}), bf16[16,2,96,128]{3,2,1,0:T(8,128)(2,1)S(1)}, u32[]{:S(2)}, u32[]{:S(2)}) async-start(bf16[16,2,96,128]{3,2,1,0:T(8,128)(2,1)} %bitcast.19), calls=%async_computation.1 | async-start | bytes 1572864 | tf_op jit(solution)/shard_map/all_to_all | solution.py:67
  41.6 4.2 %collective-permute-start.3 = (bf16[16,192,128]{2,1,0:T(8,128)(2,1)S(1)}, bf16[16,192,128]{2,1,0:T(8,128)(2,1)S(1)}, u32[]{:S(2)}, u32[]{:S(2)}) collective-permute-start(bf16[16,192,128]{2,1,0:T(8,128)(2,1)S(1)} %bitcast.17), channel_id=1, source_target_pairs={{0,16},{1,17},{2,18},{3,19},{4,20},{5,21},{6,22},{7,23},{8,24},{9,... | collective-permute-start | bytes 2359304 | tf_op jit(solution)/shard_map/ppermute | solution.py:63
  49.0 40.5 %copy-start.3 = (f32[128,384]{1,0:T(8,128)S(1)}, f32[128,384]{1,0:T(8,128)}, u32[]{:S(2)}) copy-start(f32[128,384]{1,0:T(8,128)} %weight_ref.3) | copy-start | bytes 589828
  49.0 40.5 %copy-start.4 = (f32[128,384]{1,0:T(8,128)S(1)}, f32[128,384]{1,0:T(8,128)}, u32[]{:S(2)}) copy-start(f32[128,384]{1,0:T(8,128)} %first_ref.1) | copy-start | bytes 589828
  49.0 40.5 %copy-start.5 = (f32[128,384]{1,0:T(8,128)S(1)}, f32[128,384]{1,0:T(8,128)}, u32[]{:S(2)}) copy-start(f32[128,384]{1,0:T(8,128)} %second_ref.1) | copy-start | bytes 589828
  82.3 7.2 %collective-permute-start.4 = (f32[192,128]{1,0:T(8,128)S(1)}, f32[192,128]{1,0:T(8,128)S(1)}, u32[]{:S(2)}, u32[]{:S(2)}) collective-permute-start(f32[192,128]{1,0:T(8,128)S(1)} %bitcast.20), channel_id=1, source_target_pairs={{0,16},{1,17},{2,18},{3,19},{4,20},{5,21},{6,22},{7,23},{8,24},{9,... | collective-permute-start | bytes 294920 | tf_op jit(solution)/shard_map/ppermute | solution.py:63

commit v7 on v6

--- a/solution.py
+++ b/solution.py
@@ -148,7 +148,7 @@
 
 
 def gradient_kernel(
-    logits_ref, received_ref, slope_ref, rows_ref, others_ref, head_ref, grad_ref, dpre_ref, dlogits_ref
+    logits_ref, received_ref, slope_ref, rows_ref, others_ref, head_ref, grad_ref, dlogits_ref
 ):
     positions, piles, channels = rows_ref.shape
     count = positions * piles
@@ -167,7 +167,6 @@
         ]
         dpre = spread(dlogits, heads, positions) * slope_ref[side]
         if side == 0:
-            dpre_ref[...] = dpre.astype(jnp.bfloat16)
             dlogits_ref[...] = in_lanes(dlogits)
         lefts.append(dpre.T.astype(jnp.bfloat16))
     wide = channels // X
@@ -200,21 +199,22 @@
 
 
 def input_kernel(
-    blocks_ref, others_ref, rows_ref, dpre_ref, dlogits_ref, head_ref, input_ref, weight_ref, other_ref, held_ref, sems
+    blocks_ref, others_ref, rows_ref, dlogits_ref, head_ref, input_ref, weight_ref, other_ref, held_ref, sems
 ):
     positions, piles, channels = rows_ref.shape
     assemble(blocks_ref, weight_ref)
     assemble(others_ref, other_ref)
-    heads = head_half(head_ref, 1 - core_index())
-    slope = gelu_parts(product(rows_ref, other_ref))[1]
     dlogits = [dlogits_ref[:, kind : kind + 1] for kind in range(head_ref.shape[0])]
-    rest = (spread(dlogits, heads, positions) * slope).astype(jnp.bfloat16)
+    dpres = []
+    for half, half_ref in ((core_index(), weight_ref), (1 - core_index(), other_ref)):
+        slope = gelu_parts(product(rows_ref, half_ref))[1]
+        dpres.append((spread(dlogits, head_half(head_ref, half), positions) * slope).astype(jnp.bfloat16))
     wide = channels // X
     copies = []
     for x in range(X):
         span = pl.ds(x * wide, wide)
-        back = jnp.dot(dpre_ref[...], weight_ref[:, span], preferred_element_type=jnp.float32)
-        back = back + jnp.dot(rest, other_ref[:, span], preferred_element_type=jnp.float32)
+        back = jnp.dot(dpres[0], weight_ref[:, span], preferred_element_type=jnp.float32)
+        back = back + jnp.dot(dpres[1], other_ref[:, span], preferred_element_type=jnp.float32)
         held_ref[:, :, span] = back.astype(jnp.bfloat16).reshape(positions, piles, wide)
         copies.append(
             pltpu.make_async_copy(held_ref.at[:, :, span], input_ref.at[:, :, span], sems.at[x])
@@ -286,15 +286,14 @@
     )(blocks, rows, other_rows, labels.reshape(1, piles), flat_head)
 
     received = swap_cores(logits)
-    grad, dpre, dlogits = pl.pallas_call(
+    grad, dlogits = pl.pallas_call(
         gradient_kernel,
         out_shape=(
             jax.ShapeDtypeStruct((X, PAIR, PAIR, YL // PAIR, deep, shard), jnp.bfloat16),
-            jax.ShapeDtypeStruct((count, half_outs), jnp.bfloat16),
             jax.ShapeDtypeStruct((piles, 128), jnp.float32),
         ),
         in_specs=[vmem] * 6,
-        out_specs=(vmem,) * 3,
+        out_specs=(vmem,) * 2,
         compiler_params=params,
         cost_estimate=pl.CostEstimate(flops=flops, bytes_accessed=4 << 20, transcendentals=0),
         name="gradient",
@@ -306,7 +305,7 @@
     input_grad = pl.pallas_call(
         input_kernel,
         out_shape=jax.ShapeDtypeStruct((positions, piles, channels), jnp.bfloat16),
-        in_specs=[vmem] * 6,
+        in_specs=[vmem] * 5,
         out_specs=anywhere,
         scratch_shapes=[
             pltpu.VMEM((half_outs, channels), jnp.bfloat16),
@@ -319,7 +318,7 @@
             flops=flops, bytes_accessed=4 << 20, transcendentals=count * outputs
         ),
         name="input_grad",
-    )(blocks, other_blocks, rows, dpre, dlogits, flat_head)
+    )(blocks, other_blocks, rows, dlogits, flat_head)
     parts, input_grad = lax.optimization_barrier((parts, input_grad))
     copies = pl.pallas_call(
         sum_kernel,

time: 91.1 us -> 90.3 us (level)
    unnamed x20 -> x16, local copies, waits for them, and re-layouts: 2.52 us -> 1.86 us
  transfers between devices with their start and end apart: 7 -> 7, of which waited for: 6 -> 6; matrix products, arithmetic and copies ran while one was open for 0% -> 0% of each run, Pallas kernels for 4% -> 3%
where the time goes in v7:
time: 90.3 us; the launch traced here: 89.8 us
  starting transfers between devices  37.6 us (42%)
  blocking collectives  28.2 us (31%)
  waiting for transfers between devices  12.7 us (14%)
  Pallas kernels  7.43 us (8%)
  local copies, waits for them, and re-layouts  2.92 us (3%)
    all_to_all x2, blocking collectives, exchange(): lax.all_to_all(value, AXES, 0, 0, tiled=True, axis_index_groups=members)  28.2 us
    ppermute x4, starting transfers between devices, swap_cores(): return lax.ppermute(value, AXES, SWAP)  24.1 us
    all_to_all x2, starting transfers between devices, exchange(): lax.all_to_all(value, AXES, 0, 0, tiled=True, axis_index_groups=members)  7.63 us
    ppermute x4, waiting for transfers between devices, swap_cores(): return lax.ppermute(value, AXES, SWAP)  6.35 us
    ppermute x1, starting transfers between devices, per_device(): pair = jnp.stack([half, lax.ppermute(half, AXES, CROSS)])  5.93 us
    all_to_all x2, waiting for transfers between devices, exchange(): lax.all_to_all(value, AXES, 0, 0, tiled=True, axis_index_groups=members)  4.93 us
    pallas_call x1, Pallas kernels, per_device(): pl.pallas_call(input_kernel, out_shape=jax.ShapeDtypeStruct((positions, p...  3.13 us
    unnamed x16, local copies, waits for them, and re-layouts  1.86 us
  transfers between devices with their start and end apart: 7, of which 6 were waited for; matrix products, arithmetic and copies ran while one was open for 0% of the time, Pallas kernels for 3%

profile of v7, /device:TPU:1, one launch (start us, length us, event | category | flops | bytes accessed | tf_op | source)
XLA Modules:
  0.0 89.8 jit_solution(10110210530848977687)
XLA Ops:
  0.6 0.0 copy-start.2
  0.6 0.9 %copy-done.2 = f32[128,384]{1,0:T(8,128)S(1)} copy-done((f32[128,384]{1,0:T(8,128)S(1)}, f32[128,384]{1,0:T(8,128)}, u32[]{:S(2)}) %copy-start.2) | copy-done | bytes 196632
  1.6 0.1 prepare.1
  1.7 5.9 %collective-permute-start = (bf16[192,128]{1,0:T(8,128)(2,1)S(1)}, bf16[192,128]{1,0:T(8,128)(2,1)S(1)}, u32[]{:S(2)}, u32[]{:S(2)}) collective-permute-start(bf16[192,128]{1,0:T(8,128)(2,1)S(1)} %prepare.1), channel_id=1, source_target_pairs={{0,35},{1,2},{2,1},{3,32},{4,39},{5,6},{6,5},{7,36},{8,43},{9,10},... | collective-permute-start | bytes 147464 | tf_op jit(solution)/shard_map/ppermute | solution.py:265
  7.6 1.5 %collective-permute-done = bf16[192,128]{1,0:T(8,128)(2,1)S(1)} collective-permute-done((bf16[192,128]{1,0:T(8,128)(2,1)S(1)}, bf16[192,128]{1,0:T(8,128)(2,1)S(1)}, u32[]{:S(2)}, u32[]{:S(2)}) %collective-permute-start) | collective-permute-done | bytes 49184 | tf_op jit(solution)/shard_map/ppermute | solution.py:265
  9.1 0.0 copy-start
  9.1 0.0 copy-start.6
  9.1 0.0 copy-start.7
  9.1 1.0 %broadcast_in_dim.6 = bf16[8,2,192,128]{3,2,1,0:T(8,128)(2,1)} broadcast(bf16[2,192,128]{2,1,0:T(8,128)(2,1)S(1)} %pad_maximum_fusion), dimensions={1,2,3} | broadcast | bytes 884736 | tf_op jit(solution)/shard_map/broadcast_in_dim | solution.py:268
  10.2 4.0 %all-to-all-start = ((bf16[8,2,192,128]{3,2,1,0:T(8,128)(2,1)}), bf16[8,2,192,128]{3,2,1,0:T(8,128)(2,1)S(1)}, u32[]{:S(2)}, u32[]{:S(2)}) async-start(bf16[8,2,192,128]{3,2,1,0:T(8,128)(2,1)} %broadcast_in_dim.6), calls=%async_computation | async-start | bytes 1572864 | tf_op jit(solution)/shard_map/all_to_all | solution.py:67
  14.2 0.0 copy-done
  14.2 8.1 %collective-permute-start.1 = (bf16[5,64,2048]{2,1,0:T(8,128)(2,1)S(1)}, bf16[5,64,2048]{2,1,0:T(8,128)(2,1)S(1)}, u32[]{:S(2)}, u32[]{:S(2)}) collective-permute-start(bf16[5,64,2048]{2,1,0:T(8,128)(2,1)S(1)} %bitcast.12), channel_id=1, source_target_pairs={{0,16},{1,17},{2,18},{3,19},{4,20},{5,21},{6,22},{7,23},{8,24},{9,... | collective-permute-start | bytes 3932168 | tf_op jit(solution)/shard_map/ppermute | solution.py:63
  22.3 2.6 %collective-permute-done.1.others_ref = bf16[5,64,2048]{2,1,0:T(8,128)(2,1)S(1)} collective-permute-done((bf16[5,64,2048]{2,1,0:T(8,128)(2,1)S(1)}, bf16[5,64,2048]{2,1,0:T(8,128)(2,1)S(1)}, u32[]{:S(2)}, u32[]{:S(2)}) %collective-permute-start.1) | collective-permute-done | bytes 1310752 | tf_op jit(solution)/shard_map/ppermute | solution.py:63
  24.9 0.0 all-to-all-done
  24.9 0.0 copy-done.6
  24.9 0.0 copy-done.7
  25.0 1.5 %forward.1 = (f32[2,320,192]{2,1,0:T(8,128)S(1)}, f32[2,64,128]{2,1,0:T(8,128)S(1)}) custom-call(bf16[16,192,128]{2,1,0:T(8,128)(2,1)S(1)} %bitcast.16, bf16[5,64,2048]{2,1,0:T(8,128)(2,1)S(1)} %bitcast.13, bf16[5,64,2048]{2,1,0:T(8,128)(2,1)S(1)} %collective-permute-done.1.others_ref, s32[1,64]{1,0:T(1,128)S(1)} %bitcast.26, f32[3,384]{1,0:T(4,128)S(1)} %bitcast.23), custom_call_target="tpu_custom_call" | custom-call | flops 503316480 | bytes 4194304 | tf_op jit(solution)/shard_map/forward/pallas_call | solution.py:272
  26.5 7.4 %collective-permute-start.2 = (f32[2,64,128]{2,1,0:T(8,128)S(1)}, f32[2,64,128]{2,1,0:T(8,128)S(1)}, u32[]{:S(2)}, u32[]{:S(2)}) collective-permute-start(f32[2,64,128]{2,1,0:T(8,128)S(1)} %get-tuple-element.17.logits_ref), channel_id=1, source_target_pairs={{0,16},{1,17},{2,18},{3,19},{4,20},{5,21},{6,22},{7,23},{8,24},{9,... | collective-permute-start | bytes 196616 | tf_op jit(solution)/shard_map/ppermute | solution.py:63
  33.9 0.9 collective-permute-done.2.received_ref
  34.8 1.5 %gradient.1 = (bf16[4,2,2,2,96,128]{5,4,3,2,1,0:T(8,128)(2,1)S(1)}, f32[64,128]{1,0:T(8,128)S(1)}) custom-call(f32[2,64,128]{2,1,0:T(8,128)S(1)} %get-tuple-element.17.logits_ref, f32[2,64,128]{2,1,0:T(8,128)S(1)} %collective-permute-done.2.received_ref, f32[2,320,192]{2,1,0:T(8,128)S(1)} %get-tuple-element.18.slope_ref, bf16[5,64,2048]{2,1,0:T(8,128)(2,1)S(1)} %bitcast.14, ...), custom_call_target="tpu_custom_call" | custom-call | flops 503316480 | bytes 4194304 | tf_op jit(solution)/shard_map/gradient/pallas_call | solution.py:289
  36.3 0.0 copy-start.1
  36.3 0.9 %copy-done.1 = bf16[4,2,2,2,96,128]{5,4,3,2,1,0:T(8,128)(2,1)} copy-done((bf16[4,2,2,2,96,128]{5,4,3,2,1,0:T(8,128)(2,1)}, bf16[4,2,2,2,96,128]{5,4,3,2,1,0:T(8,128)(2,1)S(1)}, u32[]{:S(2)}) %copy-start.1) | copy-done | bytes 786456
  37.2 3.6 %all-to-all-start.1 = ((bf16[16,2,96,128]{3,2,1,0:T(8,128)(2,1)}), bf16[16,2,96,128]{3,2,1,0:T(8,128)(2,1)S(1)}, u32[]{:S(2)}, u32[]{:S(2)}) async-start(bf16[16,2,96,128]{3,2,1,0:T(8,128)(2,1)} %bitcast.19), calls=%async_computation.1 | async-start | bytes 1572864 | tf_op jit(solution)/shard_map/all_to_all | solution.py:67
  40.8 2.3 %collective-permute-start.3 = (bf16[16,192,128]{2,1,0:T(8,128)(2,1)S(1)}, bf16[16,192,128]{2,1,0:T(8,128)(2,1)S(1)}, u32[]{:S(2)}, u32[]{:S(2)}) collective-permute-start(bf16[16,192,128]{2,1,0:T(8,128)(2,1)S(1)} %bitcast.17), channel_id=1, source_target_pairs={{0,16},{1,17},{2,18},{3,19},{4,20},{5,21},{6,22},{7,23},{8,24},{9,... | collective-permute-start | bytes 2359304 | tf_op jit(solution)/shard_map/ppermute | solution.py:63
  43.1 1.9 %collective-permute-done.3.others_ref = bf16[16,192,128]{2,1,0:T(8,128)(2,1)S(1)} collective-permute-done((bf16[16,192,128]{2,1,0:T(8,128)(2,1)S(1)}, bf16[16,192,128]{2,1,0:T(8,128)(2,1)S(1)}, u32[]{:S(2)}, u32[]{:S(2)}) %collective-permute-start.3) | collective-permute-done | bytes 786464 | tf_op jit(solution)/shard_map/ppermute | solution.py:63
  45.0 3.1 %input_grad.1 = bf16[5,64,2048]{2,1,0:T(8,128)(2,1)} custom-call(bf16[16,192,128]{2,1,0:T(8,128)(2,1)S(1)} %bitcast.18, bf16[16,192,128]{2,1,0:T(8,128)(2,1)S(1)} %collective-permute-done.3.others_ref, bf16[5,64,2048]{2,1,0:T(8,128)(2,1)S(1)} %bitcast.15, f32[64,128]{1,0:T(8,128)S(1)} %get-tuple-element.20.dlogits_ref, f32[3,384]{1,0:T(4,128)S(1)} %bitcast.25), custom_call_target="tpu_custom_call" | custom-call | flops 503316480 | bytes 4194304 | tf_op jit(solution)/shard_map/input_grad/pallas_call | solution.py:305
  48.1 0.0 copy-start.3
  48.1 0.0 copy-start.4
  48.2 0.0 copy-start.5
  48.2 4.9 %all-to-all-done.1.parts_ref = bf16[16,2,96,128]{3,2,1,0:T(8,128)(2,1)S(1)} async-done(((bf16[16,2,96,128]{3,2,1,0:T(8,128)(2,1)}), bf16[16,2,96,128]{3,2,1,0:T(8,128)(2,1)S(1)}, u32[]{:S(2)}, u32[]{:S(2)}) %all-to-all-start.1) | async-done | bytes 786464 | tf_op jit(solution)/shard_map/all_to_all | solution.py:67
  53.1 0.1 sum.1
  53.2 12.0 %all_to_all.20 = bf16[4,96,128]{2,1,0:T(8,128)(2,1)S(1)} all-to-all(bf16[4,96,128]{2,1,0:T(8,128)(2,1)S(1)} %sum.1), channel_id=1, replica_groups={{0,2,32,34},{1,3,33,35},{4,6,36,38},{5,7,37,39},{8,10,40,42},{9,11,41,4..., dimensions={0} | all-to-all | bytes 196608 | tf_op jit(solution)/shard_map/all_to_all | solution.py:67
  65.2 16.3 %all_to_all.21 = bf16[8,96,128]{2,1,0:T(8,128)(2,1)S(1)} all-to-all(bf16[8,96,128]{2,1,0:T(8,128)(2,1)S(1)} %broadcast_in_dim.7), channel_id=1, replica_groups={{0,128,256,384,64,192,320,448},{1,129,257,385,65,193,321,449},{2,130,25..., dimensions={0} | all-to-all | bytes 393216 | tf_op jit(solution)/shard_map/all_to_all | solution.py:67
  81.5 6.3 %collective-permute-start.4 = (f32[192,128]{1,0:T(8,128)S(1)}, f32[192,128]{1,0:T(8,128)S(1)}, u32[]{:S(2)}, u32[]{:S(2)}) collective-permute-start(f32[192,128]{1,0:T(8,128)S(1)} %bitcast.20), channel_id=1, source_target_pairs={{0,16},{1,17},{2,18},{3,19},{4,20},{5,21},{6,22},{7,23},{8,24},{9,... | collective-permute-start | bytes 294920 | tf_op jit(solution)/shard_map/ppermute | solution.py:63
  87.8 0.9 %collective-permute-done.4.other_ref = f32[192,128]{1,0:T(8,128)S(1)} collective-permute-done((f32[192,128]{1,0:T(8,128)S(1)}, f32[192,128]{1,0:T(8,128)S(1)}, u32[]{:S(2)}, u32[]{:S(2)}) %collective-permute-start.4) | collective-permute-done | bytes 98336 | tf_op jit(solution)/shard_map/ppermute | solution.py:63
  88.8 0.0 copy-done.3
  88.8 0.0 copy-done.4
  88.8 0.0 copy-done.5
  88.8 1.0 %adam.1 = (f32[128,384]{1,0:T(8,128)}, f32[128,384]{1,0:T(8,128)}, f32[128,384]{1,0:T(8,128)}) custom-call(f32[192,128]{1,0:T(8,128)S(1)} %bitcast.21, f32[192,128]{1,0:T(8,128)S(1)} %collective-permute-done.4.other_ref, f32[128,384]{1,0:T(8,128)S(1)} %copy-done.3, f32[128,384]{1,0:T(8,128)S(1)} %copy-done.4, f32[128,384]{1,0:T(8,128)S(1)} %copy-done.5), custom_call_target="tpu_custom_call" | custom-call | tf_op jit(solution)/shard_map/adam/pallas_call | solution.py:337
  (4 shorter events, 0.1 us)
Async XLA Ops:
  0.6 0.9 %copy-start.2 = (f32[128,384]{1,0:T(8,128)S(1)}, f32[128,384]{1,0:T(8,128)}, u32[]{:S(2)}) copy-start(f32[128,384]{1,0:T(8,128)} %weight_ref.3) | copy-start | bytes 589828
  1.7 7.4 %collective-permute-start = (bf16[192,128]{1,0:T(8,128)(2,1)S(1)}, bf16[192,128]{1,0:T(8,128)(2,1)S(1)}, u32[]{:S(2)}, u32[]{:S(2)}) collective-permute-start(bf16[192,128]{1,0:T(8,128)(2,1)S(1)} %prepare.1), channel_id=1, source_target_pairs={{0,35},{1,2},{2,1},{3,32},{4,39},{5,6},{6,5},{7,36},{8,43},{9,10},... | collective-permute-start | bytes 147464 | tf_op jit(solution)/shard_map/ppermute | solution.py:265
  9.1 5.1 %copy-start = (bf16[64,5,2048]{2,0,1:T(8,128)(2,1)S(1)}, bf16[64,5,2048]{2,0,1:T(8,128)(2,1)}, u32[]{:S(2)}) copy-start(bf16[64,5,2048]{2,0,1:T(8,128)(2,1)} %param.6) | copy-start | bytes 3932164
  9.1 15.8 %copy-start.6 = (f32[384,3]{0,1:T(4,128)S(1)}, f32[384,3]{0,1:T(4,128)}, u32[]{:S(2)}) copy-start(f32[384,3]{0,1:T(4,128)} %param.9) | copy-start | bytes 13828
  9.1 15.8 %copy-start.7 = (s32[64]{0:T(128)S(1)}, s32[64]{0:T(128)}, u32[]{:S(2)}) copy-start(s32[64]{0:T(128)} %param.7) | copy-start | bytes 772
  10.2 14.8 %all-to-all-start = ((bf16[8,2,192,128]{3,2,1,0:T(8,128)(2,1)}), bf16[8,2,192,128]{3,2,1,0:T(8,128)(2,1)S(1)}, u32[]{:S(2)}, u32[]{:S(2)}) async-start(bf16[8,2,192,128]{3,2,1,0:T(8,128)(2,1)} %broadcast_in_dim.6), calls=%async_computation | async-start | bytes 1572864 | tf_op jit(solution)/shard_map/all_to_all | solution.py:67
  14.2 10.8 %collective-permute-start.1 = (bf16[5,64,2048]{2,1,0:T(8,128)(2,1)S(1)}, bf16[5,64,2048]{2,1,0:T(8,128)(2,1)S(1)}, u32[]{:S(2)}, u32[]{:S(2)}) collective-permute-start(bf16[5,64,2048]{2,1,0:T(8,128)(2,1)S(1)} %bitcast.12), channel_id=1, source_target_pairs={{0,16},{1,17},{2,18},{3,19},{4,20},{5,21},{6,22},{7,23},{8,24},{9,... | collective-permute-start | bytes 3932168 | tf_op jit(solution)/shard_map/ppermute | solution.py:63
  26.5 8.3 %collective-permute-start.2 = (f32[2,64,128]{2,1,0:T(8,128)S(1)}, f32[2,64,128]{2,1,0:T(8,128)S(1)}, u32[]{:S(2)}, u32[]{:S(2)}) collective-permute-start(f32[2,64,128]{2,1,0:T(8,128)S(1)} %get-tuple-element.17.logits_ref), channel_id=1, source_target_pairs={{0,16},{1,17},{2,18},{3,19},{4,20},{5,21},{6,22},{7,23},{8,24},{9,... | collective-permute-start | bytes 196616 | tf_op jit(solution)/shard_map/ppermute | solution.py:63
  36.3 0.9 %copy-start.1 = (bf16[4,2,2,2,96,128]{5,4,3,2,1,0:T(8,128)(2,1)}, bf16[4,2,2,2,96,128]{5,4,3,2,1,0:T(8,128)(2,1)S(1)}, u32[]{:S(2)}) copy-start(bf16[4,2,2,2,96,128]{5,4,3,2,1,0:T(8,128)(2,1)S(1)} %get-tuple-element.19) | copy-start | bytes 2359300
  37.2 15.9 %all-to-all-start.1 = ((bf16[16,2,96,128]{3,2,1,0:T(8,128)(2,1)}), bf16[16,2,96,128]{3,2,1,0:T(8,128)(2,1)S(1)}, u32[]{:S(2)}, u32[]{:S(2)}) async-start(bf16[16,2,96,128]{3,2,1,0:T(8,128)(2,1)} %bitcast.19), calls=%async_computation.1 | async-start | bytes 1572864 | tf_op jit(solution)/shard_map/all_to_all | solution.py:67
  40.8 4.2 %collective-permute-start.3 = (bf16[16,192,128]{2,1,0:T(8,128)(2,1)S(1)}, bf16[16,192,128]{2,1,0:T(8,128)(2,1)S(1)}, u32[]{:S(2)}, u32[]{:S(2)}) collective-permute-start(bf16[16,192,128]{2,1,0:T(8,128)(2,1)S(1)} %bitcast.17), channel_id=1, source_target_pairs={{0,16},{1,17},{2,18},{3,19},{4,20},{5,21},{6,22},{7,23},{8,24},{9,... | collective-permute-start | bytes 2359304 | tf_op jit(solution)/shard_map/ppermute | solution.py:63
  48.1 40.6 %copy-start.3 = (f32[128,384]{1,0:T(8,128)S(1)}, f32[128,384]{1,0:T(8,128)}, u32[]{:S(2)}) copy-start(f32[128,384]{1,0:T(8,128)} %weight_ref.3) | copy-start | bytes 589828
  48.1 40.6 %copy-start.4 = (f32[128,384]{1,0:T(8,128)S(1)}, f32[128,384]{1,0:T(8,128)}, u32[]{:S(2)}) copy-start(f32[128,384]{1,0:T(8,128)} %first_ref.1) | copy-start | bytes 589828
  48.2 40.6 %copy-start.5 = (f32[128,384]{1,0:T(8,128)S(1)}, f32[128,384]{1,0:T(8,128)}, u32[]{:S(2)}) copy-start(f32[128,384]{1,0:T(8,128)} %second_ref.1) | copy-start | bytes 589828
  81.5 7.2 %collective-permute-start.4 = (f32[192,128]{1,0:T(8,128)S(1)}, f32[192,128]{1,0:T(8,128)S(1)}, u32[]{:S(2)}, u32[]{:S(2)}) collective-permute-start(f32[192,128]{1,0:T(8,128)S(1)} %bitcast.20), channel_id=1, source_target_pairs={{0,16},{1,17},{2,18},{3,19},{4,20},{5,21},{6,22},{7,23},{8,24},{9,... | collective-permute-start | bytes 294920 | tf_op jit(solution)/shard_map/ppermute | solution.py:63

commit v8 on v7

--- a/solution.py
+++ b/solution.py
@@ -42,7 +42,18 @@
     return [[at for _, at in sorted(held[name])] for name in sorted(held)]
 
 
-OVER_XY = groups(lambda z, yh, c, x, yl: (z, yh, c, yl // PAIR), lambda z, yh, c, x, yl: (x, yl))
+def pair_of(y, c):
+    return (y - c) % (YH * YL) // PAIR
+
+
+def beyond(yh, yl, c):
+    at = (yh * YL + yl + (1 if (yl + c) % PAIR else -1)) % (YH * YL)
+    return at // YL, at % YL
+
+
+OVER_XY = groups(
+    lambda z, yh, c, x, yl: (z, c, pair_of(yh * YL + yl, c)), lambda z, yh, c, x, yl: (x, yl % PAIR)
+)
 OVER_XYZ = groups(
     lambda z, yh, c, x, yl: (z // PAIR, yh, c, yl // PAIR), lambda z, yh, c, x, yl: (x, yl % PAIR, z % PAIR)
 )
@@ -51,12 +62,10 @@
 SWAP = [(index(z, yh, c, x, yl), index(z, yh, 1 - c, x, yl)) for z, yh, c, x, yl in places()]
 
 
-def beside(yh, yl):
-    at = (yh * YL + yl + (1 if yl % PAIR else -1)) % (YH * YL)
-    return at // YL, at % YL
-
-
-CROSS = [(index(z, yh, c, x, yl), index(z, *beside(yh, yl)[:1], c, x, beside(yh, yl)[1])) for z, yh, c, x, yl in places()]
+CROSS = [
+    (index(z, yh, c, x, yl), index(z, beyond(yh, yl, c)[0], c, x, beyond(yh, yl, c)[1]))
+    for z, yh, c, x, yl in places()
+]
 
 
 def swap_cores(value):
@@ -115,20 +124,53 @@
     out_ref[...] = flip_ref[pl.ds(pl.multiple_of(core_index() * half, half), half), :].astype(jnp.bfloat16)
 
 
-def assemble(blocks_ref, weight_ref):
+def shards_of(core, far):
+    yl = lax.rem(lax.axis_index("group"), YL)
+    odd = lax.rem(yl, PAIR)
+    step = 1 - 2 * core
+    even_at = lax.rem(yl - odd * step + YL, YL)
+    odd_at = lax.rem(yl + (1 - odd) * step + YL, YL)
+    return [x * YL + lax.rem(at + PAIR * far, YL) for x in range(X) for at in (even_at, odd_at)]
+
+
+def assemble(core, near_ref, far_ref, weight_ref):
+    width = near_ref.shape[2]
+    for far, blocks_ref in enumerate((near_ref, far_ref)):
+        for block, shard in enumerate(shards_of(core, far)):
+            weight_ref[:, pl.ds(pl.multiple_of(shard * width, width), width)] = blocks_ref[block]
+
+
+def channels_of(side, span):
+    return jnp.concatenate(
+        [ref[at, :, span] for ref in side for at in range(ref.shape[0])], axis=0
+    )
+
+
+def partial_product(core, far, blocks_ref, side):
     width = blocks_ref.shape[2]
-    near = lax.rem(lax.axis_index("group"), YL) // PAIR
-    for block in range(GROUP):
-        yl = near * PAIR + block // 2 % PAIR
-        shard = block // YL * YL + (yl if block % 2 == 0 else YL - 1 - yl)
-        weight_ref[:, pl.ds(pl.multiple_of(shard * width, width), width)] = blocks_ref[block]
+    shards = shards_of(core, far)
+    total = None
+    for block in range(0, len(shards), 2):
+        spans = [pl.ds(pl.multiple_of(shard * width, width), width) for shard in shards[block : block + 2]]
+        part = lax.dot_general(
+            jnp.concatenate([channels_of(side, span) for span in spans], axis=1),
+            jnp.concatenate([blocks_ref[block], blocks_ref[block + 1]], axis=1),
+            (((1,), (1,)), ((), ())),
+            preferred_element_type=jnp.float32,
+        )
+        total = part if total is None else total + part
+    return total
+
+
+def near_kernel(blocks_ref, rows_ref, first_ref, last_ref, pre_ref):
+    for at, side in enumerate(((rows_ref,), (first_ref, last_ref))):
+        pre_ref[at] = partial_product(core_index(), 0, blocks_ref, side)
 
 
 def forward_kernel(
-    blocks_ref, rows_ref, others_ref, labels_ref, head_ref, slope_ref, logits_ref, weight_ref
+    pre_ref, blocks_ref, rows_ref, first_ref, last_ref, labels_ref, head_ref, slope_ref, logits_ref
 ):
     positions, piles, channels = rows_ref.shape
-    assemble(blocks_ref, weight_ref)
     heads = head_half(head_ref, core_index())
     across = lax.broadcasted_iota(jnp.int32, (piles, piles), 0) == lax.broadcasted_iota(
         jnp.int32, (piles, piles), 1
@@ -136,8 +178,9 @@
     marks = jnp.sum(
         jnp.where(across, labels_ref[...].astype(jnp.float32), 0.0), axis=1, keepdims=True
     )
-    for side, side_ref in enumerate((rows_ref, others_ref)):
-        act, slope = gelu_parts(product(side_ref, weight_ref))
+    for side, refs in enumerate(((rows_ref,), (first_ref, last_ref))):
+        pre = pre_ref[side] + partial_product(core_index(), 1, blocks_ref, refs)
+        act, slope = gelu_parts(pre)
         slope_ref[side] = slope
         pooled = functools.reduce(
             jnp.add, [act[position * piles : (position + 1) * piles] for position in range(positions)]
@@ -148,10 +191,9 @@
 
 
 def gradient_kernel(
-    logits_ref, received_ref, slope_ref, rows_ref, others_ref, head_ref, grad_ref, dlogits_ref
+    logits_ref, received_ref, slope_ref, rows_ref, first_ref, last_ref, head_ref, grad_ref, dlogits_ref
 ):
     positions, piles, channels = rows_ref.shape
-    count = positions * piles
     classes = head_ref.shape[0]
     heads = head_half(head_ref, core_index())
     lefts = []
@@ -176,10 +218,10 @@
         parts = [
             jnp.dot(
                 left,
-                side_ref[:, :, x * wide : (x + 1) * wide].reshape(count, wide),
+                channels_of(refs, slice(x * wide, (x + 1) * wide)),
                 preferred_element_type=jnp.float32,
             )
-            for left, side_ref in zip(lefts, (rows_ref, others_ref))
+            for left, refs in zip(lefts, ((rows_ref,), (first_ref, last_ref)))
         ]
         total = (parts[0] + parts[1]).astype(jnp.bfloat16)
         for part in range(PAIR):
@@ -199,11 +241,12 @@
 
 
 def input_kernel(
-    blocks_ref, others_ref, rows_ref, dlogits_ref, head_ref, input_ref, weight_ref, other_ref, held_ref, sems
+    near_ref, far_ref, near_other_ref, far_other_ref, rows_ref, dlogits_ref, head_ref, input_ref,
+    weight_ref, other_ref, held_ref, sems
 ):
     positions, piles, channels = rows_ref.shape
-    assemble(blocks_ref, weight_ref)
-    assemble(others_ref, other_ref)
+    assemble(core_index(), near_ref, far_ref, weight_ref)
+    assemble(1 - core_index(), near_other_ref, far_other_ref, other_ref)
     dlogits = [dlogits_ref[:, kind : kind + 1] for kind in range(head_ref.shape[0])]
     dpres = []
     for half, half_ref in ((core_index(), weight_ref), (1 - core_index(), other_ref)):
@@ -262,28 +305,35 @@
         compiler_params=params,
         name="prepare",
     )(weight)
-    pair = jnp.stack([half, lax.ppermute(half, AXES, CROSS)])
-    sent_rows, pair = lax.optimization_barrier((rows, pair))
-    other_rows = swap_cores(sent_rows)
-    copies = jnp.broadcast_to(pair, (X * PAIR, PAIR, half_outs, shard))
-    blocks = exchange(copies, OVER_XY).reshape(GROUP, half_outs, shard)
+    sent_rows, half = lax.optimization_barrier((rows, half))
+    other_rows = (swap_cores(sent_rows[:2]), swap_cores(sent_rows[2:]))
+    near = exchange(jnp.broadcast_to(half, (X * PAIR, half_outs, shard)), OVER_XY)
+    far = lax.ppermute(near, AXES, CROSS)
 
     flops = 2 * count * channels * outputs
+    pre = pl.pallas_call(
+        near_kernel,
+        out_shape=jax.ShapeDtypeStruct((CORE, count, half_outs), jnp.float32),
+        in_specs=[vmem] * 4,
+        out_specs=vmem,
+        compiler_params=params,
+        cost_estimate=pl.CostEstimate(flops=flops // 2, bytes_accessed=4 << 20, transcendentals=0),
+        name="forward_near",
+    )(near, rows, *other_rows)
     slope, logits = pl.pallas_call(
         forward_kernel,
         out_shape=(
             jax.ShapeDtypeStruct((CORE, count, half_outs), jnp.float32),
             jax.ShapeDtypeStruct((CORE, piles, 128), jnp.float32),
         ),
-        in_specs=[vmem] * 5,
+        in_specs=[vmem] * 7,
         out_specs=(vmem,) * 2,
-        scratch_shapes=[pltpu.VMEM((half_outs, channels), jnp.bfloat16)],
         compiler_params=params,
         cost_estimate=pl.CostEstimate(
-            flops=flops, bytes_accessed=4 << 20, transcendentals=count * outputs
-        ),
-        name="forward",
-    )(blocks, rows, other_rows, labels.reshape(1, piles), flat_head)
+            flops=flops // 2, bytes_accessed=4 << 20, transcendentals=count * outputs
+        ),
+        name="forward_far",
+    )(pre, far, rows, *other_rows, labels.reshape(1, piles), flat_head)
 
     received = swap_cores(logits)
     grad, dlogits = pl.pallas_call(
@@ -292,20 +342,20 @@
             jax.ShapeDtypeStruct((X, PAIR, PAIR, YL // PAIR, deep, shard), jnp.bfloat16),
             jax.ShapeDtypeStruct((piles, 128), jnp.float32),
         ),
-        in_specs=[vmem] * 6,
+        in_specs=[vmem] * 7,
         out_specs=(vmem,) * 2,
         compiler_params=params,
         cost_estimate=pl.CostEstimate(flops=flops, bytes_accessed=4 << 20, transcendentals=0),
         name="gradient",
-    )(logits, received, slope, rows, other_rows, flat_head)
+    )(logits, received, slope, rows, *other_rows, flat_head)
 
     both = grad.reshape(GROUP, -1, deep, shard)
     parts = exchange(both, OVER_XYZ)
-    other_blocks = swap_cores(blocks)
+    near_other, far_other = swap_cores(near), swap_cores(far)
     input_grad = pl.pallas_call(
         input_kernel,
         out_shape=jax.ShapeDtypeStruct((positions, piles, channels), jnp.bfloat16),
-        in_specs=[vmem] * 5,
+        in_specs=[vmem] * 7,
         out_specs=anywhere,
         scratch_shapes=[
             pltpu.VMEM((half_outs, channels), jnp.bfloat16),
@@ -318,7 +368,7 @@
             flops=flops, bytes_accessed=4 << 20, transcendentals=count * outputs
         ),
         name="input_grad",
-    )(blocks, other_blocks, rows, dlogits, flat_head)
+    )(near, far, near_other, far_other, rows, dlogits, flat_head)
     parts, input_grad = lax.optimization_barrier((parts, input_grad))
     copies = pl.pallas_call(
         sum_kernel,

time: 90.3 us -> 89.8 us (level)
  local copies, waits for them, and re-layouts: 2.92 us -> 4.55 us
  blocking collectives: 28.2 us -> 27.2 us
  waiting for transfers between devices: 12.7 us -> 11.7 us
    all_to_all x2, starting transfers between devices: 7.63 us -> 11.4 us  [exchange(): lax.all_to_all(value, AXES, 0, 0, tiled=True, axis_index_groups=members)]
    ppermute x1, waiting for transfers between devices: 1.46 us -> 4.88 us  [per_device(): far = lax.ppermute(near, AXES, CROSS)]
    ppermute x4 -> x6, waiting for transfers between devices: 6.35 us -> 3.35 us  [swap_cores(): return lax.ppermute(value, AXES, SWAP)]
    ppermute x1, starting transfers between devices: 5.93 us -> 3.54 us  [per_device(): far = lax.ppermute(near, AXES, CROSS)]
    slice x0 -> x2, local copies, waits for them, and re-layouts: none -> 1.76 us  [per_device(): other_rows = (swap_cores(sent_rows[:2]), swap_cores(sent_rows[2:]))]
    all_to_all x2, waiting for transfers between devices: 4.93 us -> 3.45 us  [exchange(): lax.all_to_all(value, AXES, 0, 0, tiled=True, axis_index_groups=members)]
    ppermute x4 -> x6, starting transfers between devices: 24.1 us -> 22.8 us  [swap_cores(): return lax.ppermute(value, AXES, SWAP)]
    all_to_all x2, blocking collectives: 28.2 us -> 27.2 us  [exchange(): lax.all_to_all(value, AXES, 0, 0, tiled=True, axis_index_groups=members)]
  transfers between devices with their start and end apart: 7 -> 9, of which waited for: 6 -> 5; matrix products, arithmetic and copies ran while one was open for 0% -> 2% of each run, Pallas kernels for 3% -> 4%
where the time goes in v8:
time: 89.8 us; the launch traced here: 89.2 us
  starting transfers between devices  37.7 us (42%)
  blocking collectives  27.2 us (30%)
  waiting for transfers between devices  11.7 us (13%)
  Pallas kernels  7.23 us (8%)
  local copies, waits for them, and re-layouts  4.55 us (5%)
    all_to_all x2, blocking collectives, exchange(): lax.all_to_all(value, AXES, 0, 0, tiled=True, axis_index_groups=members)  27.2 us
    ppermute x6, starting transfers between devices, swap_cores(): return lax.ppermute(value, AXES, SWAP)  22.8 us
    all_to_all x2, starting transfers between devices, exchange(): lax.all_to_all(value, AXES, 0, 0, tiled=True, axis_index_groups=members)  11.4 us
    ppermute x1, waiting for transfers between devices, per_device(): far = lax.ppermute(near, AXES, CROSS)  4.88 us
    ppermute x1, starting transfers between devices, per_device(): far = lax.ppermute(near, AXES, CROSS)  3.54 us
    all_to_all x2, waiting for transfers between devices, exchange(): lax.all_to_all(value, AXES, 0, 0, tiled=True, axis_index_groups=members)  3.45 us
    ppermute x6, waiting for transfers between devices, swap_cores(): return lax.ppermute(value, AXES, SWAP)  3.35 us
    pallas_call x1, Pallas kernels, per_device(): pl.pallas_call(input_kernel, out_shape=jax.ShapeDtypeStruct((positions, p...  2.9 us
  transfers between devices with their start and end apart: 9, of which 5 were waited for; matrix products, arithmetic and copies ran while one was open for 2% of the time, Pallas kernels for 4%

profile of v8, /device:TPU:1, one launch (start us, length us, event | category | flops | bytes accessed | tf_op | source)
XLA Modules:
  0.0 89.2 jit_solution(12627476859013475925)
XLA Ops:
  0.6 0.0 copy-start
  0.6 0.0 copy-start.2
  0.7 1.0 %copy-done.2 = f32[128,384]{1,0:T(8,128)S(1)} copy-done((f32[128,384]{1,0:T(8,128)S(1)}, f32[128,384]{1,0:T(8,128)}, u32[]{:S(2)}) %copy-start.2) | copy-done | bytes 196632
  1.7 0.1 prepare.1
  1.8 0.8 broadcast_in_dim.6
  2.6 7.8 %all-to-all-start = ((bf16[8,192,128]{2,1,0:T(8,128)(2,1)}), bf16[8,192,128]{2,1,0:T(8,128)(2,1)S(1)}, u32[]{:S(2)}, u32[]{:S(2)}) async-start(bf16[8,192,128]{2,1,0:T(8,128)(2,1)} %broadcast_in_dim.6), calls=%async_computation | async-start | bytes 786432 | tf_op jit(solution)/shard_map/all_to_all | solution.py:76
  10.4 0.0 copy-done
  10.4 0.9 %slice.7 = bf16[3,64,2048]{2,1,0:T(8,128)(2,1)} slice(bf16[5,64,2048]{2,1,0:T(8,128)(2,1)S(1)} %bitcast.9), slice={[2:5], [0:64], [0:2048]} | slice | bytes 1572864 | tf_op jit(solution)/shard_map/slice | solution.py:309
  11.3 4.5 %collective-permute-start.1 = (bf16[3,64,2048]{2,1,0:T(8,128)(2,1)}, bf16[3,64,2048]{2,1,0:T(8,128)(2,1)S(1)}, u32[]{:S(2)}, u32[]{:S(2)}) collective-permute-start(bf16[3,64,2048]{2,1,0:T(8,128)(2,1)} %slice.7), channel_id=1, source_target_pairs={{0,16},{1,17},{2,18},{3,19},{4,20},{5,21},{6,22},{7,23},{8,24},{9,... | collective-permute-start | bytes 2359304 | tf_op jit(solution)/shard_map/ppermute | solution.py:72
  15.8 0.8 slice.6
  16.6 0.0 copy-start.6
  16.6 0.0 copy-start.7
  16.6 2.0 %collective-permute-start = (bf16[2,64,2048]{2,1,0:T(8,128)(2,1)}, bf16[2,64,2048]{2,1,0:T(8,128)(2,1)S(1)}, u32[]{:S(2)}, u32[]{:S(2)}) collective-permute-start(bf16[2,64,2048]{2,1,0:T(8,128)(2,1)} %slice.6), channel_id=1, source_target_pairs={{0,16},{1,17},{2,18},{3,19},{4,20},{5,21},{6,22},{7,23},{8,24},{9,... | collective-permute-start | bytes 1572872 | tf_op jit(solution)/shard_map/ppermute | solution.py:72
  18.7 0.0 all-to-all-done.blocks_ref.near_ref
  18.7 3.5 %collective-permute-start.2 = (bf16[8,192,128]{2,1,0:T(8,128)(2,1)S(1)}, bf16[8,192,128]{2,1,0:T(8,128)(2,1)S(1)}, u32[]{:S(2)}, u32[]{:S(2)}) collective-permute-start(bf16[8,192,128]{2,1,0:T(8,128)(2,1)S(1)} %all-to-all-done.blocks_ref.near_ref), channel_id=1, source_target_pairs={{0,35},{1,2},{2,1},{3,32},{4,39},{5,6},{6,5},{7,36},{8,43},{9,10},... | collective-permute-start | bytes 1179656 | tf_op jit(solution)/shard_map/ppermute | solution.py:311
  22.2 0.0 collective-permute-done.first_ref
  22.2 0.0 collective-permute-done.1.last_ref
  22.3 0.5 forward_near.1.pre_ref
  22.8 4.9 %collective-permute-done.2.blocks_ref.far_ref = bf16[8,192,128]{2,1,0:T(8,128)(2,1)S(1)} collective-permute-done((bf16[8,192,128]{2,1,0:T(8,128)(2,1)S(1)}, bf16[8,192,128]{2,1,0:T(8,128)(2,1)S(1)}, u32[]{:S(2)}, u32[]{:S(2)}) %collective-permute-start.2) | collective-permute-done | bytes 393248 | tf_op jit(solution)/shard_map/ppermute | solution.py:311
  27.7 0.0 copy-done.6
  27.7 0.0 copy-done.7
  27.7 1.0 %forward_far.1 = (f32[2,320,192]{2,1,0:T(8,128)S(1)}, f32[2,64,128]{2,1,0:T(8,128)S(1)}) custom-call(f32[2,320,192]{2,1,0:T(8,128)S(1)} %forward_near.1.pre_ref, bf16[8,192,128]{2,1,0:T(8,128)(2,1)S(1)} %collective-permute-done.2.blocks_ref.far_ref, bf16[5,64,2048]{2,1,0:T(8,128)(2,1)S(1)} %bitcast.12, ...), custom_call_target="tpu_custom_call" | custom-call | flops 251658240 | bytes 4194304 | tf_op jit(solution)/shard_map/forward_far/pallas_call | solution.py:323
  28.7 6.1 %collective-permute-start.3 = (f32[2,64,128]{2,1,0:T(8,128)S(1)}, f32[2,64,128]{2,1,0:T(8,128)S(1)}, u32[]{:S(2)}, u32[]{:S(2)}) collective-permute-start(f32[2,64,128]{2,1,0:T(8,128)S(1)} %get-tuple-element.17.logits_ref), channel_id=1, source_target_pairs={{0,16},{1,17},{2,18},{3,19},{4,20},{5,21},{6,22},{7,23},{8,24},{9,... | collective-permute-start | bytes 196616 | tf_op jit(solution)/shard_map/ppermute | solution.py:72
  34.8 0.9 collective-permute-done.3.received_ref
  35.7 1.5 %gradient.1 = (bf16[4,2,2,2,96,128]{5,4,3,2,1,0:T(8,128)(2,1)S(1)}, f32[64,128]{1,0:T(8,128)S(1)}) custom-call(f32[2,64,128]{2,1,0:T(8,128)S(1)} %get-tuple-element.17.logits_ref, f32[2,64,128]{2,1,0:T(8,128)S(1)} %collective-permute-done.3.received_ref, f32[2,320,192]{2,1,0:T(8,128)S(1)} %get-tuple-element.18.slope_ref, bf16[5,64,2048]{2,1,0:T(8,128)(2,1)S(1)} %bitcast.13, ...), custom_call_target="tpu_custom_call" | custom-call | flops 503316480 | bytes 4194304 | tf_op jit(solution)/shard_map/gradient/pallas_call | solution.py:339
  37.2 0.0 copy-start.1
  37.2 0.9 %copy-done.1 = bf16[4,2,2,2,96,128]{5,4,3,2,1,0:T(8,128)(2,1)} copy-done((bf16[4,2,2,2,96,128]{5,4,3,2,1,0:T(8,128)(2,1)}, bf16[4,2,2,2,96,128]{5,4,3,2,1,0:T(8,128)(2,1)S(1)}, u32[]{:S(2)}) %copy-start.1) | copy-done | bytes 786456
  38.1 3.6 %all-to-all-start.1 = ((bf16[16,2,96,128]{3,2,1,0:T(8,128)(2,1)}), bf16[16,2,96,128]{3,2,1,0:T(8,128)(2,1)S(1)}, u32[]{:S(2)}, u32[]{:S(2)}) async-start(bf16[16,2,96,128]{3,2,1,0:T(8,128)(2,1)} %bitcast.15), calls=%async_computation.1 | async-start | bytes 1572864 | tf_op jit(solution)/shard_map/all_to_all | solution.py:76
  41.7 2.3 %collective-permute-start.4 = (bf16[8,192,128]{2,1,0:T(8,128)(2,1)S(1)}, bf16[8,192,128]{2,1,0:T(8,128)(2,1)S(1)}, u32[]{:S(2)}, u32[]{:S(2)}) collective-permute-start(bf16[8,192,128]{2,1,0:T(8,128)(2,1)S(1)} %all-to-all-done.blocks_ref.near_ref), channel_id=1, source_target_pairs={{0,16},{1,17},{2,18},{3,19},{4,20},{5,21},{6,22},{7,23},{8,24},{9,... | collective-permute-start | bytes 1179656 | tf_op jit(solution)/shard_map/ppermute | solution.py:72
  44.0 2.1 %collective-permute-start.5 = (bf16[8,192,128]{2,1,0:T(8,128)(2,1)S(1)}, bf16[8,192,128]{2,1,0:T(8,128)(2,1)S(1)}, u32[]{:S(2)}, u32[]{:S(2)}) collective-permute-start(bf16[8,192,128]{2,1,0:T(8,128)(2,1)S(1)} %collective-permute-done.2.blocks_ref.far_ref), channel_id=1, source_target_pairs={{0,16},{1,17},{2,18},{3,19},{4,20},{5,21},{6,22},{7,23},{8,24},{9,... | collective-permute-start | bytes 1179656 | tf_op jit(solution)/shard_map/ppermute | solution.py:72
  46.0 0.0 collective-permute-done.4.near_other_ref
  46.1 1.5 %collective-permute-done.5.far_other_ref = bf16[8,192,128]{2,1,0:T(8,128)(2,1)S(1)} collective-permute-done((bf16[8,192,128]{2,1,0:T(8,128)(2,1)S(1)}, bf16[8,192,128]{2,1,0:T(8,128)(2,1)S(1)}, u32[]{:S(2)}, u32[]{:S(2)}) %collective-permute-start.5) | collective-permute-done | bytes 393248 | tf_op jit(solution)/shard_map/ppermute | solution.py:72
  47.6 2.9 %input_grad.1 = bf16[5,64,2048]{2,1,0:T(8,128)(2,1)} custom-call(bf16[8,192,128]{2,1,0:T(8,128)(2,1)S(1)} %all-to-all-done.blocks_ref.near_ref, bf16[8,192,128]{2,1,0:T(8,128)(2,1)S(1)} %collective-permute-done.2.blocks_ref.far_ref, bf16[8,192,128]{2,1,0:T(8,128)(2,1)S(1)} %collective-permute-done.4.near_other_ref, ...), custom_call_target="tpu_custom_call" | custom-call | flops 503316480 | bytes 4194304 | tf_op jit(solution)/shard_map/input_grad/pallas_call | solution.py:355
  50.5 0.0 copy-start.3
  50.5 0.0 copy-start.4
  50.5 0.0 copy-start.5
  50.5 3.4 %all-to-all-done.1.parts_ref = bf16[16,2,96,128]{3,2,1,0:T(8,128)(2,1)S(1)} async-done(((bf16[16,2,96,128]{3,2,1,0:T(8,128)(2,1)}), bf16[16,2,96,128]{3,2,1,0:T(8,128)(2,1)S(1)}, u32[]{:S(2)}, u32[]{:S(2)}) %all-to-all-start.1) | async-done | bytes 786464 | tf_op jit(solution)/shard_map/all_to_all | solution.py:76
  54.0 0.1 sum.1
  54.1 10.8 %all_to_all.20 = bf16[4,96,128]{2,1,0:T(8,128)(2,1)S(1)} all-to-all(bf16[4,96,128]{2,1,0:T(8,128)(2,1)S(1)} %sum.1), channel_id=1, replica_groups={{0,2,32,34},{1,3,33,35},{4,6,36,38},{5,7,37,39},{8,10,40,42},{9,11,41,4..., dimensions={0} | all-to-all | bytes 196608 | tf_op jit(solution)/shard_map/all_to_all | solution.py:76
  64.9 16.4 %all_to_all.21 = bf16[8,96,128]{2,1,0:T(8,128)(2,1)S(1)} all-to-all(bf16[8,96,128]{2,1,0:T(8,128)(2,1)S(1)} %broadcast_in_dim.7), channel_id=1, replica_groups={{0,128,256,384,64,192,320,448},{1,129,257,385,65,193,321,449},{2,130,25..., dimensions={0} | all-to-all | bytes 393216 | tf_op jit(solution)/shard_map/all_to_all | solution.py:76
  81.3 5.9 %collective-permute-start.6 = (f32[192,128]{1,0:T(8,128)S(1)}, f32[192,128]{1,0:T(8,128)S(1)}, u32[]{:S(2)}, u32[]{:S(2)}) collective-permute-start(f32[192,128]{1,0:T(8,128)S(1)} %bitcast.16), channel_id=1, source_target_pairs={{0,16},{1,17},{2,18},{3,19},{4,20},{5,21},{6,22},{7,23},{8,24},{9,... | collective-permute-start | bytes 294920 | tf_op jit(solution)/shard_map/ppermute | solution.py:72
  87.2 0.9 %collective-permute-done.6.other_ref = f32[192,128]{1,0:T(8,128)S(1)} collective-permute-done((f32[192,128]{1,0:T(8,128)S(1)}, f32[192,128]{1,0:T(8,128)S(1)}, u32[]{:S(2)}, u32[]{:S(2)}) %collective-permute-start.6) | collective-permute-done | bytes 98336 | tf_op jit(solution)/shard_map/ppermute | solution.py:72
  88.1 0.0 copy-done.3
  88.1 0.0 copy-done.4
  88.1 0.0 copy-done.5
  88.1 1.0 %adam.1 = (f32[128,384]{1,0:T(8,128)}, f32[128,384]{1,0:T(8,128)}, f32[128,384]{1,0:T(8,128)}) custom-call(f32[192,128]{1,0:T(8,128)S(1)} %bitcast.17, f32[192,128]{1,0:T(8,128)S(1)} %collective-permute-done.6.other_ref, f32[128,384]{1,0:T(8,128)S(1)} %copy-done.3, f32[128,384]{1,0:T(8,128)S(1)} %copy-done.4, f32[128,384]{1,0:T(8,128)S(1)} %copy-done.5), custom_call_target="tpu_custom_call" | custom-call | tf_op jit(solution)/shard_map/adam/pallas_call | solution.py:387
  (3 shorter events, 0.1 us)
Async XLA Ops:
  0.6 9.8 %copy-start = (bf16[64,5,2048]{2,0,1:T(8,128)(2,1)S(1)}, bf16[64,5,2048]{2,0,1:T(8,128)(2,1)}, u32[]{:S(2)}) copy-start(bf16[64,5,2048]{2,0,1:T(8,128)(2,1)} %param.6) | copy-start | bytes 3932164
  0.6 1.0 %copy-start.2 = (f32[128,384]{1,0:T(8,128)S(1)}, f32[128,384]{1,0:T(8,128)}, u32[]{:S(2)}) copy-start(f32[128,384]{1,0:T(8,128)} %weight_ref.3) | copy-start | bytes 589828
  2.6 16.1 %all-to-all-start = ((bf16[8,192,128]{2,1,0:T(8,128)(2,1)}), bf16[8,192,128]{2,1,0:T(8,128)(2,1)S(1)}, u32[]{:S(2)}, u32[]{:S(2)}) async-start(bf16[8,192,128]{2,1,0:T(8,128)(2,1)} %broadcast_in_dim.6), calls=%async_computation | async-start | bytes 786432 | tf_op jit(solution)/shard_map/all_to_all | solution.py:76
  11.3 10.9 %collective-permute-start.1 = (bf16[3,64,2048]{2,1,0:T(8,128)(2,1)}, bf16[3,64,2048]{2,1,0:T(8,128)(2,1)S(1)}, u32[]{:S(2)}, u32[]{:S(2)}) collective-permute-start(bf16[3,64,2048]{2,1,0:T(8,128)(2,1)} %slice.7), channel_id=1, source_target_pairs={{0,16},{1,17},{2,18},{3,19},{4,20},{5,21},{6,22},{7,23},{8,24},{9,... | collective-permute-start | bytes 2359304 | tf_op jit(solution)/shard_map/ppermute | solution.py:72
  16.6 11.1 %copy-start.6 = (f32[384,3]{0,1:T(4,128)S(1)}, f32[384,3]{0,1:T(4,128)}, u32[]{:S(2)}) copy-start(f32[384,3]{0,1:T(4,128)} %param.9) | copy-start | bytes 13828
  16.6 11.1 %copy-start.7 = (s32[64]{0:T(128)S(1)}, s32[64]{0:T(128)}, u32[]{:S(2)}) copy-start(s32[64]{0:T(128)} %param.7) | copy-start | bytes 772
  16.6 5.6 %collective-permute-start = (bf16[2,64,2048]{2,1,0:T(8,128)(2,1)}, bf16[2,64,2048]{2,1,0:T(8,128)(2,1)S(1)}, u32[]{:S(2)}, u32[]{:S(2)}) collective-permute-start(bf16[2,64,2048]{2,1,0:T(8,128)(2,1)} %slice.6), channel_id=1, source_target_pairs={{0,16},{1,17},{2,18},{3,19},{4,20},{5,21},{6,22},{7,23},{8,24},{9,... | collective-permute-start | bytes 1572872 | tf_op jit(solution)/shard_map/ppermute | solution.py:72
  18.7 9.0 %collective-permute-start.2 = (bf16[8,192,128]{2,1,0:T(8,128)(2,1)S(1)}, bf16[8,192,128]{2,1,0:T(8,128)(2,1)S(1)}, u32[]{:S(2)}, u32[]{:S(2)}) collective-permute-start(bf16[8,192,128]{2,1,0:T(8,128)(2,1)S(1)} %all-to-all-done.blocks_ref.near_ref), channel_id=1, source_target_pairs={{0,35},{1,2},{2,1},{3,32},{4,39},{5,6},{6,5},{7,36},{8,43},{9,10},... | collective-permute-start | bytes 1179656 | tf_op jit(solution)/shard_map/ppermute | solution.py:311
  28.7 7.0 %collective-permute-start.3 = (f32[2,64,128]{2,1,0:T(8,128)S(1)}, f32[2,64,128]{2,1,0:T(8,128)S(1)}, u32[]{:S(2)}, u32[]{:S(2)}) collective-permute-start(f32[2,64,128]{2,1,0:T(8,128)S(1)} %get-tuple-element.17.logits_ref), channel_id=1, source_target_pairs={{0,16},{1,17},{2,18},{3,19},{4,20},{5,21},{6,22},{7,23},{8,24},{9,... | collective-permute-start | bytes 196616 | tf_op jit(solution)/shard_map/ppermute | solution.py:72
  37.2 0.9 %copy-start.1 = (bf16[4,2,2,2,96,128]{5,4,3,2,1,0:T(8,128)(2,1)}, bf16[4,2,2,2,96,128]{5,4,3,2,1,0:T(8,128)(2,1)S(1)}, u32[]{:S(2)}) copy-start(bf16[4,2,2,2,96,128]{5,4,3,2,1,0:T(8,128)(2,1)S(1)} %get-tuple-element.19) | copy-start | bytes 2359300
  38.1 15.9 %all-to-all-start.1 = ((bf16[16,2,96,128]{3,2,1,0:T(8,128)(2,1)}), bf16[16,2,96,128]{3,2,1,0:T(8,128)(2,1)S(1)}, u32[]{:S(2)}, u32[]{:S(2)}) async-start(bf16[16,2,96,128]{3,2,1,0:T(8,128)(2,1)} %bitcast.15), calls=%async_computation.1 | async-start | bytes 1572864 | tf_op jit(solution)/shard_map/all_to_all | solution.py:76
  41.7 4.3 %collective-permute-start.4 = (bf16[8,192,128]{2,1,0:T(8,128)(2,1)S(1)}, bf16[8,192,128]{2,1,0:T(8,128)(2,1)S(1)}, u32[]{:S(2)}, u32[]{:S(2)}) collective-permute-start(bf16[8,192,128]{2,1,0:T(8,128)(2,1)S(1)} %all-to-all-done.blocks_ref.near_ref), channel_id=1, source_target_pairs={{0,16},{1,17},{2,18},{3,19},{4,20},{5,21},{6,22},{7,23},{8,24},{9,... | collective-permute-start | bytes 1179656 | tf_op jit(solution)/shard_map/ppermute | solution.py:72
  44.0 3.6 %collective-permute-start.5 = (bf16[8,192,128]{2,1,0:T(8,128)(2,1)S(1)}, bf16[8,192,128]{2,1,0:T(8,128)(2,1)S(1)}, u32[]{:S(2)}, u32[]{:S(2)}) collective-permute-start(bf16[8,192,128]{2,1,0:T(8,128)(2,1)S(1)} %collective-permute-done.2.blocks_ref.far_ref), channel_id=1, source_target_pairs={{0,16},{1,17},{2,18},{3,19},{4,20},{5,21},{6,22},{7,23},{8,24},{9,... | collective-permute-start | bytes 1179656 | tf_op jit(solution)/shard_map/ppermute | solution.py:72
  50.5 37.6 %copy-start.3 = (f32[128,384]{1,0:T(8,128)S(1)}, f32[128,384]{1,0:T(8,128)}, u32[]{:S(2)}) copy-start(f32[128,384]{1,0:T(8,128)} %weight_ref.3) | copy-start | bytes 589828
  50.5 37.6 %copy-start.4 = (f32[128,384]{1,0:T(8,128)S(1)}, f32[128,384]{1,0:T(8,128)}, u32[]{:S(2)}) copy-start(f32[128,384]{1,0:T(8,128)} %first_ref.1) | copy-start | bytes 589828
  50.5 37.6 %copy-start.5 = (f32[128,384]{1,0:T(8,128)S(1)}, f32[128,384]{1,0:T(8,128)}, u32[]{:S(2)}) copy-start(f32[128,384]{1,0:T(8,128)} %second_ref.1) | copy-start | bytes 589828
  81.3 6.8 %collective-permute-start.6 = (f32[192,128]{1,0:T(8,128)S(1)}, f32[192,128]{1,0:T(8,128)S(1)}, u32[]{:S(2)}, u32[]{:S(2)}) collective-permute-start(f32[192,128]{1,0:T(8,128)S(1)} %bitcast.16), channel_id=1, source_target_pairs={{0,16},{1,17},{2,18},{3,19},{4,20},{5,21},{6,22},{7,23},{8,24},{9,... | collective-permute-start | bytes 294920 | tf_op jit(solution)/shard_map/ppermute | solution.py:72

commit v9 on v8

--- a/solution.py
+++ b/solution.py
@@ -43,11 +43,11 @@
 
 
 def pair_of(y, c):
-    return (y - c) % (YH * YL) // PAIR
+    return (y - 1 + c) % (YH * YL) // PAIR
 
 
 def beyond(yh, yl, c):
-    at = (yh * YL + yl + (1 if (yl + c) % PAIR else -1)) % (YH * YL)
+    at = (yh * YL + yl + (-1 if (yl + c) % PAIR else 1)) % (YH * YL)
     return at // YL, at % YL
 
 
@@ -127,7 +127,7 @@
 def shards_of(core, far):
     yl = lax.rem(lax.axis_index("group"), YL)
     odd = lax.rem(yl, PAIR)
-    step = 1 - 2 * core
+    step = 2 * core - 1
     even_at = lax.rem(yl - odd * step + YL, YL)
     odd_at = lax.rem(yl + (1 - odd) * step + YL, YL)
     return [x * YL + lax.rem(at + PAIR * far, YL) for x in range(X) for at in (even_at, odd_at)]
@@ -306,8 +306,9 @@
         name="prepare",
     )(weight)
     sent_rows, half = lax.optimization_barrier((rows, half))
-    other_rows = (swap_cores(sent_rows[:2]), swap_cores(sent_rows[2:]))
     near = exchange(jnp.broadcast_to(half, (X * PAIR, half_outs, shard)), OVER_XY)
+    later_rows, near = lax.optimization_barrier((rows, near))
+    other_rows = (swap_cores(sent_rows[:4]), swap_cores(later_rows[4:]))
     far = lax.ppermute(near, AXES, CROSS)
 
     flops = 2 * count * channels * outputs

time: 89.8 us -> 89.2 us (level)
  starting transfers between devices: 37.7 us -> 42 us
  waiting for transfers between devices: 11.7 us -> 7.93 us
    ppermute x6, starting transfers between devices: 22.8 us -> 27.8 us  [swap_cores(): return lax.ppermute(value, AXES, SWAP)]
    ppermute x1, waiting for transfers between devices: 4.88 us -> 0.01 us  [per_device(): far = lax.ppermute(near, AXES, CROSS)]
    all_to_all x2, starting transfers between devices: 11.4 us -> 9.47 us  [exchange(): lax.all_to_all(value, AXES, 0, 0, tiled=True, axis_index_groups=members)]
    ppermute x1, starting transfers between devices: 3.54 us -> 4.75 us  [per_device(): far = lax.ppermute(near, AXES, CROSS)]
    ppermute x6, waiting for transfers between devices: 3.35 us -> 4.48 us  [swap_cores(): return lax.ppermute(value, AXES, SWAP)]
  transfers between devices with their start and end apart: 9 -> 9, of which waited for: 5 -> 5; matrix products, arithmetic and copies ran while one was open for 2% -> 1% of each run, Pallas kernels for 4% -> 4%
where the time goes in v9:
time: 89.2 us; the launch traced here: 88.6 us
  starting transfers between devices  42 us (47%)
  blocking collectives  26.7 us (30%)
  waiting for transfers between devices  7.93 us (9%)
  Pallas kernels  7.22 us (8%)
  local copies, waits for them, and re-layouts  3.86 us (4%)
    ppermute x6, starting transfers between devices, swap_cores(): return lax.ppermute(value, AXES, SWAP)  27.8 us
    all_to_all x2, blocking collectives, exchange(): lax.all_to_all(value, AXES, 0, 0, tiled=True, axis_index_groups=members)  26.7 us
    all_to_all x2, starting transfers between devices, exchange(): lax.all_to_all(value, AXES, 0, 0, tiled=True, axis_index_groups=members)  9.47 us
    ppermute x1, starting transfers between devices, per_device(): far = lax.ppermute(near, AXES, CROSS)  4.75 us
    ppermute x6, waiting for transfers between devices, swap_cores(): return lax.ppermute(value, AXES, SWAP)  4.48 us
    all_to_all x2, waiting for transfers between devices, exchange(): lax.all_to_all(value, AXES, 0, 0, tiled=True, axis_index_groups=members)  3.44 us
    pallas_call x1, Pallas kernels, per_device(): pl.pallas_call(input_kernel, out_shape=jax.ShapeDtypeStruct((positions, p...  2.9 us
    unnamed x16, local copies, waits for them, and re-layouts  1.95 us
  transfers between devices with their start and end apart: 9, of which 5 were waited for; matrix products, arithmetic and copies ran while one was open for 1% of the time, Pallas kernels for 4%

profile of v9, /device:TPU:1, one launch (start us, length us, event | category | flops | bytes accessed | tf_op | source)
XLA Modules:
  0.0 88.6 jit_solution(15071730460670549193)
XLA Ops:
  0.6 0.0 copy-start
  0.6 0.0 copy-start.2
  0.7 1.0 %copy-done.2 = f32[128,384]{1,0:T(8,128)S(1)} copy-done((f32[128,384]{1,0:T(8,128)S(1)}, f32[128,384]{1,0:T(8,128)}, u32[]{:S(2)}) %copy-start.2) | copy-done | bytes 196632
  1.7 0.1 prepare.1
  1.8 0.8 broadcast_in_dim.6
  2.6 5.9 %all-to-all-start = ((bf16[8,192,128]{2,1,0:T(8,128)(2,1)}), bf16[8,192,128]{2,1,0:T(8,128)(2,1)S(1)}, u32[]{:S(2)}, u32[]{:S(2)}) async-start(bf16[8,192,128]{2,1,0:T(8,128)(2,1)} %broadcast_in_dim.6), calls=%async_computation | async-start | bytes 786432 | tf_op jit(solution)/shard_map/all_to_all | solution.py:76
  8.5 0.0 copy-done
  8.5 1.0 %slice.6 = bf16[4,64,2048]{2,1,0:T(8,128)(2,1)} slice(bf16[5,64,2048]{2,1,0:T(8,128)(2,1)S(1)} %bitcast.9), slice={[0:4], [0:64], [0:2048]} | slice | bytes 2097152 | tf_op jit(solution)/shard_map/slice | solution.py:311
  9.5 6.4 %collective-permute-start = (bf16[4,64,2048]{2,1,0:T(8,128)(2,1)}, bf16[4,64,2048]{2,1,0:T(8,128)(2,1)S(1)}, u32[]{:S(2)}, u32[]{:S(2)}) collective-permute-start(bf16[4,64,2048]{2,1,0:T(8,128)(2,1)} %slice.6), channel_id=1, source_target_pairs={{0,16},{1,17},{2,18},{3,19},{4,20},{5,21},{6,22},{7,23},{8,24},{9,... | collective-permute-start | bytes 3145736 | tf_op jit(solution)/shard_map/ppermute | solution.py:72
  15.9 0.0 all-to-all-done.blocks_ref.near_ref
  15.9 4.8 %collective-permute-start.2 = (bf16[8,192,128]{2,1,0:T(8,128)(2,1)S(1)}, bf16[8,192,128]{2,1,0:T(8,128)(2,1)S(1)}, u32[]{:S(2)}, u32[]{:S(2)}) collective-permute-start(bf16[8,192,128]{2,1,0:T(8,128)(2,1)S(1)} %all-to-all-done.blocks_ref.near_ref), channel_id=1, source_target_pairs={{0,1},{1,0},{2,3},{3,2},{4,5},{5,4},{6,7},{7,6},{8,9},{9,8},{10,11... | collective-permute-start | bytes 1179656 | tf_op jit(solution)/shard_map/ppermute | solution.py:312
  20.7 0.0 copy-start.6
  20.7 0.0 copy-start.7
  20.7 5.2 %collective-permute-start.1 = (bf16[1,64,2048]{2,1,0:T(8,128)(2,1)S(1)}, bf16[1,64,2048]{2,1,0:T(8,128)(2,1)S(1)}, u32[]{:S(2)}, u32[]{:S(2)}) collective-permute-start(bf16[1,64,2048]{2,1,0:T(8,128)(2,1)S(1)} %slice.7), channel_id=1, source_target_pairs={{0,16},{1,17},{2,18},{3,19},{4,20},{5,21},{6,22},{7,23},{8,24},{9,... | collective-permute-start | bytes 786440 | tf_op jit(solution)/shard_map/ppermute | solution.py:72
  26.0 1.1 %collective-permute-done.1.last_ref = bf16[1,64,2048]{2,1,0:T(8,128)(2,1)S(1)} collective-permute-done((bf16[1,64,2048]{2,1,0:T(8,128)(2,1)S(1)}, bf16[1,64,2048]{2,1,0:T(8,128)(2,1)S(1)}, u32[]{:S(2)}, u32[]{:S(2)}) %collective-permute-start.1) | collective-permute-done | bytes 262176 | tf_op jit(solution)/shard_map/ppermute | solution.py:72
  27.1 0.0 collective-permute-done.first_ref
  27.1 0.5 forward_near.1.pre_ref
  27.7 0.0 collective-permute-done.2.blocks_ref.far_ref
  27.7 0.0 copy-done.6
  27.7 0.0 copy-done.7
  27.7 1.0 %forward_far.1 = (f32[2,320,192]{2,1,0:T(8,128)S(1)}, f32[2,64,128]{2,1,0:T(8,128)S(1)}) custom-call(f32[2,320,192]{2,1,0:T(8,128)S(1)} %forward_near.1.pre_ref, bf16[8,192,128]{2,1,0:T(8,128)(2,1)S(1)} %collective-permute-done.2.blocks_ref.far_ref, bf16[5,64,2048]{2,1,0:T(8,128)(2,1)S(1)} %bitcast.12, ...), custom_call_target="tpu_custom_call" | custom-call | flops 251658240 | bytes 4194304 | tf_op jit(solution)/shard_map/forward_far/pallas_call | solution.py:324
  28.7 6.0 %collective-permute-start.3 = (f32[2,64,128]{2,1,0:T(8,128)S(1)}, f32[2,64,128]{2,1,0:T(8,128)S(1)}, u32[]{:S(2)}, u32[]{:S(2)}) collective-permute-start(f32[2,64,128]{2,1,0:T(8,128)S(1)} %get-tuple-element.21.logits_ref), channel_id=1, source_target_pairs={{0,16},{1,17},{2,18},{3,19},{4,20},{5,21},{6,22},{7,23},{8,24},{9,... | collective-permute-start | bytes 196616 | tf_op jit(solution)/shard_map/ppermute | solution.py:72
  34.7 0.9 collective-permute-done.3.received_ref
  35.6 1.5 %gradient.1 = (bf16[4,2,2,2,96,128]{5,4,3,2,1,0:T(8,128)(2,1)S(1)}, f32[64,128]{1,0:T(8,128)S(1)}) custom-call(f32[2,64,128]{2,1,0:T(8,128)S(1)} %get-tuple-element.21.logits_ref, f32[2,64,128]{2,1,0:T(8,128)S(1)} %collective-permute-done.3.received_ref, f32[2,320,192]{2,1,0:T(8,128)S(1)} %get-tuple-element.22.slope_ref, bf16[5,64,2048]{2,1,0:T(8,128)(2,1)S(1)} %bitcast.13, ...), custom_call_target="tpu_custom_call" | custom-call | flops 503316480 | bytes 4194304 | tf_op jit(solution)/shard_map/gradient/pallas_call | solution.py:340
  37.1 0.0 copy-start.1
  37.1 0.9 %copy-done.1 = bf16[4,2,2,2,96,128]{5,4,3,2,1,0:T(8,128)(2,1)} copy-done((bf16[4,2,2,2,96,128]{5,4,3,2,1,0:T(8,128)(2,1)}, bf16[4,2,2,2,96,128]{5,4,3,2,1,0:T(8,128)(2,1)S(1)}, u32[]{:S(2)}) %copy-start.1) | copy-done | bytes 786456
  38.0 3.6 %all-to-all-start.1 = ((bf16[16,2,96,128]{3,2,1,0:T(8,128)(2,1)}), bf16[16,2,96,128]{3,2,1,0:T(8,128)(2,1)S(1)}, u32[]{:S(2)}, u32[]{:S(2)}) async-start(bf16[16,2,96,128]{3,2,1,0:T(8,128)(2,1)} %bitcast.15), calls=%async_computation.1 | async-start | bytes 1572864 | tf_op jit(solution)/shard_map/all_to_all | solution.py:76
  41.6 2.3 %collective-permute-start.4 = (bf16[8,192,128]{2,1,0:T(8,128)(2,1)S(1)}, bf16[8,192,128]{2,1,0:T(8,128)(2,1)S(1)}, u32[]{:S(2)}, u32[]{:S(2)}) collective-permute-start(bf16[8,192,128]{2,1,0:T(8,128)(2,1)S(1)} %all-to-all-done.blocks_ref.near_ref), channel_id=1, source_target_pairs={{0,16},{1,17},{2,18},{3,19},{4,20},{5,21},{6,22},{7,23},{8,24},{9,... | collective-permute-start | bytes 1179656 | tf_op jit(solution)/shard_map/ppermute | solution.py:72
  43.9 2.1 %collective-permute-start.5 = (bf16[8,192,128]{2,1,0:T(8,128)(2,1)S(1)}, bf16[8,192,128]{2,1,0:T(8,128)(2,1)S(1)}, u32[]{:S(2)}, u32[]{:S(2)}) collective-permute-start(bf16[8,192,128]{2,1,0:T(8,128)(2,1)S(1)} %collective-permute-done.2.blocks_ref.far_ref), channel_id=1, source_target_pairs={{0,16},{1,17},{2,18},{3,19},{4,20},{5,21},{6,22},{7,23},{8,24},{9,... | collective-permute-start | bytes 1179656 | tf_op jit(solution)/shard_map/ppermute | solution.py:72
  45.9 0.0 collective-permute-done.4.near_other_ref
  46.0 1.5 %collective-permute-done.5.far_other_ref = bf16[8,192,128]{2,1,0:T(8,128)(2,1)S(1)} collective-permute-done((bf16[8,192,128]{2,1,0:T(8,128)(2,1)S(1)}, bf16[8,192,128]{2,1,0:T(8,128)(2,1)S(1)}, u32[]{:S(2)}, u32[]{:S(2)}) %collective-permute-start.5) | collective-permute-done | bytes 393248 | tf_op jit(solution)/shard_map/ppermute | solution.py:72
  47.5 2.9 %input_grad.1 = bf16[5,64,2048]{2,1,0:T(8,128)(2,1)} custom-call(bf16[8,192,128]{2,1,0:T(8,128)(2,1)S(1)} %all-to-all-done.blocks_ref.near_ref, bf16[8,192,128]{2,1,0:T(8,128)(2,1)S(1)} %collective-permute-done.2.blocks_ref.far_ref, bf16[8,192,128]{2,1,0:T(8,128)(2,1)S(1)} %collective-permute-done.4.near_other_ref, ...), custom_call_target="tpu_custom_call" | custom-call | flops 503316480 | bytes 4194304 | tf_op jit(solution)/shard_map/input_grad/pallas_call | solution.py:356
  50.4 0.0 copy-start.3
  50.4 0.0 copy-start.4
  50.4 0.0 copy-start.5
  50.4 3.4 %all-to-all-done.1.parts_ref = bf16[16,2,96,128]{3,2,1,0:T(8,128)(2,1)S(1)} async-done(((bf16[16,2,96,128]{3,2,1,0:T(8,128)(2,1)}), bf16[16,2,96,128]{3,2,1,0:T(8,128)(2,1)S(1)}, u32[]{:S(2)}, u32[]{:S(2)}) %all-to-all-start.1) | async-done | bytes 786464 | tf_op jit(solution)/shard_map/all_to_all | solution.py:76
  53.9 0.1 sum.1
  54.0 10.1 %all_to_all.20 = bf16[4,96,128]{2,1,0:T(8,128)(2,1)S(1)} all-to-all(bf16[4,96,128]{2,1,0:T(8,128)(2,1)S(1)} %sum.1), channel_id=1, replica_groups={{0,2,32,34},{1,3,33,35},{4,6,36,38},{5,7,37,39},{8,10,40,42},{9,11,41,4..., dimensions={0} | all-to-all | bytes 196608 | tf_op jit(solution)/shard_map/all_to_all | solution.py:76
  64.1 16.6 %all_to_all.21 = bf16[8,96,128]{2,1,0:T(8,128)(2,1)S(1)} all-to-all(bf16[8,96,128]{2,1,0:T(8,128)(2,1)S(1)} %broadcast_in_dim.7), channel_id=1, replica_groups={{0,128,256,384,64,192,320,448},{1,129,257,385,65,193,321,449},{2,130,25..., dimensions={0} | all-to-all | bytes 393216 | tf_op jit(solution)/shard_map/all_to_all | solution.py:76
  80.7 5.9 %collective-permute-start.6 = (f32[192,128]{1,0:T(8,128)S(1)}, f32[192,128]{1,0:T(8,128)S(1)}, u32[]{:S(2)}, u32[]{:S(2)}) collective-permute-start(f32[192,128]{1,0:T(8,128)S(1)} %bitcast.16), channel_id=1, source_target_pairs={{0,16},{1,17},{2,18},{3,19},{4,20},{5,21},{6,22},{7,23},{8,24},{9,... | collective-permute-start | bytes 294920 | tf_op jit(solution)/shard_map/ppermute | solution.py:72
  86.6 0.9 %collective-permute-done.6.other_ref = f32[192,128]{1,0:T(8,128)S(1)} collective-permute-done((f32[192,128]{1,0:T(8,128)S(1)}, f32[192,128]{1,0:T(8,128)S(1)}, u32[]{:S(2)}, u32[]{:S(2)}) %collective-permute-start.6) | collective-permute-done | bytes 98336 | tf_op jit(solution)/shard_map/ppermute | solution.py:72
  87.5 0.0 copy-done.3
  87.5 0.0 copy-done.4
  87.5 0.0 copy-done.5
  87.5 1.0 %adam.1 = (f32[128,384]{1,0:T(8,128)}, f32[128,384]{1,0:T(8,128)}, f32[128,384]{1,0:T(8,128)}) custom-call(f32[192,128]{1,0:T(8,128)S(1)} %bitcast.17, f32[192,128]{1,0:T(8,128)S(1)} %collective-permute-done.6.other_ref, f32[128,384]{1,0:T(8,128)S(1)} %copy-done.3, f32[128,384]{1,0:T(8,128)S(1)} %copy-done.4, f32[128,384]{1,0:T(8,128)S(1)} %copy-done.5), custom_call_target="tpu_custom_call" | custom-call | tf_op jit(solution)/shard_map/adam/pallas_call | solution.py:388
  (4 shorter events, 0.1 us)
Async XLA Ops:
  0.6 7.9 %copy-start = (bf16[64,5,2048]{2,0,1:T(8,128)(2,1)S(1)}, bf16[64,5,2048]{2,0,1:T(8,128)(2,1)}, u32[]{:S(2)}) copy-start(bf16[64,5,2048]{2,0,1:T(8,128)(2,1)} %param.6) | copy-start | bytes 3932164
  0.6 1.0 %copy-start.2 = (f32[128,384]{1,0:T(8,128)S(1)}, f32[128,384]{1,0:T(8,128)}, u32[]{:S(2)}) copy-start(f32[128,384]{1,0:T(8,128)} %weight_ref.3) | copy-start | bytes 589828
  2.6 13.3 %all-to-all-start = ((bf16[8,192,128]{2,1,0:T(8,128)(2,1)}), bf16[8,192,128]{2,1,0:T(8,128)(2,1)S(1)}, u32[]{:S(2)}, u32[]{:S(2)}) async-start(bf16[8,192,128]{2,1,0:T(8,128)(2,1)} %broadcast_in_dim.6), calls=%async_computation | async-start | bytes 786432 | tf_op jit(solution)/shard_map/all_to_all | solution.py:76
  9.5 17.6 %collective-permute-start = (bf16[4,64,2048]{2,1,0:T(8,128)(2,1)}, bf16[4,64,2048]{2,1,0:T(8,128)(2,1)S(1)}, u32[]{:S(2)}, u32[]{:S(2)}) collective-permute-start(bf16[4,64,2048]{2,1,0:T(8,128)(2,1)} %slice.6), channel_id=1, source_target_pairs={{0,16},{1,17},{2,18},{3,19},{4,20},{5,21},{6,22},{7,23},{8,24},{9,... | collective-permute-start | bytes 3145736 | tf_op jit(solution)/shard_map/ppermute | solution.py:72
  15.9 11.7 %collective-permute-start.2 = (bf16[8,192,128]{2,1,0:T(8,128)(2,1)S(1)}, bf16[8,192,128]{2,1,0:T(8,128)(2,1)S(1)}, u32[]{:S(2)}, u32[]{:S(2)}) collective-permute-start(bf16[8,192,128]{2,1,0:T(8,128)(2,1)S(1)} %all-to-all-done.blocks_ref.near_ref), channel_id=1, source_target_pairs={{0,1},{1,0},{2,3},{3,2},{4,5},{5,4},{6,7},{7,6},{8,9},{9,8},{10,11... | collective-permute-start | bytes 1179656 | tf_op jit(solution)/shard_map/ppermute | solution.py:312
  20.7 7.0 %copy-start.6 = (f32[384,3]{0,1:T(4,128)S(1)}, f32[384,3]{0,1:T(4,128)}, u32[]{:S(2)}) copy-start(f32[384,3]{0,1:T(4,128)} %param.9) | copy-start | bytes 13828
  20.7 7.0 %copy-start.7 = (s32[64]{0:T(128)S(1)}, s32[64]{0:T(128)}, u32[]{:S(2)}) copy-start(s32[64]{0:T(128)} %param.7) | copy-start | bytes 772
  20.7 6.4 %collective-permute-start.1 = (bf16[1,64,2048]{2,1,0:T(8,128)(2,1)S(1)}, bf16[1,64,2048]{2,1,0:T(8,128)(2,1)S(1)}, u32[]{:S(2)}, u32[]{:S(2)}) collective-permute-start(bf16[1,64,2048]{2,1,0:T(8,128)(2,1)S(1)} %slice.7), channel_id=1, source_target_pairs={{0,16},{1,17},{2,18},{3,19},{4,20},{5,21},{6,22},{7,23},{8,24},{9,... | collective-permute-start | bytes 786440 | tf_op jit(solution)/shard_map/ppermute | solution.py:72
  28.7 6.9 %collective-permute-start.3 = (f32[2,64,128]{2,1,0:T(8,128)S(1)}, f32[2,64,128]{2,1,0:T(8,128)S(1)}, u32[]{:S(2)}, u32[]{:S(2)}) collective-permute-start(f32[2,64,128]{2,1,0:T(8,128)S(1)} %get-tuple-element.21.logits_ref), channel_id=1, source_target_pairs={{0,16},{1,17},{2,18},{3,19},{4,20},{5,21},{6,22},{7,23},{8,24},{9,... | collective-permute-start | bytes 196616 | tf_op jit(solution)/shard_map/ppermute | solution.py:72
  37.1 0.9 %copy-start.1 = (bf16[4,2,2,2,96,128]{5,4,3,2,1,0:T(8,128)(2,1)}, bf16[4,2,2,2,96,128]{5,4,3,2,1,0:T(8,128)(2,1)S(1)}, u32[]{:S(2)}) copy-start(bf16[4,2,2,2,96,128]{5,4,3,2,1,0:T(8,128)(2,1)S(1)} %get-tuple-element.23) | copy-start | bytes 2359300
  38.0 15.9 %all-to-all-start.1 = ((bf16[16,2,96,128]{3,2,1,0:T(8,128)(2,1)}), bf16[16,2,96,128]{3,2,1,0:T(8,128)(2,1)S(1)}, u32[]{:S(2)}, u32[]{:S(2)}) async-start(bf16[16,2,96,128]{3,2,1,0:T(8,128)(2,1)} %bitcast.15), calls=%async_computation.1 | async-start | bytes 1572864 | tf_op jit(solution)/shard_map/all_to_all | solution.py:76
  41.6 4.3 %collective-permute-start.4 = (bf16[8,192,128]{2,1,0:T(8,128)(2,1)S(1)}, bf16[8,192,128]{2,1,0:T(8,128)(2,1)S(1)}, u32[]{:S(2)}, u32[]{:S(2)}) collective-permute-start(bf16[8,192,128]{2,1,0:T(8,128)(2,1)S(1)} %all-to-all-done.blocks_ref.near_ref), channel_id=1, source_target_pairs={{0,16},{1,17},{2,18},{3,19},{4,20},{5,21},{6,22},{7,23},{8,24},{9,... | collective-permute-start | bytes 1179656 | tf_op jit(solution)/shard_map/ppermute | solution.py:72
  43.9 3.6 %collective-permute-start.5 = (bf16[8,192,128]{2,1,0:T(8,128)(2,1)S(1)}, bf16[8,192,128]{2,1,0:T(8,128)(2,1)S(1)}, u32[]{:S(2)}, u32[]{:S(2)}) collective-permute-start(bf16[8,192,128]{2,1,0:T(8,128)(2,1)S(1)} %collective-permute-done.2.blocks_ref.far_ref), channel_id=1, source_target_pairs={{0,16},{1,17},{2,18},{3,19},{4,20},{5,21},{6,22},{7,23},{8,24},{9,... | collective-permute-start | bytes 1179656 | tf_op jit(solution)/shard_map/ppermute | solution.py:72
  50.4 37.1 %copy-start.3 = (f32[128,384]{1,0:T(8,128)S(1)}, f32[128,384]{1,0:T(8,128)}, u32[]{:S(2)}) copy-start(f32[128,384]{1,0:T(8,128)} %weight_ref.3) | copy-start | bytes 589828
  50.4 37.1 %copy-start.4 = (f32[128,384]{1,0:T(8,128)S(1)}, f32[128,384]{1,0:T(8,128)}, u32[]{:S(2)}) copy-start(f32[128,384]{1,0:T(8,128)} %first_ref.1) | copy-start | bytes 589828
  50.4 37.1 %copy-start.5 = (f32[128,384]{1,0:T(8,128)S(1)}, f32[128,384]{1,0:T(8,128)}, u32[]{:S(2)}) copy-start(f32[128,384]{1,0:T(8,128)} %second_ref.1) | copy-start | bytes 589828
  80.7 6.8 %collective-permute-start.6 = (f32[192,128]{1,0:T(8,128)S(1)}, f32[192,128]{1,0:T(8,128)S(1)}, u32[]{:S(2)}, u32[]{:S(2)}) collective-permute-start(f32[192,128]{1,0:T(8,128)S(1)} %bitcast.16), channel_id=1, source_target_pairs={{0,16},{1,17},{2,18},{3,19},{4,20},{5,21},{6,22},{7,23},{8,24},{9,... | collective-permute-start | bytes 294920 | tf_op jit(solution)/shard_map/ppermute | solution.py:72

commit v10 on v9

--- a/solution.py
+++ b/solution.py
@@ -268,20 +268,29 @@
 
 
 def adam_kernel(
-    own_ref, other_ref, weight_ref, first_ref, second_ref, out_weight, out_first, out_second, flip_ref
+    own_ref, other_ref, weight_ref, first_ref, second_ref, out_weight, out_first, out_second, flip_ref, held_ref, sems
 ):
     half = own_ref.shape[0]
     core = core_index()
+    copies = []
+
+    def send(at, value, out_ref):
+        held_ref[at] = value
+        copies.append(pltpu.make_async_copy(held_ref.at[at], out_ref, sems.at[at]))
+        copies[-1].start()
+
     flip_ref[pl.ds(pl.multiple_of(core * half, half), half), :] = own_ref[...]
     flip_ref[pl.ds(pl.multiple_of((1 - core) * half, half), half), :] = other_ref[...]
     grad = flip_ref[...].T
     new_first = beta_one * first_ref[...] + (1.0 - beta_one) * grad
+    send(0, new_first, out_first)
     new_second = beta_two * second_ref[...] + (1.0 - beta_two) * grad * grad
+    send(1, new_second, out_second)
     first_hat = new_first / (1.0 - beta_one**bias_steps)
     second_hat = new_second / (1.0 - beta_two**bias_steps)
-    out_weight[...] = weight_ref[...] - learn_rate * first_hat / (jnp.sqrt(second_hat) + epsilon)
-    out_first[...] = new_first
-    out_second[...] = new_second
+    send(2, weight_ref[...] - learn_rate * first_hat / (jnp.sqrt(second_hat) + epsilon), out_weight)
+    for copy in copies:
+        copy.wait()
 
 
 def per_device(features, labels, weight, head, moment_one, moment_two):
@@ -379,8 +388,15 @@
         compiler_params=params,
         name="sum",
     )(parts)
-    over_y = jnp.sum(exchange(copies, OVER_Y).astype(jnp.float32), axis=0).astype(jnp.bfloat16)
-    parts = exchange(jnp.broadcast_to(over_y, (Z, deep, shard)), OVER_Z)
+    copies = pl.pallas_call(
+        sum_kernel,
+        out_shape=jax.ShapeDtypeStruct((Z, deep, shard), jnp.bfloat16),
+        in_specs=[vmem],
+        out_specs=vmem,
+        compiler_params=params,
+        name="sum_y",
+    )(exchange(copies, OVER_Y).reshape(-1, 1, deep, shard))
+    parts = exchange(copies, OVER_Z)
     mine = jnp.sum(parts.reshape(PAIR, Z // PAIR, deep, shard).astype(jnp.float32), axis=1)
     mine = mine.reshape(half_outs, shard)
 
@@ -389,8 +405,12 @@
         adam_kernel,
         out_shape=(jax.ShapeDtypeStruct((shard, outputs), jnp.float32),) * 3,
         in_specs=[vmem] * 5,
-        out_specs=(vmem,) * 3,
-        scratch_shapes=[pltpu.VMEM((outputs, shard), jnp.float32)],
+        out_specs=(anywhere,) * 3,
+        scratch_shapes=[
+            pltpu.VMEM((outputs, shard), jnp.float32),
+            pltpu.VMEM((3, shard, outputs), jnp.float32),
+            pltpu.SemaphoreType.DMA((3,)),
+        ],
         compiler_params=params,
         name="adam",
     )(mine, theirs, weight, moment_one, moment_two)

time: 89.2 us -> 89.1 us (level)
  no operation moved by 1% of the time
where the time goes in v10:
time: 89.1 us; the launch traced here: 88.5 us
  starting transfers between devices  41.9 us (47%)
  blocking collectives  26.6 us (30%)
  waiting for transfers between devices  7.93 us (9%)
  Pallas kernels  7.3 us (8%)
  local copies, waits for them, and re-layouts  3.85 us (4%)
    ppermute x6, starting transfers between devices, swap_cores(): return lax.ppermute(value, AXES, SWAP)  27.7 us
    all_to_all x2, blocking collectives, exchange(): lax.all_to_all(value, AXES, 0, 0, tiled=True, axis_index_groups=members)  26.6 us
    all_to_all x2, starting transfers between devices, exchange(): lax.all_to_all(value, AXES, 0, 0, tiled=True, axis_index_groups=members)  9.47 us
    ppermute x1, starting transfers between devices, per_device(): far = lax.ppermute(near, AXES, CROSS)  4.75 us
    ppermute x6, waiting for transfers between devices, swap_cores(): return lax.ppermute(value, AXES, SWAP)  4.48 us
    all_to_all x2, waiting for transfers between devices, exchange(): lax.all_to_all(value, AXES, 0, 0, tiled=True, axis_index_groups=members)  3.44 us
    pallas_call x1, Pallas kernels, per_device(): pl.pallas_call(input_kernel, out_shape=jax.ShapeDtypeStruct((positions, p...  2.91 us
    unnamed x16, local copies, waits for them, and re-layouts  1.94 us
  transfers between devices with their start and end apart: 9, of which 5 were waited for; matrix products, arithmetic and copies ran while one was open for 1% of the time, Pallas kernels for 4%

profile of v10, /device:TPU:1, one launch (start us, length us, event | category | flops | bytes accessed | tf_op | source)
XLA Modules:
  0.0 88.5 jit_solution(6842207549957171664)
XLA Ops:
  0.6 0.0 copy-start
  0.6 0.0 copy-start.2
  0.7 1.0 %copy-done.2 = f32[128,384]{1,0:T(8,128)S(1)} copy-done((f32[128,384]{1,0:T(8,128)S(1)}, f32[128,384]{1,0:T(8,128)}, u32[]{:S(2)}) %copy-start.2) | copy-done | bytes 196632
  1.7 0.1 prepare.1
  1.8 0.8 broadcast_in_dim.3
  2.6 5.9 %all-to-all-start = ((bf16[8,192,128]{2,1,0:T(8,128)(2,1)}), bf16[8,192,128]{2,1,0:T(8,128)(2,1)S(1)}, u32[]{:S(2)}, u32[]{:S(2)}) async-start(bf16[8,192,128]{2,1,0:T(8,128)(2,1)} %broadcast_in_dim.3), calls=%async_computation | async-start | bytes 786432 | tf_op jit(solution)/shard_map/all_to_all | solution.py:76
  8.5 0.0 copy-done
  8.5 1.1 %slice.6 = bf16[4,64,2048]{2,1,0:T(8,128)(2,1)} slice(bf16[5,64,2048]{2,1,0:T(8,128)(2,1)S(1)} %bitcast.10), slice={[0:4], [0:64], [0:2048]} | slice | bytes 2097152 | tf_op jit(solution)/shard_map/slice | solution.py:320
  9.6 6.4 %collective-permute-start = (bf16[4,64,2048]{2,1,0:T(8,128)(2,1)}, bf16[4,64,2048]{2,1,0:T(8,128)(2,1)S(1)}, u32[]{:S(2)}, u32[]{:S(2)}) collective-permute-start(bf16[4,64,2048]{2,1,0:T(8,128)(2,1)} %slice.6), channel_id=1, source_target_pairs={{0,16},{1,17},{2,18},{3,19},{4,20},{5,21},{6,22},{7,23},{8,24},{9,... | collective-permute-start | bytes 3145736 | tf_op jit(solution)/shard_map/ppermute | solution.py:72
  15.9 0.0 all-to-all-done.blocks_ref.near_ref
  16.0 4.8 %collective-permute-start.2 = (bf16[8,192,128]{2,1,0:T(8,128)(2,1)S(1)}, bf16[8,192,128]{2,1,0:T(8,128)(2,1)S(1)}, u32[]{:S(2)}, u32[]{:S(2)}) collective-permute-start(bf16[8,192,128]{2,1,0:T(8,128)(2,1)S(1)} %all-to-all-done.blocks_ref.near_ref), channel_id=1, source_target_pairs={{0,1},{1,0},{2,3},{3,2},{4,5},{5,4},{6,7},{7,6},{8,9},{9,8},{10,11... | collective-permute-start | bytes 1179656 | tf_op jit(solution)/shard_map/ppermute | solution.py:321
  20.7 0.0 copy-start.6
  20.7 0.0 copy-start.7
  20.8 5.2 %collective-permute-start.1 = (bf16[1,64,2048]{2,1,0:T(8,128)(2,1)S(1)}, bf16[1,64,2048]{2,1,0:T(8,128)(2,1)S(1)}, u32[]{:S(2)}, u32[]{:S(2)}) collective-permute-start(bf16[1,64,2048]{2,1,0:T(8,128)(2,1)S(1)} %slice.7), channel_id=1, source_target_pairs={{0,16},{1,17},{2,18},{3,19},{4,20},{5,21},{6,22},{7,23},{8,24},{9,... | collective-permute-start | bytes 786440 | tf_op jit(solution)/shard_map/ppermute | solution.py:72
  26.0 1.1 %collective-permute-done.1.last_ref = bf16[1,64,2048]{2,1,0:T(8,128)(2,1)S(1)} collective-permute-done((bf16[1,64,2048]{2,1,0:T(8,128)(2,1)S(1)}, bf16[1,64,2048]{2,1,0:T(8,128)(2,1)S(1)}, u32[]{:S(2)}, u32[]{:S(2)}) %collective-permute-start.1) | collective-permute-done | bytes 262176 | tf_op jit(solution)/shard_map/ppermute | solution.py:72
  27.1 0.0 collective-permute-done.first_ref
  27.1 0.5 forward_near.1.pre_ref
  27.7 0.0 collective-permute-done.2.blocks_ref.far_ref
  27.7 0.0 copy-done.6
  27.7 0.0 copy-done.7
  27.7 1.0 %forward_far.1 = (f32[2,320,192]{2,1,0:T(8,128)S(1)}, f32[2,64,128]{2,1,0:T(8,128)S(1)}) custom-call(f32[2,320,192]{2,1,0:T(8,128)S(1)} %forward_near.1.pre_ref, bf16[8,192,128]{2,1,0:T(8,128)(2,1)S(1)} %collective-permute-done.2.blocks_ref.far_ref, bf16[5,64,2048]{2,1,0:T(8,128)(2,1)S(1)} %bitcast.13, ...), custom_call_target="tpu_custom_call" | custom-call | flops 251658240 | bytes 4194304 | tf_op jit(solution)/shard_map/forward_far/pallas_call | solution.py:333
  28.7 6.0 %collective-permute-start.3 = (f32[2,64,128]{2,1,0:T(8,128)S(1)}, f32[2,64,128]{2,1,0:T(8,128)S(1)}, u32[]{:S(2)}, u32[]{:S(2)}) collective-permute-start(f32[2,64,128]{2,1,0:T(8,128)S(1)} %get-tuple-element.21.logits_ref), channel_id=1, source_target_pairs={{0,16},{1,17},{2,18},{3,19},{4,20},{5,21},{6,22},{7,23},{8,24},{9,... | collective-permute-start | bytes 196616 | tf_op jit(solution)/shard_map/ppermute | solution.py:72
  34.7 0.9 collective-permute-done.3.received_ref
  35.6 1.5 %gradient.1 = (bf16[4,2,2,2,96,128]{5,4,3,2,1,0:T(8,128)(2,1)S(1)}, f32[64,128]{1,0:T(8,128)S(1)}) custom-call(f32[2,64,128]{2,1,0:T(8,128)S(1)} %get-tuple-element.21.logits_ref, f32[2,64,128]{2,1,0:T(8,128)S(1)} %collective-permute-done.3.received_ref, f32[2,320,192]{2,1,0:T(8,128)S(1)} %get-tuple-element.22.slope_ref, bf16[5,64,2048]{2,1,0:T(8,128)(2,1)S(1)} %bitcast.14, ...), custom_call_target="tpu_custom_call" | custom-call | flops 503316480 | bytes 4194304 | tf_op jit(solution)/shard_map/gradient/pallas_call | solution.py:349
  37.1 0.0 copy-start.1
  37.1 0.9 copy-done.1
  37.9 3.6 %all-to-all-start.1 = ((bf16[16,2,96,128]{3,2,1,0:T(8,128)(2,1)}), bf16[16,2,96,128]{3,2,1,0:T(8,128)(2,1)S(1)}, u32[]{:S(2)}, u32[]{:S(2)}) async-start(bf16[16,2,96,128]{3,2,1,0:T(8,128)(2,1)} %bitcast.16), calls=%async_computation.1 | async-start | bytes 1572864 | tf_op jit(solution)/shard_map/all_to_all | solution.py:76
  41.6 2.3 %collective-permute-start.4 = (bf16[8,192,128]{2,1,0:T(8,128)(2,1)S(1)}, bf16[8,192,128]{2,1,0:T(8,128)(2,1)S(1)}, u32[]{:S(2)}, u32[]{:S(2)}) collective-permute-start(bf16[8,192,128]{2,1,0:T(8,128)(2,1)S(1)} %all-to-all-done.blocks_ref.near_ref), channel_id=1, source_target_pairs={{0,16},{1,17},{2,18},{3,19},{4,20},{5,21},{6,22},{7,23},{8,24},{9,... | collective-permute-start | bytes 1179656 | tf_op jit(solution)/shard_map/ppermute | solution.py:72
  43.8 2.1 %collective-permute-start.5 = (bf16[8,192,128]{2,1,0:T(8,128)(2,1)S(1)}, bf16[8,192,128]{2,1,0:T(8,128)(2,1)S(1)}, u32[]{:S(2)}, u32[]{:S(2)}) collective-permute-start(bf16[8,192,128]{2,1,0:T(8,128)(2,1)S(1)} %collective-permute-done.2.blocks_ref.far_ref), channel_id=1, source_target_pairs={{0,16},{1,17},{2,18},{3,19},{4,20},{5,21},{6,22},{7,23},{8,24},{9,... | collective-permute-start | bytes 1179656 | tf_op jit(solution)/shard_map/ppermute | solution.py:72
  45.9 0.0 collective-permute-done.4.near_other_ref
  45.9 1.5 %collective-permute-done.5.far_other_ref = bf16[8,192,128]{2,1,0:T(8,128)(2,1)S(1)} collective-permute-done((bf16[8,192,128]{2,1,0:T(8,128)(2,1)S(1)}, bf16[8,192,128]{2,1,0:T(8,128)(2,1)S(1)}, u32[]{:S(2)}, u32[]{:S(2)}) %collective-permute-start.5) | collective-permute-done | bytes 393248 | tf_op jit(solution)/shard_map/ppermute | solution.py:72
  47.5 2.9 %input_grad.1 = bf16[5,64,2048]{2,1,0:T(8,128)(2,1)} custom-call(bf16[8,192,128]{2,1,0:T(8,128)(2,1)S(1)} %all-to-all-done.blocks_ref.near_ref, bf16[8,192,128]{2,1,0:T(8,128)(2,1)S(1)} %collective-permute-done.2.blocks_ref.far_ref, bf16[8,192,128]{2,1,0:T(8,128)(2,1)S(1)} %collective-permute-done.4.near_other_ref, ...), custom_call_target="tpu_custom_call" | custom-call | flops 503316480 | bytes 4194304 | tf_op jit(solution)/shard_map/input_grad/pallas_call | solution.py:365
  50.4 0.0 copy-start.3
  50.4 0.0 copy-start.4
  50.4 0.0 copy-start.5
  50.4 3.4 %all-to-all-done.1.parts_ref = bf16[16,2,96,128]{3,2,1,0:T(8,128)(2,1)S(1)} async-done(((bf16[16,2,96,128]{3,2,1,0:T(8,128)(2,1)}), bf16[16,2,96,128]{3,2,1,0:T(8,128)(2,1)S(1)}, u32[]{:S(2)}, u32[]{:S(2)}) %all-to-all-start.1) | async-done | bytes 786464 | tf_op jit(solution)/shard_map/all_to_all | solution.py:76
  53.8 0.1 sum.1
  54.0 10.1 %all_to_all.20 = bf16[4,96,128]{2,1,0:T(8,128)(2,1)S(1)} all-to-all(bf16[4,96,128]{2,1,0:T(8,128)(2,1)S(1)} %sum.1), channel_id=1, replica_groups={{0,2,32,34},{1,3,33,35},{4,6,36,38},{5,7,37,39},{8,10,40,42},{9,11,41,4..., dimensions={0} | all-to-all | bytes 196608 | tf_op jit(solution)/shard_map/all_to_all | solution.py:76
  64.0 16.6 %all_to_all.21 = bf16[8,96,128]{2,1,0:T(8,128)(2,1)S(1)} all-to-all(bf16[8,96,128]{2,1,0:T(8,128)(2,1)S(1)} %sum_y.1), channel_id=1, replica_groups={{0,128,256,384,64,192,320,448},{1,129,257,385,65,193,321,449},{2,130,25..., dimensions={0} | all-to-all | bytes 393216 | tf_op jit(solution)/shard_map/all_to_all | solution.py:76
  80.7 5.9 %collective-permute-start.6 = (f32[192,128]{1,0:T(8,128)S(1)}, f32[192,128]{1,0:T(8,128)S(1)}, u32[]{:S(2)}, u32[]{:S(2)}) collective-permute-start(f32[192,128]{1,0:T(8,128)S(1)} %bitcast.17), channel_id=1, source_target_pairs={{0,16},{1,17},{2,18},{3,19},{4,20},{5,21},{6,22},{7,23},{8,24},{9,... | collective-permute-start | bytes 294920 | tf_op jit(solution)/shard_map/ppermute | solution.py:72
  86.5 0.9 %collective-permute-done.6.other_ref = f32[192,128]{1,0:T(8,128)S(1)} collective-permute-done((f32[192,128]{1,0:T(8,128)S(1)}, f32[192,128]{1,0:T(8,128)S(1)}, u32[]{:S(2)}, u32[]{:S(2)}) %collective-permute-start.6) | collective-permute-done | bytes 98336 | tf_op jit(solution)/shard_map/ppermute | solution.py:72
  87.5 0.0 copy-done.3
  87.5 0.0 copy-done.4
  87.5 0.0 copy-done.5
  87.5 1.1 %adam.1 = (f32[128,384]{1,0:T(8,128)}, f32[128,384]{1,0:T(8,128)}, f32[128,384]{1,0:T(8,128)}) custom-call(f32[192,128]{1,0:T(8,128)S(1)} %bitcast.18, f32[192,128]{1,0:T(8,128)S(1)} %collective-permute-done.6.other_ref, f32[128,384]{1,0:T(8,128)S(1)} %copy-done.3, f32[128,384]{1,0:T(8,128)S(1)} %copy-done.4, f32[128,384]{1,0:T(8,128)S(1)} %copy-done.5), custom_call_target="tpu_custom_call" | custom-call | tf_op jit(solution)/shard_map/adam/pallas_call | solution.py:404
  (3 shorter events, 0.1 us)
Async XLA Ops:
  0.6 7.9 %copy-start = (bf16[64,5,2048]{2,0,1:T(8,128)(2,1)S(1)}, bf16[64,5,2048]{2,0,1:T(8,128)(2,1)}, u32[]{:S(2)}) copy-start(bf16[64,5,2048]{2,0,1:T(8,128)(2,1)} %param.6) | copy-start | bytes 3932164
  0.6 1.0 %copy-start.2 = (f32[128,384]{1,0:T(8,128)S(1)}, f32[128,384]{1,0:T(8,128)}, u32[]{:S(2)}) copy-start(f32[128,384]{1,0:T(8,128)} %weight_ref.3) | copy-start | bytes 589828
  2.6 13.3 %all-to-all-start = ((bf16[8,192,128]{2,1,0:T(8,128)(2,1)}), bf16[8,192,128]{2,1,0:T(8,128)(2,1)S(1)}, u32[]{:S(2)}, u32[]{:S(2)}) async-start(bf16[8,192,128]{2,1,0:T(8,128)(2,1)} %broadcast_in_dim.3), calls=%async_computation | async-start | bytes 786432 | tf_op jit(solution)/shard_map/all_to_all | solution.py:76
  9.6 17.5 %collective-permute-start = (bf16[4,64,2048]{2,1,0:T(8,128)(2,1)}, bf16[4,64,2048]{2,1,0:T(8,128)(2,1)S(1)}, u32[]{:S(2)}, u32[]{:S(2)}) collective-permute-start(bf16[4,64,2048]{2,1,0:T(8,128)(2,1)} %slice.6), channel_id=1, source_target_pairs={{0,16},{1,17},{2,18},{3,19},{4,20},{5,21},{6,22},{7,23},{8,24},{9,... | collective-permute-start | bytes 3145736 | tf_op jit(solution)/shard_map/ppermute | solution.py:72
  16.0 11.7 %collective-permute-start.2 = (bf16[8,192,128]{2,1,0:T(8,128)(2,1)S(1)}, bf16[8,192,128]{2,1,0:T(8,128)(2,1)S(1)}, u32[]{:S(2)}, u32[]{:S(2)}) collective-permute-start(bf16[8,192,128]{2,1,0:T(8,128)(2,1)S(1)} %all-to-all-done.blocks_ref.near_ref), channel_id=1, source_target_pairs={{0,1},{1,0},{2,3},{3,2},{4,5},{5,4},{6,7},{7,6},{8,9},{9,8},{10,11... | collective-permute-start | bytes 1179656 | tf_op jit(solution)/shard_map/ppermute | solution.py:321
  20.7 6.9 %copy-start.6 = (f32[384,3]{0,1:T(4,128)S(1)}, f32[384,3]{0,1:T(4,128)}, u32[]{:S(2)}) copy-start(f32[384,3]{0,1:T(4,128)} %param.9) | copy-start | bytes 13828
  20.7 6.9 %copy-start.7 = (s32[64]{0:T(128)S(1)}, s32[64]{0:T(128)}, u32[]{:S(2)}) copy-start(s32[64]{0:T(128)} %param.7) | copy-start | bytes 772
  20.8 6.3 %collective-permute-start.1 = (bf16[1,64,2048]{2,1,0:T(8,128)(2,1)S(1)}, bf16[1,64,2048]{2,1,0:T(8,128)(2,1)S(1)}, u32[]{:S(2)}, u32[]{:S(2)}) collective-permute-start(bf16[1,64,2048]{2,1,0:T(8,128)(2,1)S(1)} %slice.7), channel_id=1, source_target_pairs={{0,16},{1,17},{2,18},{3,19},{4,20},{5,21},{6,22},{7,23},{8,24},{9,... | collective-permute-start | bytes 786440 | tf_op jit(solution)/shard_map/ppermute | solution.py:72
  28.7 6.9 %collective-permute-start.3 = (f32[2,64,128]{2,1,0:T(8,128)S(1)}, f32[2,64,128]{2,1,0:T(8,128)S(1)}, u32[]{:S(2)}, u32[]{:S(2)}) collective-permute-start(f32[2,64,128]{2,1,0:T(8,128)S(1)} %get-tuple-element.21.logits_ref), channel_id=1, source_target_pairs={{0,16},{1,17},{2,18},{3,19},{4,20},{5,21},{6,22},{7,23},{8,24},{9,... | collective-permute-start | bytes 196616 | tf_op jit(solution)/shard_map/ppermute | solution.py:72
  37.1 0.9 %copy-start.1 = (bf16[4,2,2,2,96,128]{5,4,3,2,1,0:T(8,128)(2,1)}, bf16[4,2,2,2,96,128]{5,4,3,2,1,0:T(8,128)(2,1)S(1)}, u32[]{:S(2)}) copy-start(bf16[4,2,2,2,96,128]{5,4,3,2,1,0:T(8,128)(2,1)S(1)} %get-tuple-element.23) | copy-start | bytes 2359300
  37.9 15.9 %all-to-all-start.1 = ((bf16[16,2,96,128]{3,2,1,0:T(8,128)(2,1)}), bf16[16,2,96,128]{3,2,1,0:T(8,128)(2,1)S(1)}, u32[]{:S(2)}, u32[]{:S(2)}) async-start(bf16[16,2,96,128]{3,2,1,0:T(8,128)(2,1)} %bitcast.16), calls=%async_computation.1 | async-start | bytes 1572864 | tf_op jit(solution)/shard_map/all_to_all | solution.py:76
  41.6 4.3 %collective-permute-start.4 = (bf16[8,192,128]{2,1,0:T(8,128)(2,1)S(1)}, bf16[8,192,128]{2,1,0:T(8,128)(2,1)S(1)}, u32[]{:S(2)}, u32[]{:S(2)}) collective-permute-start(bf16[8,192,128]{2,1,0:T(8,128)(2,1)S(1)} %all-to-all-done.blocks_ref.near_ref), channel_id=1, source_target_pairs={{0,16},{1,17},{2,18},{3,19},{4,20},{5,21},{6,22},{7,23},{8,24},{9,... | collective-permute-start | bytes 1179656 | tf_op jit(solution)/shard_map/ppermute | solution.py:72
  43.8 3.6 %collective-permute-start.5 = (bf16[8,192,128]{2,1,0:T(8,128)(2,1)S(1)}, bf16[8,192,128]{2,1,0:T(8,128)(2,1)S(1)}, u32[]{:S(2)}, u32[]{:S(2)}) collective-permute-start(bf16[8,192,128]{2,1,0:T(8,128)(2,1)S(1)} %collective-permute-done.2.blocks_ref.far_ref), channel_id=1, source_target_pairs={{0,16},{1,17},{2,18},{3,19},{4,20},{5,21},{6,22},{7,23},{8,24},{9,... | collective-permute-start | bytes 1179656 | tf_op jit(solution)/shard_map/ppermute | solution.py:72
  50.4 37.1 %copy-start.3 = (f32[128,384]{1,0:T(8,128)S(1)}, f32[128,384]{1,0:T(8,128)}, u32[]{:S(2)}) copy-start(f32[128,384]{1,0:T(8,128)} %weight_ref.3) | copy-start | bytes 589828
  50.4 37.1 %copy-start.4 = (f32[128,384]{1,0:T(8,128)S(1)}, f32[128,384]{1,0:T(8,128)}, u32[]{:S(2)}) copy-start(f32[128,384]{1,0:T(8,128)} %first_ref.1) | copy-start | bytes 589828
  50.4 37.1 %copy-start.5 = (f32[128,384]{1,0:T(8,128)S(1)}, f32[128,384]{1,0:T(8,128)}, u32[]{:S(2)}) copy-start(f32[128,384]{1,0:T(8,128)} %second_ref.1) | copy-start | bytes 589828
  80.7 6.8 %collective-permute-start.6 = (f32[192,128]{1,0:T(8,128)S(1)}, f32[192,128]{1,0:T(8,128)S(1)}, u32[]{:S(2)}, u32[]{:S(2)}) collective-permute-start(f32[192,128]{1,0:T(8,128)S(1)} %bitcast.17), channel_id=1, source_target_pairs={{0,16},{1,17},{2,18},{3,19},{4,20},{5,21},{6,22},{7,23},{8,24},{9,... | collective-permute-start | bytes 294920 | tf_op jit(solution)/shard_map/ppermute | solution.py:72
